TPU v7x, 32 devices: a whole 2x2x4 slice. The times are simulated.
32 devices in a mesh: spot: 16 (over z, y, x), gene: 2 (over core).
Axes of the slice: x: 2, y: 2, z: 4, core: 2. Of those that a mesh axis runs over, the one named last changes fastest.
Arguments:
- logits: bfloat16 [4096, 4096], P(('spot', 'gene')), may hold values from -8 to 8
- filt: float32 [4096], P('spot'), may hold values from -8 to 8
- expr: bfloat16 [4096, 2048], P('spot', 'gene'), may hold values from -8 to 8
- target: bfloat16 [4096, 2048], P('spot', 'gene'), may hold values from -9 to 9
- gene_mask: int32 [4, 2048], P(None, 'gene'), may hold values from 0 to 1, as said below
- density: int32 [4096], P('spot'), may hold values from 1 to 2
Outputs:
- loss: float32 [], replicated
- grad_logits: float32 [4096, 4096], P(('spot', 'gene'))
- grad_filt: float32 [4096], P('spot')
- grad_expr: float32 [4096, 2048], P('spot', 'gene')
Inputs may be any that keep to these rules, and one draw needn't show every extreme that they name: `gene_mask`: 0 or 1; a slide may measure no gene at all.
All inputs are finite; a program needn't handle non-finite values.
Results may differ from a plain program's by a relative error of at most 0.005.
Values may be sent and summed in bfloat16 or wider, within the bound.
A program may use at most 64 MiB of HBM per device.

v0:
```python
import jax
import jax.numpy as jnp
from jax import lax
from jax.sharding import PartitionSpec as P

SPOTS = 4096
SLIDES = 4


eps_norm = 1e-06


def slide_moments(onehot, pred, truth):
    hi = lax.Precision.HIGHEST
    return jnp.stack(
        [
            jnp.dot(onehot.T, pred * truth, precision=hi),
            jnp.dot(onehot.T, pred * pred, precision=hi),
            jnp.dot(onehot.T, truth * truth, precision=hi),
        ]
    )


def spot_moments(pred, truth):
    return jnp.stack(
        [
            jnp.sum(pred * truth, axis=1),
            jnp.sum(pred * pred, axis=1),
            jnp.sum(truth * truth, axis=1),
        ]
    )


def cosine_parts(slide_stats):
    dots = slide_stats[0]
    slide_a = lax.rsqrt(slide_stats[1] + eps_norm)
    slide_b = lax.rsqrt(slide_stats[2] + eps_norm)
    return (dots, slide_a, slide_b, dots * slide_a * slide_b)


def pred_gradient(onehot, weight_slide, dots, slide_a, slide_b, spot_stats, pred, truth):
    hi = lax.Precision.HIGHEST
    spot_a = lax.rsqrt(spot_stats[1] + eps_norm)
    spot_b = lax.rsqrt(spot_stats[2] + eps_norm)
    coef_truth = -weight_slide * slide_a * slide_b
    coef_pred = weight_slide * dots * slide_a**3 * slide_b
    grad_pred = (
        jnp.dot(onehot, coef_truth, precision=hi) * truth
        + jnp.dot(onehot, coef_pred, precision=hi) * pred
    )
    grad_pred = (
        grad_pred
        + (
            -(spot_a * spot_b)[:, None] * truth
            + (spot_stats[0] * spot_a**3 * spot_b)[:, None] * pred
        )
        / SPOTS
    )
    return (grad_pred, spot_stats[0] * spot_a * spot_b)


def per_device(logits, filt, expr, target, gene_mask, density):
    f32 = jnp.float32
    bf16 = jnp.bfloat16
    nspot = lax.axis_size("spot")
    ngene = lax.axis_size("gene")
    spot_dev = logits.shape[0]
    cells = logits.shape[1]
    cell_dev = filt.shape[0]
    owned = target.shape[0]
    half = target.shape[1]
    spots_all = owned * nspot
    slide_len = SPOTS // SLIDES
    scores = logits.astype(f32)
    shifted = jnp.exp(scores - jnp.max(scores, axis=1, keepdims=True))
    probs = shifted / jnp.sum(shifted, axis=1, keepdims=True)
    moved = lax.all_to_all(probs.astype(bf16), "spot", split_axis=1, concat_axis=0, tiled=True)
    paired = lax.all_gather(moved.reshape(nspot, 1, spot_dev, cell_dev), "gene", axis=1, tiled=True)
    paired = paired.reshape(spots_all, cell_dev)
    gate = jax.nn.sigmoid(filt)
    weighted = (paired.astype(f32) * gate[None, :]).astype(bf16)
    partial_pred = jnp.dot(weighted, expr, preferred_element_type=f32)
    partial_mass = jnp.sum(weighted.astype(f32), axis=1)
    gate_part = jnp.sum(gate)
    maskf = gene_mask.astype(f32)
    mask_part = jnp.sum(maskf, axis=1)
    pred_three, mass_two = (
        lax.psum_scatter(
            partial_pred.reshape(nspot, owned, half), "spot", scatter_dimension=0, tiled=True
        ),
        lax.psum_scatter(
            partial_mass.reshape(nspot, owned), "spot", scatter_dimension=0, tiled=True
        ),
    )
    pred = pred_three.reshape(owned, half)
    mass = mass_two.reshape(owned)
    truth = target.astype(f32)
    dens = density.astype(f32)
    spot_ids = lax.axis_index("spot") * owned + jnp.arange(owned, dtype=jnp.int32)
    onehot = (
        spot_ids[:, None] // slide_len == jnp.arange(SLIDES, dtype=jnp.int32)[None, :]
    ).astype(f32)
    slide_stats, mass_total, gate_total, count_total = lax.psum(
        (slide_moments(onehot, pred, truth), jnp.sum(mass), gate_part, jnp.sum(dens)), "spot"
    )
    dots, slide_a, slide_b, cos_gene = cosine_parts(slide_stats)
    spot_stats, kept_genes, gene_numer = lax.psum(
        (spot_moments(pred, truth), mask_part, jnp.sum(maskf * cos_gene, axis=1)), "gene"
    )
    genes_kept = jnp.maximum(kept_genes, 1.0)
    weight_slide = maskf / genes_kept[:, None] / SLIDES
    grad_pred, cos_spot = pred_gradient(
        onehot, weight_slide, dots, slide_a, slide_b, spot_stats, pred, truth
    )
    share = dens / count_total
    kl_local = jnp.sum(share * (jnp.log(share) - jnp.log(mass) + jnp.log(mass_total)))
    cos_total, kl_total = lax.psum((jnp.sum(cos_spot), kl_local), "spot")
    grad_mass = 1.0 / mass_total - share / mass
    spread_three, spread_two = (
        lax.all_gather(grad_pred.astype(bf16).reshape(1, owned, half), "spot", axis=0, tiled=True),
        lax.all_gather(grad_mass.astype(bf16).reshape(1, owned), "spot", axis=0, tiled=True),
    )
    spread_pred = spread_three.reshape(spots_all, half)
    spread_mass = spread_two.reshape(spots_all)
    gene_term = jnp.mean(gene_numer / genes_kept)
    excess = gate_total / count_total - 1.0
    loss = -gene_term - cos_total / SPOTS + kl_total + excess * excess
    grad_expr = lax.dot_general(
        weighted, spread_pred, (((0,), (0,)), ((), ())), preferred_element_type=f32
    )
    first_half = (lax.axis_index("gene") == 0).astype(f32)
    grad_weighted = lax.dot_general(
        spread_pred, expr, (((1,), (1,)), ((), ())), preferred_element_type=f32
    )
    grad_weighted = grad_weighted + first_half * spread_mass.astype(f32)[:, None]
    filter_part = jnp.sum(grad_weighted * paired.astype(f32), axis=0)
    filter_total = lax.psum(filter_part, "gene")
    grad_filt = (filter_total + 2.0 * excess / count_total) * gate * (1.0 - gate)
    terms = (grad_weighted * gate[None, :]).reshape(nspot, ngene, spot_dev, cell_dev)
    moved_back = lax.all_to_all(terms, "spot", split_axis=0, concat_axis=3, tiled=True)
    folded = lax.psum_scatter(moved_back, "gene", scatter_dimension=1, tiled=True)
    rounded = lax.optimization_barrier(folded.reshape(spot_dev, cells).astype(bf16))
    grad_probs = rounded.astype(f32)
    grad_logits = probs * (grad_probs - jnp.sum(probs * grad_probs, axis=1, keepdims=True))
    return (loss, grad_logits, grad_filt, grad_expr)


def solution(mesh):
    in_specs = (
        P(("spot", "gene"), None),
        P("spot"),
        P("spot", "gene"),
        P("spot", "gene"),
        P(None, "gene"),
        P("spot"),
    )
    out_specs = (P(), P(("spot", "gene"), None), P("spot"), P("spot", "gene"))
    return jax.shard_map(
        per_device, mesh=mesh, in_specs=in_specs, out_specs=out_specs, check_vma=False
    )
```

profile of v0, /device:TPU:0, one launch (start us, length us, event | category | flops | bytes accessed | tf_op | source)
XLA Modules:
  0.0 749.4 jit_solution(4258948392055940909)
XLA Ops:
  7.2 1.6 reduce_max.14
  8.8 1.7 fusion.6
  11.1 34.6 %all_to_all.34 = bf16[128,16,256]{2,0,1:T(8,128)(2,1)} all-to-all(bf16[128,16,256]{2,0,1:T(8,128)(2,1)S(1)} %bitcast.93), channel_id=1, replica_groups=mesh['spot'=16,'gene'=2] {'spot'}, dimensions={1} | all-to-all | bytes 2097152 | tf_op jit(solution)/shard_map/all_to_all | solution.py:77
  45.8 0.6 fusion.48
  46.4 8.3 %all-gather.7.cloned.1.call-done = bf16[16,256,256]{2,1,0:T(8,128)(2,1)} async-done(((bf16[16,128,256]{2,1,0:T(8,128)(2,1)}), bf16[16,256,256]{2,1,0:T(8,128)(2,1)}) %all-gather.7.cloned.1.call-update) | async-done | bytes 2097168 | tf_op jit(solution)/shard_map/all_gather | solution.py:78
  54.7 9.7 %fusion.3 = f32[16,256,1024]{2,1,0:T(8,128)} fusion(f32[256]{0:T(256)S(1)} %get-tuple-element.18, bf16[16,256,256]{2,1,0:T(8,128)(2,1)} %all-gather.7.cloned.1.call-done, bf16[256,1024]{1,0:T(8,128)(2,1)S(1)} %copy-done), kind=kOutput, calls=%fused_computation.10 | convolution fusion | flops 2150629376 | bytes 19399680 | tf_op jit(solution)/shard_map/dot_general | solution.py:82
  65.7 0.6 convert_reduce_fusion.2
  66.3 3.5 convert_reduce_fusion
  69.7 88.4 %all-reduce = f32[16,256]{1,0:T(8,128)S(1)} all-reduce(f32[16,256]{1,0:T(8,128)S(1)} %bitcast.96), channel_id=6, replica_groups=mesh['spot'=16,'gene'=2] {'spot'}, use_global_device_ids=true, to_apply=%region_18.19.clone | all-reduce | flops 4096 | bytes 32768
  158.1 1.2 fusion.45
  159.9 38.8 %all-reduce.2 = (f32[]{:T(128)}, f32[]{:T(128)}) all-reduce(f32[]{:T(128)} %fusion.45, f32[]{:T(128)} %convert_reduce_fusion.2), channel_id=1, replica_groups=mesh['spot'=16,'gene'=2] {'spot'}, use_global_device_ids=true, to_apply=%region_20.21 | all-reduce | flops 2 | bytes 16 | tf_op jit(solution)/shard_map/psum | solution.py:103
  200.1 1.3 broadcast_multiply_fusion.1
  201.3 1.2 subtract_convert_fusion
  202.6 213.5 %reduce-scatter.3.cloned.1.call-done = f32[1,256,1024]{2,1,0:T(8,128)} async-done(((f32[16,256,1024]{2,1,0:T(8,128)}), f32[1,256,1024]{2,1,0:T(8,128)}) %reduce-scatter.3.cloned.1.call-update) | async-done | bytes 1048592 | tf_op jit(solution)/shard_map/reduce_scatter | solution.py:88
  416.1 1.7 fusion.17
  417.8 2.5 psum.73
  420.3 0.6 fusion.40
  422.0 79.2 %all-reduce.1 = (f32[3,4,1024]{2,1,0:T(4,128)S(1)}, f32[]{:T(128)}, f32[]{:T(128)}, f32[]{:T(128)}) all-reduce(f32[3,4,1024]{2,1,0:T(4,128)S(1)} %pad_maximum_fusion, f32[]{:T(128)} %get-tuple-element.29, f32[]{:T(128)} %get-tuple-element.32, f32[]{:T(128)} %get-tuple-element.17), channel_id=1, replica_groups=mesh['spot'=16,'gene'=2] {'spot'}, use_global_device_ids=true, to_apply=%region_3.0 | all-reduce | flops 12291 | bytes 98328 | tf_op jit(solution)/shard_map/psum | solution.py:103
  501.4 2.5 psum.72
  503.8 0.6 convert_multiply_fusion.2
  504.5 1.6 fusion.9
  506.2 35.7 %all-gather.3 = bf16[16,1,256]{2,1,0:T(2,128)(2,1)S(1)} all-gather(bf16[1,1,256]{2,1,0:T(2,128)(2,1)S(1)} %reshape.184), channel_id=4, replica_groups=mesh['spot'=16,'gene'=2] {'spot'}, dimensions={0}, use_global_device_ids=true | all-gather | bytes 8704 | tf_op jit(solution)/shard_map/all_gather | solution.py:121
  541.9 73.4 %all-gather.9.cloned.1.call-done = bf16[4096,1024]{1,0:T(8,128)(2,1)} async-done(((bf16[256,1024]{1,0:T(8,128)(2,1)}), bf16[4096,1024]{1,0:T(8,128)(2,1)}) %all-gather.9.cloned.1.call-update) | async-done | bytes 8388624 | tf_op jit(solution)/shard_map/all_gather | solution.py:120
  615.3 6.5 broadcast_multiply_fusion
  621.9 97.5 %all_to_all.35 = f32[16,2,128,256]{3,2,1,0:T(8,128)S(1)} all-to-all(f32[16,2,128,256]{3,2,1,0:T(8,128)S(1)} %bitcast.91), channel_id=1, replica_groups=mesh['spot'=16,'gene'=2] {'spot'}, dimensions={0} | all-to-all | bytes 8388608 | tf_op jit(solution)/shard_map/all_to_all | solution.py:140
  719.3 2.5 copy.15
  724.5 2.5 all-reduce.3
  727.0 0.6 divide_reduce_fusion
  729.5 7.9 %fusion.49 = f32[256,1024]{1,0:T(8,128)} fusion(bf16[4096,256]{1,0:T(8,128)(2,1)} %bitcast.90, bf16[4096,1024]{1,0:T(8,128)(2,1)} %all-gather.9.cloned.1.call-done), kind=kOutput, calls=%fused_computation.95 | convolution fusion | flops 2147483648 | bytes 11534336 | tf_op jit(solution)/shard_map/dot_general | solution.py:128
  737.4 1.7 convert_bitcast_fusion
  739.1 0.7 fusion.1
  739.8 2.0 fusion.2
  (42 shorter events, 4.4 us)
Async XLA Ops:
  7.2 47.6 %copy-start = (bf16[256,1024]{1,0:T(8,128)(2,1)S(1)}, bf16[256,1024]{1,0:T(8,128)(2,1)}, u32[]{:S(2)}) copy-start(bf16[256,1024]{1,0:T(8,128)(2,1)} %param.8) | copy-start | bytes 1572868
  7.2 3.3 copy-start.1
  7.2 47.5 %all-gather.7.cloned.1.call-start = ((), (), s32[]{:S(2)}) async-start(), calls=%async_computation.6 | async-start | bytes 3145728 | tf_op jit(solution)/shard_map/all_gather | solution.py:78
  11.1 34.7 %copy-start.5 = (f32[256]{0:T(256)S(1)}, f32[256]{0:T(256)}, u32[]{:S(2)}) copy-start(f32[256]{0:T(256)} %param.7) | copy-start | bytes 3076
  45.7 370.3 %reduce-scatter.3.cloned.1.call-start = ((), (), s32[]{:S(2)}) async-start(), calls=%async_computation.4 | async-start | bytes 17825792 | tf_op jit(solution)/shard_map/reduce_scatter | solution.py:88
  64.4 0.7 copy-start.7
  64.4 1.2 copy-start.6
  64.4 550.9 %all-gather.9.cloned.1.call-start = ((), (), s32[]{:S(2)}) async-start(), calls=%async_computation.7 | async-start | bytes 8912896 | tf_op jit(solution)/shard_map/all_gather | solution.py:120
  66.3 93.1 %copy-start.3 = (bf16[256,1024]{1,0:T(8,128)(2,1)S(1)}, bf16[256,1024]{1,0:T(8,128)(2,1)}, u32[]{:S(2)}) copy-start(bf16[256,1024]{1,0:T(8,128)(2,1)} %param.9) | copy-start | bytes 1572868
  202.6 298.6 %copy-start.4 = (s32[4,1024]{1,0:T(4,128)S(1)}, s32[4,1024]{1,0:T(4,128)}, u32[]{:S(2)}) copy-start(s32[4,1024]{1,0:T(4,128)} %param.10) | copy-start | bytes 49156
  416.1 4.8 copy-start.2
  506.1 231.2 %reduce-scatter.5.cloned.1.call-start = ((), (), s32[]{:S(2)}) async-start(), calls=%async_computation.5 | async-start | bytes 6291456 | tf_op jit(solution)/shard_map/reduce_scatter | solution.py:141
Sparse Core Ops, SparseCore 0:
  45.8 8.8 all-gather.6
  64.5 351.4 reduce-scatter.2
  506.2 109.0 all-gather.8
  722.0 10.3 reduce-scatter.4
where the time goes:
time: 750 us; the launch traced here: 749 us
  blocking collectives  382 us (51%)
  waiting for transfers between devices  295 us (39%)
  matrix products  28 us (4%)
  other arithmetic  20.3 us (3%)
  between operations  20.3 us (3%)
    reduce_scatter x1, waiting for transfers between devices, per_device(): lax.psum_scatter(partial_pred.reshape(nspot, owned, half), 'spot', scatte...  214 us
    psum x2, blocking collectives, per_device(): lax.psum((slide_moments(onehot, pred, truth), jnp.sum(mass), gate_part, j...  118 us
    all_to_all x1, blocking collectives, per_device(): lax.all_to_all(terms, 'spot', split_axis=0, concat_axis=3, tiled=True)  97.5 us
    unnamed x1, blocking collectives  88.4 us
    all_gather x1, waiting for transfers between devices, per_device(): lax.all_gather(grad_pred.astype(bf16).reshape(1, owned, half), 'spot', ax...  73.4 us
    all_gather x1, blocking collectives, per_device(): lax.all_gather(grad_mass.astype(bf16).reshape(1, owned), 'spot', axis=0,...  35.7 us
    all_to_all x1, blocking collectives, per_device(): lax.all_to_all(probs.astype(bf16), 'spot', split_axis=1, concat_axis=0, t...  34.6 us
  transfers between devices with their start and end apart: 4, of which 3 were waited for; matrix products, arithmetic and copies ran while one was open for 2% of the time, Pallas kernels for 0%

commit v1 on v0

--- a/solution.py
+++ b/solution.py
@@ -1,6 +1,10 @@
+import functools
+
 import jax
 import jax.numpy as jnp
 from jax import lax
+from jax.experimental import pallas as pl
+from jax.experimental.pallas import tpu as pltpu
 from jax.sharding import PartitionSpec as P
 
 SPOTS = 4096
@@ -59,7 +63,7 @@
     return (grad_pred, spot_stats[0] * spot_a * spot_b)
 
 
-def per_device(logits, filt, expr, target, gene_mask, density):
+def streamed(logits, filt, expr, target, gene_mask, density):
     f32 = jnp.float32
     bf16 = jnp.bfloat16
     nspot = lax.axis_size("spot")
@@ -145,6 +149,698 @@
     return (loss, grad_logits, grad_filt, grad_expr)
 
 
+GROUP = 4
+MESH = pl.DeviceIdType.MESH
+VMEM_BYTES = 60 << 20
+POS = {0: 0, 1: 1, 3: 2, 2: 3}
+
+
+def remote(src, dst, send, recv, dev):
+    return pltpu.make_async_remote_copy(
+        src_ref=src, dst_ref=dst, send_sem=send, recv_sem=recv, device_id=dev, device_id_type=MESH
+    )
+
+
+def dot_nt(a, b):
+    return lax.dot_general(a, b, (((1,), (1,)), ((), ())), preferred_element_type=jnp.float32)
+
+
+def column(row, length):
+    return jnp.transpose(jnp.broadcast_to(row, (128, length)))
+
+
+def lanes_to_row(values):
+    folded = values[:, 0:128]
+    for i in range(1, values.shape[1] // 128):
+        folded = folded + values[:, i * 128 : (i + 1) * 128]
+    return jnp.sum(jnp.transpose(folded), axis=0, keepdims=True)
+
+
+def group_kernel(
+    nspot, logits, filt, expr, target, mask, dens,
+    loss_o, gl_o, gf_o, ge_o,
+    probs, gateb, wbuf, ebuf, tbuf, pbuf, dpb, dps, dpt,
+    small, massb, lossb, pair_s, pair_r, stat_s, stat_r,
+    sendx, recvx, sendy, recvy, send2x, recv2x, send2y, recv2y, gwr, held,
+    grad, dsend, dright, dleft, fins, finr, fsend, frecv, fpart,
+    lc, ea_s, ea_r, ez_s, ez_r, es_s, es_r, w_s, w_r, wd_s, wd_r, t_s, t_r,
+    sm_s, sm_r, ma_s, ma_r, lo_s, lo_r, fi_s, fi_r, pr_s, pr_r, st_s, st_r,
+    x_s, x_r, y_s, y_r, x2_s, x2_r, y2_s, y2_r, dr_s, dr_r, dl_s, dl_r, fn_s, fn_r, dp_s, dp_r,
+):
+    f32, bf16 = jnp.float32, jnp.bfloat16
+    rows, cells = logits.shape
+    cd = expr.shape[0]
+    gq = expr.shape[1] // GROUP
+    nz = nspot // GROUP
+    grp = GROUP * rows
+    half = cells // 2
+    cc = half // 4
+    spots_all = nspot * 2 * rows
+    me, j = lax.axis_index("spot"), lax.axis_index("gene")
+    sib = 1 - j
+    z, q = me // GROUP, me % GROUP
+    x, y = q % 2, q // 2
+    nbr = [me, me + 1 - 2 * x, me + 2 - 4 * y, me + 3 - 2 * x - 4 * y]
+    nq = [n % GROUP for n in nbr]
+    here = (me, sib)
+
+    barrier = pltpu.get_barrier_semaphore()
+
+    @pl.loop(1, nspot)
+    def _(r):
+        pl.semaphore_signal(barrier, inc=1, device_id=((me + r) % nspot, j), device_id_type=MESH)
+
+    for k in range(GROUP):
+        pl.semaphore_signal(barrier, inc=1, device_id=(nbr[k], sib), device_id_type=MESH)
+
+    def eblock(h, o):
+        return ebuf.at[h, pl.ds(pl.multiple_of(o * cd, cd), cd), :]
+
+    def ecols(ref, k):
+        return ref.at[:, pl.ds(pl.multiple_of(nq[k] * gq, gq), gq)]
+
+    own_e = pltpu.make_async_copy(ecols(expr, 0), eblock(0, me), lc.at[0])
+    own_e.start()
+    own_t = pltpu.make_async_copy(
+        target.at[pl.ds(pl.multiple_of(j * rows, rows), rows), pl.ds(pl.multiple_of(q * gq, gq), gq)],
+        tbuf.at[0, pl.ds(0, rows), :],
+        lc.at[1],
+    )
+    own_t.start()
+    small[pl.ds(me, 1), 0:2, :] = filt[...][None]
+    small[pl.ds(me, 1), 2:4, :] = dens[...].astype(f32)[None]
+    small[pl.ds(me, 1), 4:8, :] = jnp.zeros((1, 4, 128), f32)
+    mrow = mask[pl.ds(z, 1), :].astype(f32)
+    mine_mask = mask[pl.ds(z, 1), pl.ds(pl.multiple_of(q * gq, gq), gq)].astype(f32)
+    kept_mine = jnp.sum(mrow)
+    pair_s[0, :, 0:gq] = jnp.broadcast_to(mine_mask, (8, gq))
+    pair_s[0, :, gq : 2 * gq] = jnp.broadcast_to(kept_mine, (8, gq))
+    pl.semaphore_wait(barrier, nspot - 1 + GROUP)
+
+    ea = [
+        remote(ecols(expr, k), eblock(0, me), ea_s.at[k], ea_r.at[k], (nbr[k], j))
+        for k in range(1, GROUP)
+    ]
+    for c in ea:
+        c.start()
+
+    def zsend(way, o):
+        return remote(
+            eblock(0, o), eblock(0, o), ez_s.at[way, o], ez_r.at[o], (me + (GROUP if way == 0 else -GROUP), j)
+        )
+
+    def ezwait(o):
+        remote(eblock(0, o), eblock(0, o), ez_s.at[0, o], ez_r.at[o], here).wait_recv()
+
+    def esib(o):
+        return remote(eblock(0, o), eblock(1, o), es_s.at[o], es_r.at[o], here)
+
+    own_e.wait()
+
+    def spread(o):
+        @pl.when(z < nz - 1)
+        def _():
+            zsend(0, o).start()
+
+        @pl.when(z > 0)
+        def _():
+            zsend(1, o).start()
+
+        esib(o).start()
+
+    spread(me)
+
+    def gather(buf, r, ss, rs):
+        return remote(buf.at[me], buf.at[me], ss.at[r], rs.at[r], ((me + r) % nspot, j))
+
+    def gather_start(buf, ss, rs):
+        @pl.loop(1, nspot)
+        def _(r):
+            gather(buf, r, ss, rs).start()
+
+    def gather_wait(buf, ss, rs):
+        @pl.loop(1, nspot)
+        def _(r):
+            o = (me + nspot - r) % nspot
+            remote(buf.at[o], buf.at[o], ss.at[r], rs.at[r], here).wait_recv()
+
+    def gather_sent(buf, ss, rs):
+        @pl.loop(1, nspot)
+        def _(r):
+            gather(buf, r, ss, rs).wait_send()
+
+    gather_start(small, sm_s, sm_r)
+
+    def pair(i):
+        return remote(pair_s.at[i], pair_r.at[i], pr_s.at[i], pr_r.at[i], here)
+
+    pair(0).start()
+
+    def tcopy(k, h):
+        jj = j if h == 0 else sib
+        src = target.at[
+            pl.ds(pl.multiple_of(jj * rows, rows), rows), pl.ds(pl.multiple_of(nq[k] * gq, gq), gq)
+        ]
+        i = k * 2 + h
+        return remote(
+            src, tbuf.at[h, pl.ds(POS[k] * rows, rows), :], t_s.at[i], t_r.at[i], (nbr[k], jj)
+        )
+
+    tlist = [(k, h) for k in (1, 2, 3, 0) for h in (0, 1) if (k, h) != (0, 0)]
+    for k, h in tlist:
+        tcopy(k, h).start()
+
+    for k in range(1, GROUP):
+        remote(eblock(0, nbr[k]), eblock(0, nbr[k]), ea_s.at[k], ea_r.at[k], here).wait_recv()
+        spread(nbr[k])
+
+    step = 16
+
+    @pl.loop(0, rows // step)
+    def _(i):
+        at = pl.ds(pl.multiple_of(i * step, step), step)
+        s = logits[at, :].astype(f32)
+        e = jnp.exp(s - jnp.max(s, axis=1, keepdims=True))
+        probs[at, :] = e / jnp.sum(e, axis=1, keepdims=True)
+
+    gather_wait(small, sm_s, sm_r)
+    for o in range(nspot):
+        for h in range(cd // 128):
+            g = jax.nn.sigmoid(small[o, h : h + 1, :])
+            gateb[:, o * cd + h * 128 : o * cd + (h + 1) * 128] = jnp.broadcast_to(g, (8, 128))
+
+    @pl.loop(0, rows // step)
+    def _(i):
+        at = pl.ds(pl.multiple_of(i * step, step), step)
+        sent = probs[at, :].astype(bf16).astype(f32)
+        wbuf[0, at, :] = (gateb[0:1, :] * sent).astype(bf16)
+
+    lo, hi = pl.ds(0, half), pl.ds(half, half)
+
+    def wrows(h, k):
+        return wbuf.at[h, pl.ds(POS[k] * rows, rows), :]
+
+    def wcopy(i):
+        src_k, dst_k, cols, to = (
+            (0, 1, lo, 1), (0, 1, hi, 1), (0, 2, hi, 2), (0, 2, lo, 2), (1, 3, lo, 2), (2, 3, hi, 1),
+        )[i]
+        return remote(
+            wbuf.at[0, pl.ds(POS[src_k] * rows, rows), cols],
+            wbuf.at[0, pl.ds(POS[dst_k] * rows, rows), cols],
+            w_s.at[i],
+            w_r.at[i],
+            (nbr[to], j),
+        )
+
+    def wsib(k):
+        return remote(wrows(0, k), wrows(1, k), wd_s.at[k], wd_r.at[k], here)
+
+    for i in (0, 2, 1, 3):
+        wcopy(i).start()
+    wsib(0).start()
+
+    massb[pl.ds(me, 1), :, :] = dot_nt(jnp.ones((8, cells), bf16), wbuf[0, 0:rows, :])[None]
+    gather_start(massb, ma_s, ma_r)
+
+    for s in range(1, nz):
+        for k in range(GROUP):
+
+            @pl.when(z >= s)
+            def _():
+                o = nbr[k] - GROUP * s
+                ezwait(o)
+
+                @pl.when(z < nz - 1)
+                def _():
+                    zsend(0, o).start()
+
+                esib(o).start()
+
+            @pl.when(z + s <= nz - 1)
+            def _():
+                o = nbr[k] + GROUP * s
+                ezwait(o)
+
+                @pl.when(z > 0)
+                def _():
+                    zsend(1, o).start()
+
+                esib(o).start()
+
+        if s == max(nz - 2, 1):
+            wcopy(0).wait_recv()
+            wcopy(4).start()
+            wcopy(2).wait_recv()
+            wcopy(5).start()
+    wcopy(1).wait_recv()
+    wsib(1).start()
+    wcopy(3).wait_recv()
+    wsib(2).start()
+
+    gather_wait(massb, ma_s, ma_r)
+    count_total = jnp.zeros((1, 128), f32)
+    gate_sum = jnp.zeros((1, 128), f32)
+    for o in range(nspot):
+        count_total = count_total + small[o, 2:3, :] + small[o, 3:4, :]
+    for o in range(cells // 128):
+        gate_sum = gate_sum + gateb[0:1, o * 128 : (o + 1) * 128]
+    count_total = jnp.sum(count_total)
+    gate_total = jnp.sum(gate_sum)
+    mass_sum = jnp.zeros((1, 128), f32)
+    kl_sum = jnp.zeros((1, 128), f32)
+    share_sum = jnp.zeros((1, 128), f32)
+    for o in range(nspot):
+        m = massb[o, 0:1, :]
+        share = jnp.where(j == 0, small[o, 2:3, :], small[o, 3:4, :]) / count_total
+        mass_sum = mass_sum + m
+        share_sum = share_sum + share
+        kl_sum = kl_sum + share * (jnp.log(share) - jnp.log(m))
+    pair_s[1, 0:1, 0:128] = mass_sum
+    pair_s[1, 1:2, 0:128] = kl_sum
+    pair_s[1, 2:3, 0:128] = share_sum
+    pair(1).start()
+    pair(0).wait_recv()
+    kept = jnp.maximum(kept_mine + jnp.sum(pair_r[0, 0:1, gq : gq + 1]), 1.0)
+    pair(1).wait_recv()
+    mass_total = jnp.sum(mass_sum + pair_r[1, 0:1, 0:128])
+    kl_all = jnp.sum(kl_sum + pair_r[1, 1:2, 0:128])
+    share_all = jnp.sum(share_sum + pair_r[1, 2:3, 0:128])
+    log_total = jnp.log(jnp.full((1, 128), mass_total))
+    excess = gate_total / count_total - 1.0
+    my_dens = small[pl.ds(me, 1), pl.ds(2 + j, 1), :].reshape(1, 128)
+    my_mass = massb[pl.ds(me, 1), 0:1, :].reshape(1, 128)
+    gm_row = (1.0 / mass_total - my_dens / count_total / my_mass).astype(bf16).astype(f32)
+    gm = column(gm_row, rows)
+
+    wcopy(4).wait_recv()
+    wcopy(5).wait_recv()
+    wsib(3).start()
+
+    @pl.loop(0, nspot)
+    def _(o):
+        esib(o).wait_recv()
+
+    own_t.wait()
+    for k, h in tlist:
+        tcopy(k, h).wait_recv()
+    kb = 512
+    for h in range(2):
+        pbuf[:, h * gq : (h + 1) * gq] = jnp.dot(
+            wbuf[0, :, 0:kb], ebuf[h, 0:kb, :], preferred_element_type=f32
+        )
+
+    @pl.loop(1, cells // kb)
+    def _(i):
+        at = pl.ds(pl.multiple_of(i * kb, kb), kb)
+        for h in range(2):
+            pbuf[:, h * gq : (h + 1) * gq] += jnp.dot(
+                wbuf[0, :, at], ebuf[h, at, :], preferred_element_type=f32
+            )
+
+    for h in range(2):
+        p = pbuf[:, h * gq : (h + 1) * gq]
+        t = tbuf[h].astype(f32)
+        for i, v in enumerate((p * t, p * p, t * t)):
+            stat_s[0, i : i + 1, h * gq : (h + 1) * gq] = jnp.sum(v, axis=0, keepdims=True)
+            r = lanes_to_row(v)
+            if h == 0:
+                stat_s[1, i : i + 1, 0:grp] = r
+            else:
+                stat_s[1, i : i + 1, 0:grp] += r
+
+    def stat(k):
+        if k == 0:
+            return remote(stat_s.at[0], stat_r.at[0], st_s.at[0], st_r.at[0], here)
+        return remote(stat_s.at[1], stat_r.at[k], st_s.at[k], st_r.at[k], (nbr[k], j))
+
+    for k in (3, 1, 2, 0):
+        stat(k).start()
+    stat(0).wait_recv()
+    order = (slice(gq, 2 * gq), slice(0, gq))
+    slide = [
+        jnp.concatenate([stat_r[0, i : i + 1, c] for c in order], axis=1) + stat_s[0, i : i + 1, :]
+        for i in range(3)
+    ]
+    dots = slide[0]
+    slide_a = lax.rsqrt(slide[1] + eps_norm)
+    slide_b = lax.rsqrt(slide[2] + eps_norm)
+    maskf = jnp.concatenate([mine_mask, pair_r[0, 0:1, 0:gq]], axis=1)
+    weight = maskf / kept / SLIDES
+    coef_t = -weight * slide_a * slide_b
+    coef_p = weight * dots * slide_a**3 * slide_b
+    cos_gene = (dots * slide_a * slide_b)[:, 0:gq]
+    gene_part = jnp.sum(mine_mask * cos_gene / kept)
+    for k in (1, 2, 3):
+        stat(k).wait_recv()
+    at_pos = {0: 0, 1: 1, 2: 3, 3: 2}
+    spot = []
+    for i in range(3):
+        parts = []
+        for p in range(GROUP):
+            k = at_pos[p]
+            v = stat_s[1, i : i + 1, p * rows : (p + 1) * rows]
+            there = [
+                stat_r[m, i : i + 1, POS[k ^ m] * rows : (POS[k ^ m] + 1) * rows] for m in (1, 2, 3)
+            ]
+            parts.append((v + there[0]) + (there[1] + there[2]))
+        spot.append(jnp.concatenate(parts, axis=1))
+    spot_a = lax.rsqrt(spot[1] + eps_norm)
+    spot_b = lax.rsqrt(spot[2] + eps_norm)
+    cos_spot = (spot[0] * spot_a * spot_b)[:, 0:rows]
+    col_t = column(-(spot_a * spot_b) / spots_all, grp)
+    col_p = column(spot[0] * spot_a**3 * spot_b / spots_all, grp)
+
+    for g in range(2 * gq // 128):
+        at = slice(g * 128, (g + 1) * 128)
+        t = tbuf[g * 128 // gq, :, (g * 128) % gq : (g * 128) % gq + 128].astype(f32)
+        dpb[:, at] = ((coef_t[:, at] + col_t) * t + (coef_p[:, at] + col_p) * pbuf[:, at]).astype(bf16)
+    dps_copy = remote(dpb.at[:, pl.ds(gq, gq)], dps, dp_s.at[0], dp_r.at[0], here)
+    dps_copy.start()
+    lossb[pl.ds(me, 1), :, :] = jnp.broadcast_to(
+        (-gene_part / SLIDES - jnp.sum(cos_spot) / spots_all), (1, 8, 128)
+    )
+    gather_start(lossb, lo_s, lo_r)
+
+    def xcopy(c):
+        return remote(sendx.at[c], recvx.at[c], x_s.at[c], x_r.at[c], (nbr[1], j))
+
+    def ycopy(c):
+        return remote(sendy.at[c], recvy.at[c], y_s.at[c], y_r.at[c], (nbr[2], j))
+
+    def x2copy(c):
+        return remote(send2x.at[c], recv2x.at[c], x2_s.at[c], x2_r.at[c], (nbr[1], j))
+
+    def y2copy(c):
+        return remote(send2y.at[c], recv2y.at[c], y2_s.at[c], y2_r.at[c], (nbr[2], j))
+
+    def weight_grad(at):
+        return dot_nt(dpb[:, 0:gq], ebuf[0, at, :]) + dot_nt(dpb[:, gq : 2 * gq], ebuf[1, at, :])
+
+    dpt[:, 0:grp] = jnp.transpose(dpb[:, 0:gq].astype(f32)).astype(bf16)
+    wsib_pos = [wsib(k) for k in range(GROUP)]
+    for w in wsib_pos:
+        w.wait_recv()
+    dps_copy.wait_recv()
+    dpt[:, grp : 2 * grp] = jnp.transpose(dps[...].astype(f32)).astype(bf16)
+
+    def dsend_to(way, o):
+        if way == 0:
+            return remote(dsend.at[o], dright.at[o], dr_s.at[o], dr_r.at[o], (me + GROUP, j))
+        return remote(dsend.at[o], dleft.at[o], dl_s.at[o], dl_r.at[o], (me - GROUP, j))
+
+    up = z // (nz // 2)
+
+    @pl.loop(0, 4)
+    def _(c):
+        lo_at = pl.ds(pl.multiple_of(c * cc, cc), cc)
+        d = weight_grad(lo_at)
+        gwr[:, lo_at] = d[0:rows]
+        sendx[c] = d[rows : 3 * rows].astype(bf16)
+        held[0, :, lo_at] = d[3 * rows : 4 * rows]
+        xcopy(c).start()
+        hi_at = pl.ds(pl.multiple_of(half + c * cc, cc), cc)
+        d = weight_grad(hi_at)
+        gwr[:, hi_at] = d[0:rows]
+        sendy[c] = d[2 * rows : 4 * rows].astype(bf16)
+        held[1, :, lo_at] = d[rows : 2 * rows]
+        ycopy(c).start()
+        k = 3 - c
+        kx, ky = k % 2, k // 2
+        kq = (x + kx - 2 * x * kx) + 2 * (y + ky - 2 * y * ky)
+
+        @pl.loop(0, nz)
+        def _(u):
+            to = up * u + (1 - up) * (nz - 1 - u)
+            o = to * GROUP + kq
+            at = pl.ds(pl.multiple_of(o * cd, cd), cd)
+            v = jnp.dot(dpt[:, 0:grp], wbuf[0, :, at], preferred_element_type=f32) + jnp.dot(
+                dpt[:, grp : 2 * grp], wbuf[1, :, at], preferred_element_type=f32
+            )
+            grad[o] = v
+
+            @pl.when((z == 0) & (to > 0))
+            def _():
+                dsend[o] = v.astype(bf16)
+                dsend_to(0, o).start()
+
+            @pl.when((z == nz - 1) & (to < nz - 1))
+            def _():
+                dsend[o] = v.astype(bf16)
+                dsend_to(1, o).start()
+
+    def fin(k):
+        return remote(fins.at[k - 1], finr.at[k - 1], fn_s.at[k], fn_r.at[k], (nbr[k], j))
+
+    def relay(c):
+        lo_at = pl.ds(c * cc, cc)
+        xcopy(c).wait_recv()
+        send2y[c] = (held[0, :, lo_at] + recvx[c, rows : 2 * rows].astype(f32)).astype(bf16)
+        y2copy(c).start()
+        gwr[:, lo_at] += recvx[c, 0:rows].astype(f32)
+        ycopy(c).wait_recv()
+        send2x[c] = (held[1, :, lo_at] + recvy[c, 0:rows].astype(f32)).astype(bf16)
+        x2copy(c).start()
+        gwr[:, pl.ds(half + c * cc, cc)] += recvy[c, rows : 2 * rows].astype(f32)
+
+    for n, k in enumerate((3, 2, 1, 0)):
+        for s in range(nz - 1, 0, -1):
+
+            @pl.when((z > 0) & (z + s <= nz - 1))
+            def _():
+                o = nbr[k] + GROUP * s
+                dsend_to(0, o).wait_recv()
+                dsend[o] = (grad[o] + dright[o].astype(f32)).astype(bf16)
+                dsend_to(0, o).start()
+
+            @pl.when((z < nz - 1) & (z >= s))
+            def _():
+                o = nbr[k] - GROUP * s
+                dsend_to(1, o).wait_recv()
+                dsend[o] = (grad[o] + dleft[o].astype(f32)).astype(bf16)
+                dsend_to(1, o).start()
+
+        relay(n)
+        o = nbr[k]
+
+        @pl.when(z > 0)
+        def _():
+            dsend_to(0, o).wait_recv()
+            grad[o] += dright[o].astype(f32)
+
+        @pl.when(z < nz - 1)
+        def _():
+            dsend_to(1, o).wait_recv()
+            grad[o] += dleft[o].astype(f32)
+
+        v = jnp.transpose(grad[o])
+        if k:
+            fins[k - 1] = v.astype(bf16)
+            fin(k).start()
+        else:
+            ge_o[:, pl.ds(pl.multiple_of(q * gq, gq), gq)] = v
+
+    gather_wait(lossb, lo_s, lo_r)
+    total = jnp.zeros((8, 128), f32)
+    for o in range(nspot):
+        total = total + lossb[o]
+    pair_s[2, :, 0:128] = total
+    pair(2).start()
+
+    fpart[...] = jnp.zeros_like(fpart)
+    rowsum = jnp.zeros((rows, 128), f32)
+
+    def whole(base, got, rowsum):
+        def one(c, rowsum):
+            at = pl.ds(pl.multiple_of(base + c * cc, cc), cc)
+            got(c).wait_recv()
+            piece = (recv2y if base == 0 else recv2x)[c]
+            p = probs[:, at]
+            gw = gwr[:, at] + piece.astype(f32) + jnp.concatenate([gm] * (cc // 128), axis=1)
+            fpart[:, at] = jnp.sum(gw * p.astype(bf16).astype(f32), axis=0, keepdims=True)
+            gp = (gateb[0:1, at] * gw).astype(bf16).astype(f32)
+            gwr[:, at] = gp
+            v = p * gp
+            for i in range(cc // 128):
+                rowsum = rowsum + v[:, i * 128 : (i + 1) * 128]
+            return rowsum
+
+        return lax.fori_loop(0, 4, one, rowsum)
+
+    rowsum = whole(0, y2copy, rowsum)
+    rowsum = whole(half, x2copy, rowsum)
+
+    for o in range(nspot):
+        fsend[o] = fpart[:, o * cd : (o + 1) * cd]
+    frecv[pl.ds(me, 1)] = fsend[pl.ds(me, 1)]
+
+    def fcopy(r):
+        o = (me + r) % nspot
+        return remote(fsend.at[o], frecv.at[me], fi_s.at[r], fi_r.at[r], (o, j))
+
+    @pl.loop(1, nspot)
+    def _(r):
+        fcopy(r).start()
+
+    total_row = jnp.sum(rowsum, axis=1, keepdims=True)
+
+    @pl.loop(0, cells // cc)
+    def _(c):
+        at = pl.ds(pl.multiple_of(c * cc, cc), cc)
+        gl_o[:, at] = probs[:, at] * (gwr[:, at] - total_row)
+
+    for k in (3, 2, 1):
+        fin(k).wait_recv()
+        ge_o[:, pl.ds(pl.multiple_of(nq[k] * gq, gq), gq)] = finr[k - 1].astype(f32)
+
+    @pl.loop(1, nspot)
+    def _(r):
+        o = (me + nspot - r) % nspot
+        remote(fsend.at[o], frecv.at[o], fi_s.at[r], fi_r.at[r], here).wait_recv()
+
+    ftotal = frecv[0]
+    for o in range(1, nspot):
+        ftotal = ftotal + frecv[o]
+    pair_s[3, 0:1, 0:cd] = ftotal
+    pair(3).start()
+    pair(2).wait_recv()
+    loss_sum = jnp.sum(total[0:1, 0:1] + pair_r[2, 0:1, 0:1])
+    log_all = jnp.sum(log_total[:, 0:1])
+    loss_o[0, 0] = loss_sum + kl_all + share_all * log_all + excess * excess
+    pair(3).wait_recv()
+    my_gate = jax.nn.sigmoid(
+        jnp.concatenate([small[pl.ds(me, 1), h : h + 1, :].reshape(1, 128) for h in range(cd // 128)], axis=1)
+    )
+    gf_o[...] = (ftotal + pair_r[3, 0:1, 0:cd] + 2.0 * excess / count_total) * my_gate * (1.0 - my_gate)
+
+    for c in ea:
+        c.wait_send()
+    gather_sent(small, sm_s, sm_r)
+    gather_sent(massb, ma_s, ma_r)
+    gather_sent(lossb, lo_s, lo_r)
+
+    @pl.loop(1, nspot)
+    def _(r):
+        fcopy(r).wait_send()
+
+    for i in range(4):
+        pair(i).wait_send()
+        stat(i).wait_send()
+        wsib(i).wait_send()
+    for k, h in tlist:
+        tcopy(k, h).wait_send()
+    for i in range(6):
+        wcopy(i).wait_send()
+    for k in range(1, GROUP):
+        fin(k).wait_send()
+    dps_copy.wait_send()
+
+    @pl.loop(0, 4)
+    def _(c):
+        xcopy(c).wait_send()
+        ycopy(c).wait_send()
+        x2copy(c).wait_send()
+        y2copy(c).wait_send()
+
+    @pl.loop(0, nspot)
+    def _(o):
+        esib(o).wait_send()
+        at = o // GROUP
+
+        @pl.when((z < nz - 1) & (at <= z))
+        def _():
+            zsend(0, o).wait_send()
+
+        @pl.when((z > 0) & (at >= z))
+        def _():
+            zsend(1, o).wait_send()
+
+        @pl.when((z < nz - 1) & (at > z))
+        def _():
+            dsend_to(0, o).wait_send()
+
+        @pl.when((z > 0) & (at < z))
+        def _():
+            dsend_to(1, o).wait_send()
+
+
+def grouped(logits, filt, expr, target, gene_mask, density):
+    f32, bf16 = jnp.float32, jnp.bfloat16
+    nspot = lax.axis_size("spot")
+    rows, cells = logits.shape
+    cd, half = expr.shape
+    gq = half // GROUP
+    grp = GROUP * rows
+    hc = cells // 2
+    cc = hc // 4
+    wide = max(2 * gq, grp, cd, 128)
+    dma = pltpu.SemaphoreType.DMA
+
+    def vmem(*shape, dtype=f32):
+        return pltpu.VMEM(shape, dtype)
+
+    buffers = [
+        vmem(rows, cells), vmem(8, cells), vmem(2, grp, cells, dtype=bf16), vmem(2, cells, gq, dtype=bf16),
+        vmem(2, grp, gq, dtype=bf16), vmem(grp, 2 * gq), vmem(grp, 2 * gq, dtype=bf16),
+        vmem(grp, gq, dtype=bf16), vmem(gq, 2 * grp, dtype=bf16),
+        vmem(nspot, 8, 128), vmem(nspot, 8, 128), vmem(nspot, 8, 128),
+        vmem(4, 8, wide), vmem(4, 8, wide), vmem(2, 8, wide), vmem(4, 8, wide),
+        vmem(4, 2 * rows, cc, dtype=bf16), vmem(4, 2 * rows, cc, dtype=bf16),
+        vmem(4, 2 * rows, cc, dtype=bf16), vmem(4, 2 * rows, cc, dtype=bf16),
+        vmem(4, rows, cc, dtype=bf16), vmem(4, rows, cc, dtype=bf16),
+        vmem(4, rows, cc, dtype=bf16), vmem(4, rows, cc, dtype=bf16),
+        vmem(rows, cells), vmem(2, rows, hc),
+        vmem(nspot, gq, cd), vmem(nspot, gq, cd, dtype=bf16),
+        vmem(nspot, gq, cd, dtype=bf16), vmem(nspot, gq, cd, dtype=bf16),
+        vmem(3, cd, gq, dtype=bf16), vmem(3, cd, gq, dtype=bf16),
+        vmem(nspot, 1, cd), vmem(nspot, 1, cd), vmem(1, cells),
+    ]
+    sems = [
+        dma((2,)), dma((4,)), dma((4,)), dma((2, nspot)), dma((nspot,)), dma((nspot,)), dma((nspot,)),
+        dma((6,)), dma((6,)), dma((4,)), dma((4,)), dma((8,)), dma((8,)),
+        dma((nspot,)), dma((nspot,)), dma((nspot,)), dma((nspot,)),
+        dma((nspot,)), dma((nspot,)), dma((nspot,)), dma((nspot,)),
+        dma((4,)), dma((4,)), dma((4,)), dma((4,)),
+        dma((4,)), dma((4,)), dma((4,)), dma((4,)), dma((4,)), dma((4,)), dma((4,)), dma((4,)),
+        dma((nspot,)), dma((nspot,)), dma((nspot,)), dma((nspot,)), dma((4,)), dma((4,)), dma((1,)), dma((1,)),
+    ]
+    v, a = pl.BlockSpec(memory_space=pltpu.VMEM), pl.BlockSpec(memory_space=pl.ANY)
+    loss, grad_logits, grad_filt, grad_expr = pl.pallas_call(
+        functools.partial(group_kernel, nspot),
+        out_shape=[
+            jax.ShapeDtypeStruct((1, 1), f32),
+            jax.ShapeDtypeStruct((rows, cells), f32),
+            jax.ShapeDtypeStruct((1, cd), f32),
+            jax.ShapeDtypeStruct((cd, half), f32),
+        ],
+        in_specs=[v, v, a, a, v, v],
+        out_specs=[pl.BlockSpec(memory_space=pltpu.SMEM), v, v, v],
+        scratch_shapes=buffers + sems,
+        compiler_params=pltpu.CompilerParams(
+            collective_id=0, has_side_effects=True, vmem_limit_bytes=VMEM_BYTES
+        ),
+        name="group_step",
+    )(logits, filt.reshape(-1, 128), expr, target, gene_mask, density.reshape(-1, 128))
+    return (loss.reshape(()), grad_logits, grad_filt.reshape(-1), grad_expr)
+
+
+def fits(logits, filt, expr):
+    nspot = lax.axis_size("spot")
+    rows, cells = logits.shape
+    held = cells * (expr.shape[1] // GROUP) * 2 * 2 + 2 * GROUP * rows * cells * 2
+    return (
+        nspot == GROUP * SLIDES
+        and lax.axis_size("gene") == 2
+        and rows == 128
+        and filt.shape[0] == 256
+        and held <= 16 << 20
+    )
+
+
+def per_device(logits, filt, expr, target, gene_mask, density):
+    plan = grouped if fits(logits, filt, expr) else streamed
+    return plan(logits, filt, expr, target, gene_mask, density)
+
+
 def solution(mesh):
     in_specs = (
         P(("spot", "gene"), None),

time: 750 us -> 130 us (0.17)
  blocking collectives: 382 us -> 0 us
  waiting for transfers between devices: 295 us -> 0 us
  Pallas kernels: 0 us -> 123 us
  matrix products: 28 us -> 0 us
  other arithmetic: 20.3 us -> 0 us
  between operations: 20.3 us -> 2.33 us
    reduce_scatter x2 -> x0, waiting for transfers between devices: 214 us -> none  [the longest x1 214 us: per_device(): lax.psum_scatter(partial_pred.reshape(nspot, owned, half), 'spot', scatte...]
    all_to_all x2 -> x0, blocking collectives: 132 us -> none  [the longest x1 97.5 us: per_device(): lax.all_to_all(terms, 'spot', split_axis=0, concat_axis=3, tiled=True)]
    psum x5 -> x0, blocking collectives: 125 us -> none  [the longest x2 118 us: per_device(): lax.psum((slide_moments(onehot, pred, truth), jnp.sum(mass), gate_part, j...]
    pallas_call x0 -> x1, Pallas kernels: none -> 123 us  [grouped(): pl.pallas_call(functools.partial(group_kernel, nspot), out_shape=[jax.Sha...]
    unnamed x1 -> x0, blocking collectives: 88.4 us -> none
    all_gather x2 -> x0, waiting for transfers between devices: 81.7 us -> none  [the longest x1 73.4 us: per_device(): lax.all_gather(grad_pred.astype(bf16).reshape(1, owned, half), 'spot', ax...]
    all_gather x1 -> x0, blocking collectives: 35.7 us -> none  [per_device(): lax.all_gather(grad_mass.astype(bf16).reshape(1, owned), 'spot', axis=0,...]
    dot_general x8 -> x0, matrix products: 28 us -> none  [the longest x1 9.65 us: per_device(): partial_pred = jnp.dot(weighted, expr, preferred_element_type=f32)]
  transfers between devices with their start and end apart: 4 -> 0, of which waited for: 3 -> 0; matrix products, arithmetic and copies ran while one was open for 2% -> 0% of each run, Pallas kernels for 0% -> 0%
where the time goes in v1:
time: 130 us
  Pallas kernels  123 us (95%)
  local copies, waits for them, and re-layouts  4.74 us (4%)
  between operations  2.33 us (2%)
    pallas_call x1, Pallas kernels, grouped(): pl.pallas_call(functools.partial(group_kernel, nspot), out_shape=[jax.Sha...  123 us
    unnamed x7, local copies, waits for them, and re-layouts  4.74 us

profile of v1, /device:TPU:0, one launch (start us, length us, event | category | flops | bytes accessed | tf_op | source)
XLA Modules:
  0.0 129.8 jit_solution(599939128032480500)
XLA Ops:
  0.6 122.7 %group_step.1 = (f32[1,1]{1,0:T(1,128)}, f32[128,4096]{1,0:T(8,128)}, f32[1,256]{1,0:T(1,128)}, f32[256,1024]{1,0:T(8,128)}) custom-call(bf16[128,4096]{1,0:T(8,128)(2,1)} %logits.1, f32[2,128]{1,0:T(2,128)} %bitcast.4, bf16[256,1024]{1,0:T(8,128)(2,1)} %expr.1, bf16[256,1024]{1,0:T(8,128)(2,1)} %target.1, s32[4,1024]{1,0:T(4,128)} %mask.1, s32[2,128]{1,0:T(2,128)} %bitcast.5), custom_call_target="tpu_custom_call" | custom-call | tf_op jit(solution)/shard_map/group_step/pallas_call | solution.py:807
  123.9 0.0 copy-start.1
  123.9 0.0 copy-start
  123.9 3.2 %copy.15 = f32[128,4096]{1,0:T(8,128)} copy(f32[128,4096]{1,0:T(8,128)} %get-tuple-element.17) | data formatting | bytes 4194304
  127.1 0.0 copy-done.1
  127.1 0.6 copy.16
  127.7 0.0 copy-done
  127.7 1.0 copy.17
Async XLA Ops:
  123.9 3.2 %copy-start.1 = (f32[1,256]{1,0:T(1,128)S(1)}, f32[1,256]{1,0:T(1,128)}, u32[]{:S(2)}) copy-start(f32[1,256]{1,0:T(1,128)} %get-tuple-element.10) | copy-start | bytes 3076
  123.9 3.8 %copy-start = (f32[256,1024]{1,0:T(8,128)S(1)}, f32[256,1024]{1,0:T(8,128)}, u32[]{:S(2)}) copy-start(f32[256,1024]{1,0:T(8,128)} %get-tuple-element.19) | copy-start | bytes 3145732

commit v2 on v0

--- a/solution.py
+++ b/solution.py
@@ -1,6 +1,10 @@
+import functools
+
 import jax
 import jax.numpy as jnp
 from jax import lax
+from jax.experimental import pallas as pl
+from jax.experimental.pallas import tpu as pltpu
 from jax.sharding import PartitionSpec as P
 
 SPOTS = 4096
@@ -59,7 +63,7 @@
     return (grad_pred, spot_stats[0] * spot_a * spot_b)
 
 
-def per_device(logits, filt, expr, target, gene_mask, density):
+def streamed(logits, filt, expr, target, gene_mask, density):
     f32 = jnp.float32
     bf16 = jnp.bfloat16
     nspot = lax.axis_size("spot")
@@ -145,6 +149,896 @@
     return (loss, grad_logits, grad_filt, grad_expr)
 
 
+GROUP = 4
+MESH = pl.DeviceIdType.MESH
+VMEM_BYTES = 48 << 20
+LAST_BYTES = 16 << 20
+POS = {0: 0, 1: 1, 3: 2, 2: 3}
+
+
+def remote(src, dst, send, recv, dev):
+    return pltpu.make_async_remote_copy(
+        src_ref=src, dst_ref=dst, send_sem=send, recv_sem=recv, device_id=dev, device_id_type=MESH
+    )
+
+
+def dot_nt(a, b):
+    return lax.dot_general(a, b, (((1,), (1,)), ((), ())), preferred_element_type=jnp.float32)
+
+
+def column(row, length):
+    return jnp.transpose(jnp.broadcast_to(row, (128, length)))
+
+
+def fold(values):
+    total = values[:, 0:128]
+    for i in range(1, values.shape[1] // 128):
+        total = total + values[:, i * 128 : (i + 1) * 128]
+    return total
+
+
+def lanes_to_row(values):
+    return jnp.sum(jnp.transpose(fold(values)), axis=0, keepdims=True)
+
+
+def group_kernel(
+    nspot, logits_h, filt_h, expr, target, mask_h, dens_h,
+    loss_o, probs, gpb, tot_o, gf_o, ge_o,
+    logits, filt, mask, dens, gateb, raw, wbuf, ebuf, tbuf, pbuf, dpb, dps, dpt,
+    small, massb, pair_s, pair_r, stat_s, stat_r,
+    sendx, recvx, sendy, recvy, send2x, recv2x, send2y, recv2y, gwr, held, rowsum,
+    grad, dsend, dright, dleft, fins, gexpr, fsend, frecv,
+    lc, ea_s, ea_r, ez_s, ez_r, es_s, es_r, wx_s, wx_r, wy_s, wy_r, wd_s, wd_r, t_s, t_r,
+    sm_s, sm_r, sz_s, sz_r, ma_s, ma_r, fi_s, fi_r, pr_s, pr_r, st_s, st_r,
+    x_s, x_r, y_s, y_r, x2_s, x2_r, y2_s, y2_r, dr_s, dr_r, dl_s, dl_r, fn_s, fn_r, dp_s, dp_r,
+):
+    f32, bf16 = jnp.float32, jnp.bfloat16
+    rows, cells = probs.shape
+    cd = expr.shape[0]
+    gq = expr.shape[1] // GROUP
+    nz = nspot // GROUP
+    grp = GROUP * rows
+    half = cells // 2
+    cc = half // 4
+    spots_all = nspot * 2 * rows
+    me, j = lax.axis_index("spot"), lax.axis_index("gene")
+    sib = 1 - j
+    z, q = me // GROUP, me % GROUP
+    x, y = q % 2, q // 2
+    nbr = [me, me + 1 - 2 * x, me + 2 - 4 * y, me + 3 - 2 * x - 4 * y]
+    nq = [n % GROUP for n in nbr]
+    here = (me, sib)
+    has_right, has_left = z < nz - 1, z > 0
+
+    barrier = pltpu.get_barrier_semaphore()
+
+    def greet(dev):
+        pl.semaphore_signal(barrier, inc=1, device_id=dev, device_id_type=MESH)
+
+    for k in (1, 2, 3):
+        greet((nbr[k], j))
+
+    @pl.when(has_right)
+    def _():
+        greet((me + GROUP, j))
+
+    @pl.when(has_left)
+    def _():
+        greet((me - GROUP, j))
+
+    for k in (3, 1, 2, 0):
+        greet((nbr[k], sib))
+
+    def eblock(h, o):
+        return ebuf.at[h, pl.ds(pl.multiple_of(o * cd, cd), cd), :]
+
+    def ecols(ref, k):
+        return ref.at[:, pl.ds(pl.multiple_of(nq[k] * gq, gq), gq)]
+
+    step = 32
+    loads = [
+        pltpu.make_async_copy(logits_h, logits, lc.at[0]),
+        pltpu.make_async_copy(filt_h, filt, lc.at[1]),
+        pltpu.make_async_copy(mask_h, mask, lc.at[2]),
+        pltpu.make_async_copy(dens_h, dens, lc.at[3]),
+        pltpu.make_async_copy(ecols(expr, 0), eblock(0, me), lc.at[4]),
+        pltpu.make_async_copy(
+            target.at[
+                pl.ds(pl.multiple_of(j * rows, rows), rows), pl.ds(pl.multiple_of(q * gq, gq), gq)
+            ],
+            tbuf.at[0, pl.ds(0, rows), :],
+            lc.at[5],
+        ),
+    ]
+    for c in loads:
+        c.start()
+    loads[0].wait()
+
+    @pl.loop(0, rows // step)
+    def _(i):
+        at = pl.ds(pl.multiple_of(i * step, step), step)
+        s = logits[at, :].astype(f32)
+        top = jnp.max(s, axis=1, keepdims=True)
+        e = jnp.exp(s - top)
+        total = jnp.sum(e, axis=1, keepdims=True)
+        p = e * (1.0 / total)
+        probs[at, :] = p
+        raw[at, :] = p.astype(bf16)
+
+    for c in loads[1:4]:
+        c.wait()
+    small[pl.ds(me, 1), 0:2, :] = filt[...][None]
+    small[pl.ds(me, 1), 2:4, :] = dens[...].astype(f32)[None]
+    small[pl.ds(me, 1), 4:8, :] = jnp.zeros((1, 4, 128), f32)
+    mine_mask = mask[pl.ds(z, 1), pl.ds(pl.multiple_of(q * gq, gq), gq)].astype(f32)
+    kept_mine = jnp.sum(mask[pl.ds(z, 1), :].astype(f32))
+    pair_s[0, :, 0:gq] = jnp.broadcast_to(mine_mask, (8, gq))
+    pair_s[0, :, gq : 2 * gq] = jnp.broadcast_to(kept_mine, (8, gq))
+    for c in loads[4:]:
+        c.wait()
+    pl.semaphore_wait(barrier, 7 + has_right.astype(jnp.int32) + has_left.astype(jnp.int32))
+
+    def smalls(k):
+        return remote(small.at[me], small.at[me], sm_s.at[k], sm_r.at[k], (nbr[k], j))
+
+    for k in (3, 1, 2):
+        smalls(k).start()
+    ea = [
+        remote(ecols(expr, k), eblock(0, me), ea_s.at[k], ea_r.at[k], (nbr[k], j))
+        for k in range(1, GROUP)
+    ]
+    for c in ea:
+        c.start()
+
+    def zsend(way, o):
+        return remote(
+            eblock(0, o), eblock(0, o), ez_s.at[way, o], ez_r.at[o], (me + (GROUP if way == 0 else -GROUP), j)
+        )
+
+    def ezwait(o):
+        remote(eblock(0, o), eblock(0, o), ez_s.at[0, o], ez_r.at[o], here).wait_recv()
+
+    def esib(o):
+        return remote(eblock(0, o), eblock(1, o), es_s.at[o], es_r.at[o], here)
+
+    def spread(o):
+        @pl.when(has_right)
+        def _():
+            zsend(0, o).start()
+
+        @pl.when(has_left)
+        def _():
+            zsend(1, o).start()
+
+        esib(o).start()
+
+    spread(me)
+
+    def plane(at):
+        return small.at[pl.ds(at * GROUP, GROUP)]
+
+    def zsmall(way, at):
+        return remote(
+            plane(at), plane(at), sz_s.at[way, at], sz_r.at[at], (me + (GROUP if way == 0 else -GROUP), j)
+        )
+
+    def pair(i):
+        return remote(pair_s.at[i], pair_r.at[i], pr_s.at[i], pr_r.at[i], here)
+
+    pair(0).start()
+
+    def tcopy(k, h):
+        jj = j if h == 0 else sib
+        src = target.at[
+            pl.ds(pl.multiple_of(jj * rows, rows), rows), pl.ds(pl.multiple_of(nq[k] * gq, gq), gq)
+        ]
+        i = k * 2 + h
+        return remote(
+            src, tbuf.at[h, pl.ds(POS[k] * rows, rows), :], t_s.at[i], t_r.at[i], (nbr[k], jj)
+        )
+
+    tlist = [(k, h) for k in (3, 1, 2, 0) for h in (0, 1) if (k, h) != (0, 0)]
+    for k, h in tlist:
+        tcopy(k, h).start()
+
+    def wcols(way, u):
+        u = u if way == 0 else (u + 4) % 8
+        return pl.ds(u * cc, cc)
+
+    def wrows(p):
+        return pl.ds(p * rows, rows)
+
+    def wown(way, u):
+        to, ss, rs = ((1, wx_s, wx_r), (2, wy_s, wy_r))[way]
+        at = wcols(way, u)
+        return remote(
+            raw.at[wrows(0), at], raw.at[wrows(POS[to]), at], ss.at[u], rs.at[u], (nbr[to], j)
+        )
+
+    def wpass(way, m):
+        to, ss, rs = ((1, wx_s, wx_r), (2, wy_s, wy_r))[way]
+        at = wcols(1 - way, m)
+        return remote(
+            raw.at[wrows(POS[3 - to]), at], raw.at[wrows(2), at], ss.at[8 + m], rs.at[8 + m], (nbr[to], j)
+        )
+
+    def wsib(p, i, at):
+        return remote(wbuf.at[0, wrows(p), at], wbuf.at[1, wrows(p), at], wd_s.at[i], wd_r.at[i], here)
+
+    every = pl.ds(0, cells)
+    for u in range(8):
+        wown(0, u).start()
+        wown(1, u).start()
+
+    for k in (1, 2, 3):
+        remote(small.at[nbr[k]], small.at[nbr[k]], sm_s.at[k], sm_r.at[k], here).wait_recv()
+
+    @pl.when(has_right)
+    def _():
+        zsmall(0, z).start()
+
+    @pl.when(has_left)
+    def _():
+        zsmall(1, z).start()
+
+    def small_hop(s):
+        @pl.when(z >= s)
+        def _():
+            zsmall(0, z - s).wait_recv()
+
+            @pl.when(has_right)
+            def _():
+                zsmall(0, z - s).start()
+
+        @pl.when(z + s <= nz - 1)
+        def _():
+            zsmall(1, z + s).wait_recv()
+
+            @pl.when(has_left)
+            def _():
+                zsmall(1, z + s).start()
+
+    for k in (1, 2, 3):
+        remote(eblock(0, nbr[k]), eblock(0, nbr[k]), ea_s.at[k], ea_r.at[k], here).wait_recv()
+        spread(nbr[k])
+        if k < nz:
+            small_hop(k)
+
+    def gated(p, at):
+        wbuf[0, wrows(p), at] = (gateb[0:1, at] * raw[wrows(p), at].astype(f32)).astype(bf16)
+
+    def gates():
+        for o in range(nspot):
+            for h in range(cd // 128):
+                g = jax.nn.sigmoid(small[o, h : h + 1, :])
+                gateb[:, o * cd + h * 128 : o * cd + (h + 1) * 128] = jnp.broadcast_to(g, (8, 128))
+
+        @pl.loop(0, 8)
+        def _(u):
+            gated(0, pl.ds(pl.multiple_of(u * cc, cc), cc))
+
+        wsib(0, 0, every).start()
+        massb[pl.ds(me, 1), :, :] = dot_nt(jnp.ones((8, cells), bf16), wbuf[0, 0:rows, :])[None]
+
+    n = 0
+    for s in range(1, nz):
+        for k in range(GROUP):
+
+            @pl.when(z >= s)
+            def _():
+                o = nbr[k] - GROUP * s
+                ezwait(o)
+
+                @pl.when(has_right)
+                def _():
+                    zsend(0, o).start()
+
+                esib(o).start()
+
+            @pl.when(z + s <= nz - 1)
+            def _():
+                o = nbr[k] + GROUP * s
+                ezwait(o)
+
+                @pl.when(has_left)
+                def _():
+                    zsend(1, o).start()
+
+                esib(o).start()
+
+            if n == 0:
+                gates()
+            if n >= 4:
+                u = n - 4
+                wown(0, u).wait_recv()
+                wown(1, u).wait_recv()
+                if u < 4:
+                    wpass(0, u).start()
+                    wpass(1, u).start()
+                gated(1, wcols(0, u))
+                gated(3, wcols(1, u))
+            n += 1
+    wsib(1, 1, every).start()
+    wsib(3, 2, every).start()
+
+    @pl.loop(0, nspot)
+    def _(o):
+        esib(o).wait_recv()
+
+    kb = cc
+
+    def project(at, span, first):
+        for h in range(2):
+            v = jnp.dot(wbuf[0, span, at], ebuf[h, at, :], preferred_element_type=f32)
+            to = (span, slice(h * gq, (h + 1) * gq))
+            if first:
+                pbuf[to] = v
+            else:
+                pbuf[to] += v
+
+    early = (slice(0, 2 * rows), slice(3 * rows, 4 * rows))
+    late = slice(2 * rows, 3 * rows)
+    for span in early:
+        project(pl.ds(0, kb), span, True)
+
+    @pl.loop(1, cells // kb)
+    def _(i):
+        for span in early:
+            project(pl.ds(pl.multiple_of(i * kb, kb), kb), span, False)
+
+    for k, h in tlist:
+        tcopy(k, h).wait_recv()
+
+    def moments(p, which):
+        span = slice(p * rows, (p + 1) * rows)
+        for h in range(2):
+            at = slice(h * gq, (h + 1) * gq)
+            t = tbuf[h, span, :].astype(f32)
+            v = pbuf[span, at]
+            for i in which:
+                w = (v * t, v * v, t * t)[i]
+                by_gene = jnp.sum(w, axis=0, keepdims=True)
+                if p == 0:
+                    stat_s[0, i : i + 1, at] = by_gene
+                else:
+                    stat_s[0, i : i + 1, at] += by_gene
+                by_spot = lanes_to_row(w)
+                if h == 0:
+                    stat_s[1, i : i + 1, span] = by_spot
+                else:
+                    stat_s[1, i : i + 1, span] += by_spot
+
+    for p in (0, 1, 3):
+        moments(p, (0, 1, 2))
+    moments(2, (2,))
+    pair(0).wait_recv()
+    kept = jnp.maximum(kept_mine + jnp.sum(pair_r[0, 0:1, gq : gq + 1]), 1.0)
+    weight = jnp.concatenate([mine_mask, pair_r[0, 0:1, 0:gq]], axis=1) / kept / SLIDES
+
+    def gather(buf, r, ss, rs):
+        return remote(buf.at[me], buf.at[me], ss.at[r], rs.at[r], ((me + r) % nspot, j))
+
+    def gather_start(buf, ss, rs):
+        @pl.loop(1, nspot)
+        def _(r):
+            gather(buf, r, ss, rs).start()
+
+    def gather_wait(buf, ss, rs):
+        @pl.loop(1, nspot)
+        def _(r):
+            o = (me + nspot - r) % nspot
+            remote(buf.at[o], buf.at[o], ss.at[r], rs.at[r], here).wait_recv()
+
+    def gather_sent(buf, ss, rs):
+        @pl.loop(1, nspot)
+        def _(r):
+            gather(buf, r, ss, rs).wait_send()
+
+    gather_start(massb, ma_s, ma_r)
+
+    for m in range(4):
+        wpass(0, m).wait_recv()
+        wpass(1, m).wait_recv()
+        for way in (0, 1):
+            at = wcols(1 - way, m)
+            gated(2, at)
+            project(at, late, m == 0 and way == 0)
+    wsib(2, 3, every).start()
+    moments(2, (0, 1))
+
+    def stat(k):
+        if k == 0:
+            return remote(stat_s.at[0], stat_r.at[0], st_s.at[0], st_r.at[0], here)
+        return remote(stat_s.at[1], stat_r.at[k], st_s.at[k], st_r.at[k], (nbr[k], j))
+
+    for k in (3, 1, 2, 0):
+        stat(k).start()
+    stat(0).wait_recv()
+    order = (slice(gq, 2 * gq), slice(0, gq))
+    slide = [
+        jnp.concatenate([stat_r[0, i : i + 1, c] for c in order], axis=1) + stat_s[0, i : i + 1, :]
+        for i in range(3)
+    ]
+    dots = slide[0]
+    slide_a = lax.rsqrt(slide[1] + eps_norm)
+    slide_b = lax.rsqrt(slide[2] + eps_norm)
+    coef_t = -weight * slide_a * slide_b
+    coef_p = weight * dots * slide_a**3 * slide_b
+    cos_gene = (dots * slide_a * slide_b)[:, 0:gq]
+    gene_part = jnp.sum(mine_mask * cos_gene / kept)
+    for k in (1, 2, 3):
+        stat(k).wait_recv()
+    at_pos = {0: 0, 1: 1, 2: 3, 3: 2}
+    spot = []
+    for i in range(3):
+        parts = []
+        for p in range(GROUP):
+            k = at_pos[p]
+            v = stat_s[1, i : i + 1, p * rows : (p + 1) * rows]
+            there = [
+                stat_r[m, i : i + 1, POS[k ^ m] * rows : (POS[k ^ m] + 1) * rows] for m in (1, 2, 3)
+            ]
+            parts.append((v + there[0]) + (there[1] + there[2]))
+        spot.append(jnp.concatenate(parts, axis=1))
+    spot_a = lax.rsqrt(spot[1] + eps_norm)
+    spot_b = lax.rsqrt(spot[2] + eps_norm)
+    cos_spot = (spot[0] * spot_a * spot_b)[:, 0:rows]
+    col_t = column(-(spot_a * spot_b) / spots_all, grp)
+    col_p = column(spot[0] * spot_a**3 * spot_b / spots_all, grp)
+
+    for g in range(2 * gq // 128):
+        at = slice(g * 128, (g + 1) * 128)
+        t = tbuf[g * 128 // gq, :, (g * 128) % gq : (g * 128) % gq + 128].astype(f32)
+        dpb[:, at] = ((coef_t[:, at] + col_t) * t + (coef_p[:, at] + col_p) * pbuf[:, at]).astype(bf16)
+    dps_copy = remote(dpb.at[:, pl.ds(gq, gq)], dps, dp_s.at[0], dp_r.at[0], here)
+    dps_copy.start()
+
+    def xcopy(c):
+        return remote(sendx.at[c], recvx.at[c], x_s.at[c], x_r.at[c], (nbr[1], j))
+
+    def ycopy(c):
+        return remote(sendy.at[c], recvy.at[c], y_s.at[c], y_r.at[c], (nbr[2], j))
+
+    def x2copy(c):
+        return remote(send2x.at[c], recv2x.at[c], x2_s.at[c], x2_r.at[c], (nbr[1], j))
+
+    def y2copy(c):
+        return remote(send2y.at[c], recv2y.at[c], y2_s.at[c], y2_r.at[c], (nbr[2], j))
+
+    def weight_grad(at):
+        return dot_nt(dpb[:, 0:gq], ebuf[0, at, :]) + dot_nt(dpb[:, gq : 2 * gq], ebuf[1, at, :])
+
+    def dsend_to(way, o):
+        if way == 0:
+            return remote(dsend.at[o], dright.at[o], dr_s.at[o], dr_r.at[o], (me + GROUP, j))
+        return remote(dsend.at[o], dleft.at[o], dl_s.at[o], dl_r.at[o], (me - GROUP, j))
+
+    up = z // (nz // 2)
+
+    def weight_chunk(c):
+        lo_at = pl.ds(pl.multiple_of(c * cc, cc), cc)
+        d = weight_grad(lo_at)
+        gwr[:, lo_at] = d[0:rows]
+        sendx[c] = d[rows : 3 * rows].astype(bf16)
+        held[0, :, lo_at] = d[3 * rows : 4 * rows]
+        xcopy(c).start()
+        hi_at = pl.ds(pl.multiple_of(half + c * cc, cc), cc)
+        d = weight_grad(hi_at)
+        gwr[:, hi_at] = d[0:rows]
+        sendy[c] = d[2 * rows : 4 * rows].astype(bf16)
+        held[1, :, lo_at] = d[rows : 2 * rows]
+        ycopy(c).start()
+
+    def expr_block(k, u):
+        kx, ky = k % 2, k // 2
+        kq = (x + kx - 2 * x * kx) + 2 * (y + ky - 2 * y * ky)
+        to = up * u + (1 - up) * (nz - 1 - u)
+        o = to * GROUP + kq
+        at = pl.ds(pl.multiple_of(o * cd, cd), cd)
+        v = jnp.dot(dpt[:, 0:grp], wbuf[0, :, at], preferred_element_type=f32) + jnp.dot(
+            dpt[:, grp : 2 * grp], wbuf[1, :, at], preferred_element_type=f32
+        )
+        grad[o] = v
+
+        @pl.when((z == 0) & (to > 0))
+        def _():
+            dsend[o] = v.astype(bf16)
+            dsend_to(0, o).start()
+
+        @pl.when((z == nz - 1) & (to < nz - 1))
+        def _():
+            dsend[o] = v.astype(bf16)
+            dsend_to(1, o).start()
+
+    @pl.loop(0, GROUP + nz - 1)
+    def _(w):
+        @pl.when(w < 4)
+        def _():
+            weight_chunk(w)
+
+        @pl.when(w == 0)
+        def _():
+            dpt[:, 0:grp] = jnp.transpose(dpb[:, 0:gq].astype(f32)).astype(bf16)
+            for i, p in enumerate((0, 1, 3, 2)):
+                wsib(p, i, every).wait_recv()
+            dps_copy.wait_recv()
+            dpt[:, grp : 2 * grp] = jnp.transpose(dps[...].astype(f32)).astype(bf16)
+
+        @pl.loop(0, nz)
+        def _(u):
+            @pl.when((w >= u) & (w - u < GROUP))
+            def _():
+                expr_block(GROUP - 1 - (w - u), u)
+
+    def chain(hops, u, k):
+        @pl.when((z == hops) & (z < nz - 1 - u))
+        def _():
+            o = nbr[k] + GROUP * (nz - 1 - u - z)
+            dsend_to(0, o).wait_recv()
+            dsend[o] = (grad[o] + dright[o].astype(f32)).astype(bf16)
+            dsend_to(0, o).start()
+
+        @pl.when((nz - 1 - z == hops) & (z > u))
+        def _():
+            o = nbr[k] - GROUP * (z - u)
+            dsend_to(1, o).wait_recv()
+            dsend[o] = (grad[o] + dleft[o].astype(f32)).astype(bf16)
+            dsend_to(1, o).start()
+
+    mine_cols = pl.ds(pl.multiple_of(q * gq, gq), gq)
+
+    def fin(k):
+        return remote(fins.at[k - 1], gexpr.at[:, mine_cols], fn_s.at[k], fn_r.at[k], (nbr[k], j))
+
+    def fin_wait(k):
+        remote(fins.at[k - 1], gexpr.at[:, pl.ds(pl.multiple_of(nq[k] * gq, gq), gq)],
+               fn_s.at[k], fn_r.at[k], here).wait_recv()
+
+    def finish(k):
+        o = nbr[k]
+
+        @pl.when(has_left)
+        def _():
+            dsend_to(0, o).wait_recv()
+            grad[o] += dright[o].astype(f32)
+
+        @pl.when(has_right)
+        def _():
+            dsend_to(1, o).wait_recv()
+            grad[o] += dleft[o].astype(f32)
+
+        v = jnp.transpose(grad[o]).astype(bf16)
+        if k:
+            fins[k - 1] = v
+            fin(k).start()
+        else:
+            gexpr[:, mine_cols] = v
+
+    def relay(c):
+        lo_at = pl.ds(c * cc, cc)
+        xcopy(c).wait_recv()
+        send2y[c] = (held[0, :, lo_at] + recvx[c, rows : 2 * rows].astype(f32)).astype(bf16)
+        y2copy(c).start()
+        ycopy(c).wait_recv()
+        send2x[c] = (held[1, :, lo_at] + recvy[c, 0:rows].astype(f32)).astype(bf16)
+        x2copy(c).start()
+        gwr[:, lo_at] += recvx[c, 0:rows].astype(f32)
+        gwr[:, pl.ds(half + c * cc, cc)] += recvy[c, rows : 2 * rows].astype(f32)
+
+    def fcopy(o):
+        return remote(fsend.at[o], frecv.at[me], fi_s.at[o], fi_r.at[me], (o, j))
+
+    def whole(c, gm):
+        for base, got, pieces in ((0, y2copy, recv2y), (half, x2copy, recv2x)):
+            got(c).wait_recv()
+            start = base + c * cc
+            at = slice(start, start + cc)
+            p = probs[:, at]
+            gw = gwr[:, at] + pieces[c].astype(f32) + jnp.concatenate([gm] * (cc // 128), axis=1)
+            part = jnp.sum(gw * p.astype(bf16).astype(f32), axis=0, keepdims=True)
+            for i in range(cc // cd):
+                o = start // cd + i
+                fsend[o, 0:1] = part[:, i * cd : (i + 1) * cd]
+                fsend[o, 1:2] = loss_part
+
+                @pl.when(me != o)
+                def _():
+                    fcopy(o).start()
+
+            gp = (gateb[0:1, at] * gw).astype(bf16)
+            gpb[:, at] = gp
+            v = fold(p * gp.astype(f32))
+            if c == 0 and base == 0:
+                rowsum[...] = v
+            else:
+                rowsum[...] += v
+
+    def mass_parts():
+        gather_wait(massb, ma_s, ma_r)
+        count_total = jnp.zeros((1, 128), f32)
+        gate_sum = jnp.zeros((1, 128), f32)
+        for o in range(nspot):
+            count_total = count_total + small[o, 2:3, :] + small[o, 3:4, :]
+        for o in range(cells // 128):
+            gate_sum = gate_sum + gateb[0:1, o * 128 : (o + 1) * 128]
+        count_total = jnp.sum(count_total)
+        gate_total = jnp.sum(gate_sum)
+        mass_sum = jnp.zeros((1, 128), f32)
+        kl_sum = jnp.zeros((1, 128), f32)
+        share_sum = jnp.zeros((1, 128), f32)
+        for o in range(nspot):
+            m = massb[o, 0:1, :]
+            share = jnp.where(j == 0, small[o, 2:3, :], small[o, 3:4, :]) / count_total
+            mass_sum = mass_sum + m
+            share_sum = share_sum + share
+            kl_sum = kl_sum + share * (jnp.log(share) - jnp.log(m))
+        pair_s[1, 0:1, 0:128] = mass_sum
+        pair_s[1, 1:2, 0:128] = kl_sum
+        pair_s[1, 2:3, 0:128] = share_sum
+        pair(1).start()
+        return count_total, gate_total, mass_sum, kl_sum, share_sum
+
+    def mass_totals(count_total, gate_total, mass_sum, kl_sum, share_sum):
+        pair(1).wait_recv()
+        mass_total = jnp.sum(mass_sum + pair_r[1, 0:1, 0:128])
+        kl_all = jnp.sum(kl_sum + pair_r[1, 1:2, 0:128])
+        share_all = jnp.sum(share_sum + pair_r[1, 2:3, 0:128])
+        log_total = jnp.sum(jnp.log(jnp.full((1, 128), mass_total))[:, 0:1])
+        excess = gate_total / count_total - 1.0
+        my_dens = small[pl.ds(me, 1), pl.ds(2 + j, 1), :].reshape(1, 128)
+        my_mass = massb[pl.ds(me, 1), 0:1, :].reshape(1, 128)
+        gm_row = (1.0 / mass_total - my_dens / count_total / my_mass).astype(bf16).astype(f32)
+        return kl_all + share_all * log_total + excess * excess, excess, column(gm_row, rows)
+
+    def forward_sent():
+        for c in ea:
+            c.wait_send()
+        for k, h in tlist:
+            tcopy(k, h).wait_send()
+        for k in (1, 2, 3):
+            smalls(k).wait_send()
+        for way in (0, 1):
+            for u in range(8):
+                wown(way, u).wait_send()
+            for m in range(4):
+                wpass(way, m).wait_send()
+        for i, p in enumerate((0, 1, 3, 2)):
+            wsib(p, i, every).wait_send()
+        for i in range(4):
+            stat(i).wait_send()
+        dps_copy.wait_send()
+
+    def along_sent():
+        @pl.loop(0, nspot)
+        def _(o):
+            esib(o).wait_send()
+            at = o // GROUP
+
+            @pl.when(has_right & (at <= z))
+            def _():
+                zsend(0, o).wait_send()
+
+            @pl.when(has_left & (at >= z))
+            def _():
+                zsend(1, o).wait_send()
+
+        @pl.loop(0, nz)
+        def _(at):
+            @pl.when(has_right & (at <= z))
+            def _():
+                zsmall(0, at).wait_send()
+
+            @pl.when(has_left & (at >= z))
+            def _():
+                zsmall(1, at).wait_send()
+
+    relay(0)
+    chain(1, 0, 3)
+    chain(1, 1, 3)
+    totals = mass_parts()
+    chain(1, 0, 2)
+    rest, excess, gm = mass_totals(*totals)
+    relay(1)
+    chain(2, 0, 3)
+    forward_sent()
+    chain(2, 0, 2)
+    chain(1, 1, 2)
+    relay(2)
+    chain(1, 0, 1)
+    along_sent()
+    gather_sent(massb, ma_s, ma_r)
+    relay(3)
+    finish(3)
+    finish(2)
+    chain(2, 0, 1)
+    chain(1, 1, 1)
+    loss_part = jnp.broadcast_to(-gene_part / SLIDES - jnp.sum(cos_spot) / spots_all, (1, cd))
+    whole(0, gm)
+    chain(1, 0, 0)
+    whole(1, gm)
+    finish(1)
+    chain(2, 0, 0)
+    chain(1, 1, 0)
+    whole(2, gm)
+    whole(3, gm)
+
+    frecv[pl.ds(me, 1)] = fsend[pl.ds(me, 1)]
+
+    def others(act):
+        @pl.loop(0, nspot)
+        def _(o):
+            @pl.when(o != me)
+            def _():
+                act(o)
+
+    tot_o[...] = jnp.broadcast_to(jnp.sum(rowsum[...], axis=1, keepdims=True), (rows, 128))
+    finish(0)
+    others(lambda o: remote(fsend.at[o], frecv.at[o], fi_s.at[o], fi_r.at[o], here).wait_recv())
+    ftotal = frecv[0]
+    for o in range(1, nspot):
+        ftotal = ftotal + frecv[o]
+    pair_s[2, 0:2, 0:cd] = ftotal
+    pair(2).start()
+    count_total = totals[0]
+    my_gate = jax.nn.sigmoid(filt[...])
+
+    others(lambda o: fcopy(o).wait_send())
+    for k in range(1, GROUP):
+        fin(k).wait_send()
+
+    @pl.loop(0, 4)
+    def _(c):
+        xcopy(c).wait_send()
+        ycopy(c).wait_send()
+        x2copy(c).wait_send()
+        y2copy(c).wait_send()
+
+    @pl.loop(0, nspot)
+    def _(o):
+        at = o // GROUP
+
+        @pl.when(has_right & (at > z))
+        def _():
+            dsend_to(0, o).wait_send()
+
+        @pl.when(has_left & (at < z))
+        def _():
+            dsend_to(1, o).wait_send()
+
+    for i in range(3):
+        pair(i).wait_send()
+    pair(2).wait_recv()
+    fsum = ftotal + pair_r[2, 0:2, 0:cd]
+    loss_o[0, 0] = jnp.sum(fsum[1:2, 0:1]) + rest
+    fsum = fsum[0:1] + 2.0 * excess / count_total
+    for h in range(cd // 128):
+        g = my_gate[h : h + 1, :]
+        gf_o[h : h + 1, :] = fsum[:, h * 128 : (h + 1) * 128] * g * (1.0 - g)
+    for k in (3, 2, 1):
+        fin_wait(k)
+    ge_o[...] = gexpr[...]
+
+
+def finish_kernel(probs, gp, tot, ge, loss, gf, gl_o, ge_o, loss_o, gf_o, gl, gx, out_s):
+    f32 = jnp.float32
+    parts = 4
+    cc = probs.shape[1] // parts
+    copies = []
+    for i in range(parts):
+        for c in range(i * cc, (i + 1) * cc, 128):
+            at = slice(c, c + 128)
+            gl[:, at] = probs[:, at] * (gp[:, at].astype(f32) - tot[...])
+        at = pl.ds(i * cc, cc)
+        copies.append(pltpu.make_async_copy(gl.at[:, at], gl_o.at[:, at], out_s.at[i]))
+        copies[-1].start()
+    gx[...] = ge[...].astype(f32)
+    copies.append(pltpu.make_async_copy(gx, ge_o, out_s.at[parts]))
+    copies[-1].start()
+    gf_o[...] = gf[...]
+    loss_o[0, 0] = loss[0, 0]
+    for c in copies:
+        c.wait()
+
+
+def grouped(logits, filt, expr, target, gene_mask, density):
+    f32, bf16, i32 = jnp.float32, jnp.bfloat16, jnp.int32
+    nspot = lax.axis_size("spot")
+    rows, cells = logits.shape
+    cd, half = expr.shape
+    gq = half // GROUP
+    grp = GROUP * rows
+    hc = cells // 2
+    cc = hc // 4
+    nz = nspot // GROUP
+    wide = max(2 * gq, grp, cd, 128)
+
+    def vmem(*shape, dtype=f32):
+        return pltpu.VMEM(shape, dtype)
+
+    def dma(*shape):
+        return pltpu.SemaphoreType.DMA(shape)
+
+    buffers = [
+        vmem(rows, cells, dtype=bf16), vmem(cd // 128, 128), vmem(*gene_mask.shape, dtype=i32),
+        vmem(2 * rows // 128, 128, dtype=i32),
+        vmem(8, cells), vmem(grp, cells, dtype=bf16), vmem(2, grp, cells, dtype=bf16),
+        vmem(2, cells, gq, dtype=bf16),
+        vmem(2, grp, gq, dtype=bf16), vmem(grp, 2 * gq), vmem(grp, 2 * gq, dtype=bf16),
+        vmem(grp, gq, dtype=bf16), vmem(gq, 2 * grp, dtype=bf16),
+        vmem(nspot, 8, 128), vmem(nspot, 8, 128),
+        vmem(4, 8, wide), vmem(4, 8, wide), vmem(2, 8, wide), vmem(4, 8, wide),
+        vmem(4, 2 * rows, cc, dtype=bf16), vmem(4, 2 * rows, cc, dtype=bf16),
+        vmem(4, 2 * rows, cc, dtype=bf16), vmem(4, 2 * rows, cc, dtype=bf16),
+        vmem(4, rows, cc, dtype=bf16), vmem(4, rows, cc, dtype=bf16),
+        vmem(4, rows, cc, dtype=bf16), vmem(4, rows, cc, dtype=bf16),
+        vmem(rows, cells), vmem(2, rows, hc), vmem(rows, 128),
+        vmem(nspot, gq, cd), vmem(nspot, gq, cd, dtype=bf16),
+        vmem(nspot, gq, cd, dtype=bf16), vmem(nspot, gq, cd, dtype=bf16),
+        vmem(3, cd, gq, dtype=bf16), vmem(cd, half, dtype=bf16),
+        vmem(nspot, 2, cd), vmem(nspot, 2, cd),
+    ]
+    sems = [
+        dma(6), dma(4), dma(4), dma(2, nspot), dma(nspot), dma(nspot), dma(nspot),
+        dma(12), dma(12), dma(12), dma(12), dma(4), dma(4), dma(8), dma(8),
+        dma(4), dma(4), dma(2, nz), dma(nz), dma(nspot), dma(nspot),
+        dma(nspot), dma(nspot),
+        dma(4), dma(4), dma(4), dma(4),
+        dma(4), dma(4), dma(4), dma(4), dma(4), dma(4), dma(4), dma(4),
+        dma(nspot), dma(nspot), dma(nspot), dma(nspot), dma(4), dma(4), dma(1), dma(1),
+    ]
+    v, a = pl.BlockSpec(memory_space=pltpu.VMEM), pl.BlockSpec(memory_space=pl.ANY)
+    s, hbm = pl.BlockSpec(memory_space=pltpu.SMEM), pl.BlockSpec(memory_space=pltpu.HBM)
+    shape = jax.ShapeDtypeStruct
+    fparts = (cd // 128, 128)
+    given = (logits, filt.reshape(-1, 128), expr, target, gene_mask, density.reshape(-1, 128))
+    loss, probs, gp, tot, grad_filt, grad_expr = pl.pallas_call(
+        functools.partial(group_kernel, nspot),
+        out_shape=[
+            shape((1, 1), f32),
+            vmem(rows, cells),
+            vmem(rows, cells, dtype=bf16),
+            vmem(rows, 128),
+            vmem(*fparts),
+            vmem(cd, half, dtype=bf16),
+        ],
+        in_specs=[hbm] * 6,
+        out_specs=[s, v, v, v, v, v],
+        scratch_shapes=buffers + sems,
+        compiler_params=pltpu.CompilerParams(
+            collective_id=0, has_side_effects=True, vmem_limit_bytes=VMEM_BYTES
+        ),
+        name="group_step",
+    )(*(pltpu.with_memory_space_constraint(v, pltpu.HBM) for v in given))
+    grad_logits, grad_expr, loss, grad_filt = pl.pallas_call(
+        finish_kernel,
+        out_shape=[shape((rows, cells), f32), shape((cd, half), f32), shape((1, 1), f32), shape(fparts, f32)],
+        in_specs=[v, v, v, v, s, v],
+        out_specs=[a, a, s, v],
+        scratch_shapes=[vmem(rows, cells), vmem(cd, half), dma(5)],
+        compiler_params=pltpu.CompilerParams(vmem_limit_bytes=LAST_BYTES),
+        name="finish_step",
+    )(probs, gp, tot, grad_expr, loss, grad_filt)
+    return (loss.reshape(()), grad_logits, grad_filt.reshape(-1), grad_expr)
+
+
+def fits(logits, filt, expr):
+    nspot = lax.axis_size("spot")
+    rows, cells = logits.shape
+    held = cells * (expr.shape[1] // GROUP) * 2 * 2 + 2 * GROUP * rows * cells * 2
+    return (
+        nspot == GROUP * SLIDES
+        and lax.axis_size("gene") == 2
+        and rows == 128
+        and filt.shape[0] == 256
+        and held <= 16 << 20
+    )
+
+
+def per_device(logits, filt, expr, target, gene_mask, density):
+    plan = grouped if fits(logits, filt, expr) else streamed
+    return plan(logits, filt, expr, target, gene_mask, density)
+
+
 def solution(mesh):
     in_specs = (
         P(("spot", "gene"), None),

time: 750 us -> 108 us (0.14)
  blocking collectives: 382 us -> 0 us
  waiting for transfers between devices: 295 us -> 0 us
  Pallas kernels: 0 us -> 107 us
  matrix products: 28 us -> 0 us
  other arithmetic: 20.3 us -> 0 us
  between operations: 20.3 us -> 0.64 us
    reduce_scatter x2 -> x0, waiting for transfers between devices: 214 us -> none  [the longest x1 214 us: per_device(): lax.psum_scatter(partial_pred.reshape(nspot, owned, half), 'spot', scatte...]
    all_to_all x2 -> x0, blocking collectives: 132 us -> none  [the longest x1 97.5 us: per_device(): lax.all_to_all(terms, 'spot', split_axis=0, concat_axis=3, tiled=True)]
    psum x5 -> x0, blocking collectives: 125 us -> none  [the longest x2 118 us: per_device(): lax.psum((slide_moments(onehot, pred, truth), jnp.sum(mass), gate_part, j...]
    pallas_call x0 -> x2, Pallas kernels: none -> 107 us  [the longest x1 104 us: grouped(): pl.pallas_call(functools.partial(group_kernel, nspot), out_shape=[shape((...]
    unnamed x1 -> x0, blocking collectives: 88.4 us -> none
    all_gather x2 -> x0, waiting for transfers between devices: 81.7 us -> none  [the longest x1 73.4 us: per_device(): lax.all_gather(grad_pred.astype(bf16).reshape(1, owned, half), 'spot', ax...]
    all_gather x1 -> x0, blocking collectives: 35.7 us -> none  [per_device(): lax.all_gather(grad_mass.astype(bf16).reshape(1, owned), 'spot', axis=0,...]
    dot_general x8 -> x0, matrix products: 28 us -> none  [the longest x1 9.65 us: per_device(): partial_pred = jnp.dot(weighted, expr, preferred_element_type=f32)]
  transfers between devices with their start and end apart: 4 -> 0, of which waited for: 3 -> 0; matrix products, arithmetic and copies ran while one was open for 2% -> 0% of each run, Pallas kernels for 0% -> 0%
where the time goes in v2:
time: 108 us; the launch traced here: 107 us
  Pallas kernels  107 us (99%)
    pallas_call x1, Pallas kernels, grouped(): pl.pallas_call(functools.partial(group_kernel, nspot), out_shape=[shape((...  104 us
    pallas_call x1, Pallas kernels, grouped(): pl.pallas_call(finish_kernel, out_shape=[shape((rows, cells), f32), shape...  2.98 us

profile of v2, /device:TPU:0, one launch (start us, length us, event | category | flops | bytes accessed | tf_op | source)
XLA Modules:
  0.0 107.4 jit_solution(4100978112376362153)
XLA Ops:
  0.6 103.8 %group_step.1 = (f32[1,1]{1,0:T(1,128)}, f32[128,4096]{1,0:T(8,128)S(1)}, bf16[128,4096]{1,0:T(8,128)(2,1)S(1)}, f32[128,128]{1,0:T(8,128)S(1)}, f32[2,128]{1,0:T(2,128)S(1)}, /*index=5*/bf16[256,1024]{1,0:T(8,128)(2,1)S(1)}) custom-call(bf16[128,4096]{1,0:T(8,128)(2,1)} %logits_h.1, f32[2,128]{1,0:T(2,128)} %bitcast.4, bf16[256,1024]{1,0:T(8,128)(2,1)} %expr.1, ...), custom_call_target="tpu_custom_call" | custom-call | tf_op jit(solution)/shard_map/group_step/pallas_call | solution.py:994
  104.5 3.0 %finish_step.1 = (f32[128,4096]{1,0:T(8,128)}, f32[256,1024]{1,0:T(8,128)}, f32[1,1]{1,0:T(1,128)}, f32[2,128]{1,0:T(2,128)}) custom-call(f32[128,4096]{1,0:T(8,128)S(1)} %get-tuple-element.14.probs, bf16[128,4096]{1,0:T(8,128)(2,1)S(1)} %get-tuple-element.15.gp, f32[128,128]{1,0:T(8,128)S(1)} %get-tuple-element.16.tot, ...), custom_call_target="tpu_custom_call" | custom-call | tf_op jit(solution)/shard_map/finish_step/pallas_call | solution.py:1012

commit v3 on v2

--- a/solution.py
+++ b/solution.py
@@ -153,7 +153,6 @@
 MESH = pl.DeviceIdType.MESH
 VMEM_BYTES = 48 << 20
 LAST_BYTES = 16 << 20
-POS = {0: 0, 1: 1, 3: 2, 2: 3}
 
 
 def remote(src, dst, send, recv, dev):
@@ -183,7 +182,7 @@
 
 def group_kernel(
     nspot, logits_h, filt_h, expr, target, mask_h, dens_h,
-    loss_o, probs, gpb, tot_o, gf_o, ge_o,
+    probs, gpb, tot_o, last_o, ge_o,
     logits, filt, mask, dens, gateb, raw, wbuf, ebuf, tbuf, pbuf, dpb, dps, dpt,
     small, massb, pair_s, pair_r, stat_s, stat_r,
     sendx, recvx, sendy, recvy, send2x, recv2x, send2y, recv2y, gwr, held, rowsum,
@@ -215,8 +214,8 @@
     def greet(dev):
         pl.semaphore_signal(barrier, inc=1, device_id=dev, device_id_type=MESH)
 
-    for k in (1, 2, 3):
-        greet((nbr[k], j))
+    greet((nbr[1], j))
+    greet((nbr[2], j))
 
     @pl.when(has_right)
     def _():
@@ -226,8 +225,7 @@
     def _():
         greet((me - GROUP, j))
 
-    for k in (3, 1, 2, 0):
-        greet((nbr[k], sib))
+    greet(here)
 
     def eblock(h, o):
         return ebuf.at[h, pl.ds(pl.multiple_of(o * cd, cd), cd), :]
@@ -276,19 +274,17 @@
     pair_s[0, :, gq : 2 * gq] = jnp.broadcast_to(kept_mine, (8, gq))
     for c in loads[4:]:
         c.wait()
-    pl.semaphore_wait(barrier, 7 + has_right.astype(jnp.int32) + has_left.astype(jnp.int32))
+    pl.semaphore_wait(barrier, 3 + has_right.astype(jnp.int32) + has_left.astype(jnp.int32))
 
     def smalls(k):
         return remote(small.at[me], small.at[me], sm_s.at[k], sm_r.at[k], (nbr[k], j))
 
-    for k in (3, 1, 2):
+    ea = {
+        k: remote(ecols(expr, k), eblock(0, me), ea_s.at[k], ea_r.at[k], (nbr[k], j)) for k in (1, 2, 3)
+    }
+    for k in (1, 2):
         smalls(k).start()
-    ea = [
-        remote(ecols(expr, k), eblock(0, me), ea_s.at[k], ea_r.at[k], (nbr[k], j))
-        for k in range(1, GROUP)
-    ]
-    for c in ea:
-        c.start()
+        ea[k].start()
 
     def zsend(way, o):
         return remote(
@@ -334,12 +330,8 @@
         ]
         i = k * 2 + h
         return remote(
-            src, tbuf.at[h, pl.ds(POS[k] * rows, rows), :], t_s.at[i], t_r.at[i], (nbr[k], jj)
+            src, tbuf.at[h, pl.ds((k) * rows, rows), :], t_s.at[i], t_r.at[i], (nbr[k], jj)
         )
-
-    tlist = [(k, h) for k in (3, 1, 2, 0) for h in (0, 1) if (k, h) != (0, 0)]
-    for k, h in tlist:
-        tcopy(k, h).start()
 
     def wcols(way, u):
         u = u if way == 0 else (u + 4) % 8
@@ -352,35 +344,30 @@
         to, ss, rs = ((1, wx_s, wx_r), (2, wy_s, wy_r))[way]
         at = wcols(way, u)
         return remote(
-            raw.at[wrows(0), at], raw.at[wrows(POS[to]), at], ss.at[u], rs.at[u], (nbr[to], j)
+            raw.at[wrows(0), at], raw.at[wrows(to), at], ss.at[u], rs.at[u], (nbr[to], j)
         )
 
     def wpass(way, m):
         to, ss, rs = ((1, wx_s, wx_r), (2, wy_s, wy_r))[way]
         at = wcols(1 - way, m)
         return remote(
-            raw.at[wrows(POS[3 - to]), at], raw.at[wrows(2), at], ss.at[8 + m], rs.at[8 + m], (nbr[to], j)
+            raw.at[wrows(3 - to), at], raw.at[wrows(3), at], ss.at[8 + m], rs.at[8 + m], (nbr[to], j)
         )
 
     def wsib(p, i, at):
         return remote(wbuf.at[0, wrows(p), at], wbuf.at[1, wrows(p), at], wd_s.at[i], wd_r.at[i], here)
 
     every = pl.ds(0, cells)
+    def small_wait(k):
+        remote(small.at[nbr[k]], small.at[nbr[k]], sm_s.at[k], sm_r.at[k], here).wait_recv()
+
+    small_wait(1)
+    smalls(3).start()
+    ea[3].start()
     for u in range(8):
         wown(0, u).start()
         wown(1, u).start()
 
-    for k in (1, 2, 3):
-        remote(small.at[nbr[k]], small.at[nbr[k]], sm_s.at[k], sm_r.at[k], here).wait_recv()
-
-    @pl.when(has_right)
-    def _():
-        zsmall(0, z).start()
-
-    @pl.when(has_left)
-    def _():
-        zsmall(1, z).start()
-
     def small_hop(s):
         @pl.when(z >= s)
         def _():
@@ -397,12 +384,6 @@
             @pl.when(has_left)
             def _():
                 zsmall(1, z + s).start()
-
-    for k in (1, 2, 3):
-        remote(eblock(0, nbr[k]), eblock(0, nbr[k]), ea_s.at[k], ea_r.at[k], here).wait_recv()
-        spread(nbr[k])
-        if k < nz:
-            small_hop(k)
 
     def gated(p, at):
         wbuf[0, wrows(p), at] = (gateb[0:1, at] * raw[wrows(p), at].astype(f32)).astype(bf16)
@@ -420,52 +401,97 @@
         wsib(0, 0, every).start()
         massb[pl.ds(me, 1), :, :] = dot_nt(jnp.ones((8, cells), bf16), wbuf[0, 0:rows, :])[None]
 
-    n = 0
-    for s in range(1, nz):
+    tlist = [(0, 1)] + [(k, h) for k in (3, 1, 2) for h in (0, 1)]
+
+    def target_start():
         for k in range(GROUP):
-
-            @pl.when(z >= s)
+            esib(nbr[k]).wait_recv()
+        for k, h in tlist:
+            tcopy(k, h).start()
+
+    def plane_start():
+        small_wait(2)
+        small_wait(3)
+
+        @pl.when(has_right)
+        def _():
+            zsmall(0, z).start()
+
+        @pl.when(has_left)
+        def _():
+            zsmall(1, z).start()
+
+    def along(s, k):
+        if s == 0:
+            remote(eblock(0, nbr[k]), eblock(0, nbr[k]), ea_s.at[k], ea_r.at[k], here).wait_recv()
+            spread(nbr[k])
+            return
+
+        @pl.when(z >= s)
+        def _():
+            o = nbr[k] - GROUP * s
+            ezwait(o)
+
+            @pl.when(has_right)
             def _():
-                o = nbr[k] - GROUP * s
-                ezwait(o)
-
-                @pl.when(has_right)
-                def _():
-                    zsend(0, o).start()
-
-                esib(o).start()
-
-            @pl.when(z + s <= nz - 1)
+                zsend(0, o).start()
+
+            esib(o).start()
+
+        @pl.when(z + s <= nz - 1)
+        def _():
+            o = nbr[k] + GROUP * s
+            ezwait(o)
+
+            @pl.when(has_left)
             def _():
-                o = nbr[k] + GROUP * s
-                ezwait(o)
-
-                @pl.when(has_left)
-                def _():
-                    zsend(1, o).start()
-
-                esib(o).start()
-
-            if n == 0:
-                gates()
-            if n >= 4:
-                u = n - 4
+                zsend(1, o).start()
+
+            esib(o).start()
+
+    def pass_on(m):
+        wown(0, m).wait_recv()
+        wown(1, m).wait_recv()
+        wpass(0, m).start()
+        wpass(1, m).start()
+
+    def gate_pieces(first, last):
+        for u in range(first, last):
+            if u >= 4:
                 wown(0, u).wait_recv()
                 wown(1, u).wait_recv()
-                if u < 4:
-                    wpass(0, u).start()
-                    wpass(1, u).start()
-                gated(1, wcols(0, u))
-                gated(3, wcols(1, u))
-            n += 1
+            gated(1, wcols(0, u))
+            gated(2, wcols(1, u))
+
+    along(0, 1)
+    along(0, 2)
+    along(1, 0)
+    plane_start()
+    along(1, 1)
+    pass_on(0)
+    along(0, 3)
+    along(1, 2)
+    pass_on(1)
+    along(2, 0)
+    small_hop(1)
+    pass_on(2)
+    along(1, 3)
+    pass_on(3)
+    target_start()
+    along(2, 1)
+    small_hop(2)
+    along(2, 2)
+    along(3, 0)
+    along(2, 3)
+    small_hop(3)
+    gates()
+    gate_pieces(0, 8)
     wsib(1, 1, every).start()
-    wsib(3, 2, every).start()
-
-    @pl.loop(0, nspot)
-    def _(o):
-        esib(o).wait_recv()
-
-    kb = cc
+    wsib(2, 2, every).start()
+
+    early, late = slice(0, 3 * rows), slice(3 * rows, 4 * rows)
+    pc = GROUP * cd
+    kb = min(pc, cc)
 
     def project(at, span, first):
         for h in range(2):
@@ -476,41 +502,56 @@
             else:
                 pbuf[to] += v
 
-    early = (slice(0, 2 * rows), slice(3 * rows, 4 * rows))
-    late = slice(2 * rows, 3 * rows)
-    for span in early:
-        project(pl.ds(0, kb), span, True)
-
-    @pl.loop(1, cells // kb)
-    def _(i):
-        for span in early:
-            project(pl.ds(pl.multiple_of(i * kb, kb), kb), span, False)
-
-    for k, h in tlist:
-        tcopy(k, h).wait_recv()
-
-    def moments(p, which):
+    def project_plane(at, first):
+        for k in range(GROUP):
+            if not first:
+                esib(at * GROUP + k).wait_recv()
+        for i in range(pc // kb):
+            project(pl.ds(pl.multiple_of(at * pc + i * kb, kb), kb), early, first and i == 0)
+
+    def project_from(s):
+        @pl.when(z >= s)
+        def _():
+            project_plane(z - s, False)
+
+        @pl.when(z + s <= nz - 1)
+        def _():
+            project_plane(z + s, False)
+
+    project_plane(z, True)
+    project_from(1)
+    project_from(2)
+    along(3, 1)
+    along(3, 2)
+    along(3, 3)
+    project_from(3)
+
+    def moment(i, p, values, first):
+        by_gene = jnp.sum(values, axis=0, keepdims=True)
+        if first:
+            stat_s[0, i] = by_gene
+        else:
+            stat_s[0, i] += by_gene
+        stat_s[1, i, :, p * rows : (p + 1) * rows] = lanes_to_row(values)
+
+    def squares(p):
+        v = pbuf[p * rows : (p + 1) * rows, :]
+        moment(0, p, v * v, p == 0)
+
+    def with_target(p, first):
         span = slice(p * rows, (p + 1) * rows)
-        for h in range(2):
-            at = slice(h * gq, (h + 1) * gq)
-            t = tbuf[h, span, :].astype(f32)
-            v = pbuf[span, at]
-            for i in which:
-                w = (v * t, v * v, t * t)[i]
-                by_gene = jnp.sum(w, axis=0, keepdims=True)
-                if p == 0:
-                    stat_s[0, i : i + 1, at] = by_gene
-                else:
-                    stat_s[0, i : i + 1, at] += by_gene
-                by_spot = lanes_to_row(w)
-                if h == 0:
-                    stat_s[1, i : i + 1, span] = by_spot
-                else:
-                    stat_s[1, i : i + 1, span] += by_spot
-
-    for p in (0, 1, 3):
-        moments(p, (0, 1, 2))
-    moments(2, (2,))
+        t = jnp.concatenate([tbuf[h, span, :].astype(f32) for h in range(2)], axis=1)
+        moment(1, p, pbuf[span, :] * t, first)
+        moment(2, p, t * t, first)
+
+    def stat(k, late):
+        at = pl.ds(1, 2) if late else pl.ds(0, 1)
+        i = 2 * k + late
+        src, dev = (stat_s.at[0, at], here) if k == 0 else (stat_s.at[1, at], (nbr[k], j))
+        return remote(src, stat_r.at[k, at], st_s.at[i], st_r.at[i], dev)
+
+    for p in (0, 1, 2):
+        squares(p)
     pair(0).wait_recv()
     kept = jnp.maximum(kept_mine + jnp.sum(pair_r[0, 0:1, gq : gq + 1]), 1.0)
     weight = jnp.concatenate([mine_mask, pair_r[0, 0:1, 0:gq]], axis=1) / kept / SLIDES
@@ -541,50 +582,50 @@
         wpass(1, m).wait_recv()
         for way in (0, 1):
             at = wcols(1 - way, m)
-            gated(2, at)
+            gated(3, at)
             project(at, late, m == 0 and way == 0)
-    wsib(2, 3, every).start()
-    moments(2, (0, 1))
-
-    def stat(k):
-        if k == 0:
-            return remote(stat_s.at[0], stat_r.at[0], st_s.at[0], st_r.at[0], here)
-        return remote(stat_s.at[1], stat_r.at[k], st_s.at[k], st_r.at[k], (nbr[k], j))
-
+    wsib(3, 3, every).start()
+    squares(3)
     for k in (3, 1, 2, 0):
-        stat(k).start()
-    stat(0).wait_recv()
+        stat(k, 0).start()
+    tcopy(0, 1).wait_recv()
+    with_target(0, True)
+    for k in (3, 1, 2):
+        tcopy(k, 0).wait_recv()
+        tcopy(k, 1).wait_recv()
+        with_target(k, False)
+    for k in (3, 1, 2, 0):
+        stat(k, 1).start()
+
+    for n in (0, 1):
+        stat(0, n).wait_recv()
     order = (slice(gq, 2 * gq), slice(0, gq))
-    slide = [
-        jnp.concatenate([stat_r[0, i : i + 1, c] for c in order], axis=1) + stat_s[0, i : i + 1, :]
-        for i in range(3)
-    ]
-    dots = slide[0]
-    slide_a = lax.rsqrt(slide[1] + eps_norm)
-    slide_b = lax.rsqrt(slide[2] + eps_norm)
+    pred_sq, dots, truth_sq = (
+        jnp.concatenate([stat_r[0, i, :, c] for c in order], axis=1) + stat_s[0, i] for i in range(3)
+    )
+    slide_a = lax.rsqrt(pred_sq + eps_norm)
+    slide_b = lax.rsqrt(truth_sq + eps_norm)
     coef_t = -weight * slide_a * slide_b
     coef_p = weight * dots * slide_a**3 * slide_b
     cos_gene = (dots * slide_a * slide_b)[:, 0:gq]
-    gene_part = jnp.sum(mine_mask * cos_gene / kept)
+
     for k in (1, 2, 3):
-        stat(k).wait_recv()
-    at_pos = {0: 0, 1: 1, 2: 3, 3: 2}
+        for n in (0, 1):
+            stat(k, n).wait_recv()
     spot = []
     for i in range(3):
         parts = []
-        for p in range(GROUP):
-            k = at_pos[p]
-            v = stat_s[1, i : i + 1, p * rows : (p + 1) * rows]
-            there = [
-                stat_r[m, i : i + 1, POS[k ^ m] * rows : (POS[k ^ m] + 1) * rows] for m in (1, 2, 3)
-            ]
+        for k in range(GROUP):
+            v = stat_s[1, i, :, k * rows : (k + 1) * rows]
+            there = [stat_r[m, i, :, (k ^ m) * rows : ((k ^ m) + 1) * rows] for m in (1, 2, 3)]
             parts.append((v + there[0]) + (there[1] + there[2]))
         spot.append(jnp.concatenate(parts, axis=1))
-    spot_a = lax.rsqrt(spot[1] + eps_norm)
-    spot_b = lax.rsqrt(spot[2] + eps_norm)
-    cos_spot = (spot[0] * spot_a * spot_b)[:, 0:rows]
+    spot_pp, spot_dot, spot_tt = spot
+    spot_a = lax.rsqrt(spot_pp + eps_norm)
+    spot_b = lax.rsqrt(spot_tt + eps_norm)
+    cos_spot = (spot_dot * spot_a * spot_b)[:, 0:rows]
     col_t = column(-(spot_a * spot_b) / spots_all, grp)
-    col_p = column(spot[0] * spot_a**3 * spot_b / spots_all, grp)
+    col_p = column(spot_dot * spot_a**3 * spot_b / spots_all, grp)
 
     for g in range(2 * gq // 128):
         at = slice(g * 128, (g + 1) * 128)
@@ -619,13 +660,15 @@
         lo_at = pl.ds(pl.multiple_of(c * cc, cc), cc)
         d = weight_grad(lo_at)
         gwr[:, lo_at] = d[0:rows]
-        sendx[c] = d[rows : 3 * rows].astype(bf16)
-        held[0, :, lo_at] = d[3 * rows : 4 * rows]
+        sendx[c, 0:rows] = d[rows : 2 * rows].astype(bf16)
+        sendx[c, rows : 2 * rows] = d[3 * rows : 4 * rows].astype(bf16)
+        held[0, :, lo_at] = d[2 * rows : 3 * rows]
         xcopy(c).start()
         hi_at = pl.ds(pl.multiple_of(half + c * cc, cc), cc)
         d = weight_grad(hi_at)
         gwr[:, hi_at] = d[0:rows]
-        sendy[c] = d[2 * rows : 4 * rows].astype(bf16)
+        sendy[c, 0:rows] = d[3 * rows : 4 * rows].astype(bf16)
+        sendy[c, rows : 2 * rows] = d[2 * rows : 3 * rows].astype(bf16)
         held[1, :, lo_at] = d[rows : 2 * rows]
         ycopy(c).start()
 
@@ -659,8 +702,8 @@
         @pl.when(w == 0)
         def _():
             dpt[:, 0:grp] = jnp.transpose(dpb[:, 0:gq].astype(f32)).astype(bf16)
-            for i, p in enumerate((0, 1, 3, 2)):
-                wsib(p, i, every).wait_recv()
+            for k in range(GROUP):
+                wsib(k, k, every).wait_recv()
             dps_copy.wait_recv()
             dpt[:, grp : 2 * grp] = jnp.transpose(dps[...].astype(f32)).astype(bf16)
 
@@ -791,7 +834,7 @@
         return kl_all + share_all * log_total + excess * excess, excess, column(gm_row, rows)
 
     def forward_sent():
-        for c in ea:
+        for c in ea.values():
             c.wait_send()
         for k, h in tlist:
             tcopy(k, h).wait_send()
@@ -802,10 +845,11 @@
                 wown(way, u).wait_send()
             for m in range(4):
                 wpass(way, m).wait_send()
-        for i, p in enumerate((0, 1, 3, 2)):
-            wsib(p, i, every).wait_send()
+        for k in range(GROUP):
+            wsib(k, k, every).wait_send()
         for i in range(4):
-            stat(i).wait_send()
+            stat(i, 0).wait_send()
+            stat(i, 1).wait_send()
         dps_copy.wait_send()
 
     def along_sent():
@@ -852,6 +896,7 @@
     finish(2)
     chain(2, 0, 1)
     chain(1, 1, 1)
+    gene_part = jnp.sum(mine_mask * cos_gene / kept)
     loss_part = jnp.broadcast_to(-gene_part / SLIDES - jnp.sum(cos_spot) / spots_all, (1, cd))
     whole(0, gm)
     chain(1, 0, 0)
@@ -909,33 +954,38 @@
         pair(i).wait_send()
     pair(2).wait_recv()
     fsum = ftotal + pair_r[2, 0:2, 0:cd]
-    loss_o[0, 0] = jnp.sum(fsum[1:2, 0:1]) + rest
+    last_o[cd // 128 : cd // 128 + 1, :] = fsum[1:2, 0:128] + rest
     fsum = fsum[0:1] + 2.0 * excess / count_total
     for h in range(cd // 128):
         g = my_gate[h : h + 1, :]
-        gf_o[h : h + 1, :] = fsum[:, h * 128 : (h + 1) * 128] * g * (1.0 - g)
+        last_o[h : h + 1, :] = fsum[:, h * 128 : (h + 1) * 128] * g * (1.0 - g)
     for k in (3, 2, 1):
         fin_wait(k)
     ge_o[...] = gexpr[...]
 
 
-def finish_kernel(probs, gp, tot, ge, loss, gf, gl_o, ge_o, loss_o, gf_o, gl, gx, out_s):
+def finish_kernel(probs, gp, tot, ge, last, gl_o, ge_o, loss_o, gf_o, gl, gx, loss, out_s):
     f32 = jnp.float32
     parts = 4
     cc = probs.shape[1] // parts
     copies = []
+
+    def send(src, dst):
+        copies.append(pltpu.make_async_copy(src, dst, out_s.at[len(copies)]))
+        copies[-1].start()
+
+    gx[...] = ge[...].astype(f32)
+    send(gx, ge_o)
+    n = gf_o.shape[0]
+    loss[...] = last[n : n + 1, 0:1]
+    send(last.at[pl.ds(0, n)], gf_o)
+    send(loss, loss_o)
     for i in range(parts):
         for c in range(i * cc, (i + 1) * cc, 128):
             at = slice(c, c + 128)
             gl[:, at] = probs[:, at] * (gp[:, at].astype(f32) - tot[...])
         at = pl.ds(i * cc, cc)
-        copies.append(pltpu.make_async_copy(gl.at[:, at], gl_o.at[:, at], out_s.at[i]))
-        copies[-1].start()
-    gx[...] = ge[...].astype(f32)
-    copies.append(pltpu.make_async_copy(gx, ge_o, out_s.at[parts]))
-    copies[-1].start()
-    gf_o[...] = gf[...]
-    loss_o[0, 0] = loss[0, 0]
+        send(gl.at[:, at], gl_o.at[:, at])
     for c in copies:
         c.wait()
 
@@ -966,7 +1016,7 @@
         vmem(2, grp, gq, dtype=bf16), vmem(grp, 2 * gq), vmem(grp, 2 * gq, dtype=bf16),
         vmem(grp, gq, dtype=bf16), vmem(gq, 2 * grp, dtype=bf16),
         vmem(nspot, 8, 128), vmem(nspot, 8, 128),
-        vmem(4, 8, wide), vmem(4, 8, wide), vmem(2, 8, wide), vmem(4, 8, wide),
+        vmem(4, 8, wide), vmem(4, 8, wide), vmem(2, 3, 1, wide), vmem(4, 3, 1, wide),
         vmem(4, 2 * rows, cc, dtype=bf16), vmem(4, 2 * rows, cc, dtype=bf16),
         vmem(4, 2 * rows, cc, dtype=bf16), vmem(4, 2 * rows, cc, dtype=bf16),
         vmem(4, rows, cc, dtype=bf16), vmem(4, rows, cc, dtype=bf16),
@@ -982,42 +1032,40 @@
         dma(12), dma(12), dma(12), dma(12), dma(4), dma(4), dma(8), dma(8),
         dma(4), dma(4), dma(2, nz), dma(nz), dma(nspot), dma(nspot),
         dma(nspot), dma(nspot),
-        dma(4), dma(4), dma(4), dma(4),
+        dma(4), dma(4), dma(8), dma(8),
         dma(4), dma(4), dma(4), dma(4), dma(4), dma(4), dma(4), dma(4),
         dma(nspot), dma(nspot), dma(nspot), dma(nspot), dma(4), dma(4), dma(1), dma(1),
     ]
     v, a = pl.BlockSpec(memory_space=pltpu.VMEM), pl.BlockSpec(memory_space=pl.ANY)
-    s, hbm = pl.BlockSpec(memory_space=pltpu.SMEM), pl.BlockSpec(memory_space=pltpu.HBM)
     shape = jax.ShapeDtypeStruct
     fparts = (cd // 128, 128)
     given = (logits, filt.reshape(-1, 128), expr, target, gene_mask, density.reshape(-1, 128))
-    loss, probs, gp, tot, grad_filt, grad_expr = pl.pallas_call(
+    probs, gp, tot, last, grad_expr = pl.pallas_call(
         functools.partial(group_kernel, nspot),
         out_shape=[
-            shape((1, 1), f32),
             vmem(rows, cells),
             vmem(rows, cells, dtype=bf16),
             vmem(rows, 128),
-            vmem(*fparts),
+            vmem(8, 128),
             vmem(cd, half, dtype=bf16),
         ],
-        in_specs=[hbm] * 6,
-        out_specs=[s, v, v, v, v, v],
+        in_specs=[a] * 6,
+        out_specs=[v] * 5,
         scratch_shapes=buffers + sems,
         compiler_params=pltpu.CompilerParams(
             collective_id=0, has_side_effects=True, vmem_limit_bytes=VMEM_BYTES
         ),
         name="group_step",
-    )(*(pltpu.with_memory_space_constraint(v, pltpu.HBM) for v in given))
+    )(*(pltpu.with_memory_space_constraint(g, pltpu.HBM) for g in given))
     grad_logits, grad_expr, loss, grad_filt = pl.pallas_call(
         finish_kernel,
         out_shape=[shape((rows, cells), f32), shape((cd, half), f32), shape((1, 1), f32), shape(fparts, f32)],
-        in_specs=[v, v, v, v, s, v],
-        out_specs=[a, a, s, v],
-        scratch_shapes=[vmem(rows, cells), vmem(cd, half), dma(5)],
+        in_specs=[v] * 5,
+        out_specs=[a] * 4,
+        scratch_shapes=[vmem(rows, cells), vmem(cd, half), vmem(1, 1), dma(7)],
         compiler_params=pltpu.CompilerParams(vmem_limit_bytes=LAST_BYTES),
         name="finish_step",
-    )(probs, gp, tot, grad_expr, loss, grad_filt)
+    )(probs, gp, tot, grad_expr, last)
     return (loss.reshape(()), grad_logits, grad_filt.reshape(-1), grad_expr)
 
 

time: 108 us -> 106 us (0.981)
  Pallas kernels: 107 us -> 104 us
    pallas_call x1, Pallas kernels: 104 us -> 102 us  [grouped(): pl.pallas_call(functools.partial(group_kernel, nspot), out_shape=[vmem(ro...]
    pallas_call x1, Pallas kernels: 2.98 us -> 1.8 us  [grouped(): pl.pallas_call(finish_kernel, out_shape=[shape((rows, cells), f32), shape...]
where the time goes in v3:
time: 106 us; the launch traced here: 105 us
  Pallas kernels  104 us (98%)
    pallas_call x1, Pallas kernels, grouped(): pl.pallas_call(functools.partial(group_kernel, nspot), out_shape=[vmem(ro...  102 us

profile of v3, /device:TPU:0, one launch (start us, length us, event | category | flops | bytes accessed | tf_op | source)
XLA Modules:
  0.0 104.8 jit_solution(1678854073923672113)
XLA Ops:
  0.6 102.4 %group_step.1 = (f32[128,4096]{1,0:T(8,128)S(1)}, bf16[128,4096]{1,0:T(8,128)(2,1)S(1)}, f32[128,128]{1,0:T(8,128)S(1)}, f32[8,128]{1,0:T(8,128)S(1)}, bf16[256,1024]{1,0:T(8,128)(2,1)S(1)}) custom-call(bf16[128,4096]{1,0:T(8,128)(2,1)} %logits_h.1, f32[2,128]{1,0:T(2,128)} %bitcast.4, bf16[256,1024]{1,0:T(8,128)(2,1)} %expr.1, bf16[256,1024]{1,0:T(8,128)(2,1)} %target.1, ...), custom_call_target="tpu_custom_call" | custom-call | tf_op jit(solution)/shard_map/group_step/pallas_call | solution.py:1043
  103.0 1.8 %finish_step.1 = (f32[128,4096]{1,0:T(8,128)}, f32[256,1024]{1,0:T(8,128)}, f32[1,1]{1,0:T(1,128)}, f32[2,128]{1,0:T(2,128)}) custom-call(f32[128,4096]{1,0:T(8,128)S(1)} %get-tuple-element.13.probs, bf16[128,4096]{1,0:T(8,128)(2,1)S(1)} %get-tuple-element.14.gp, f32[128,128]{1,0:T(8,128)S(1)} %get-tuple-element.15.tot, ...), custom_call_target="tpu_custom_call" | custom-call | tf_op jit(solution)/shard_map/finish_step/pallas_call | solution.py:1060

commit v4 on v0

--- a/solution.py
+++ b/solution.py
@@ -1,6 +1,10 @@
+import functools
+
 import jax
 import jax.numpy as jnp
 from jax import lax
+from jax.experimental import pallas as pl
+from jax.experimental.pallas import tpu as pltpu
 from jax.sharding import PartitionSpec as P
 
 SPOTS = 4096
@@ -59,7 +63,7 @@
     return (grad_pred, spot_stats[0] * spot_a * spot_b)
 
 
-def per_device(logits, filt, expr, target, gene_mask, density):
+def streamed(logits, filt, expr, target, gene_mask, density):
     f32 = jnp.float32
     bf16 = jnp.bfloat16
     nspot = lax.axis_size("spot")
@@ -145,6 +149,944 @@
     return (loss, grad_logits, grad_filt, grad_expr)
 
 
+GROUP = 4
+PIECE = 128
+MESH = pl.DeviceIdType.MESH
+VMEM_BYTES = 44 << 20
+LAST_BYTES = 16 << 20
+
+
+def remote(src, dst, send, recv, dev):
+    return pltpu.make_async_remote_copy(
+        src_ref=src, dst_ref=dst, send_sem=send, recv_sem=recv, device_id=dev, device_id_type=MESH
+    )
+
+
+def dot_nt(a, b):
+    return lax.dot_general(a, b, (((1,), (1,)), ((), ())), preferred_element_type=jnp.float32)
+
+
+def column(row, length):
+    return jnp.transpose(jnp.broadcast_to(row, (128, length)))
+
+
+def fold(values):
+    total = values[:, 0:128]
+    for i in range(1, values.shape[1] // 128):
+        total = total + values[:, i * 128 : (i + 1) * 128]
+    return total
+
+
+def group_kernel(
+    nspot, logits_h, filt_h, expr, target, mask_h, dens_h,
+    probs, gpb, tot_o, last_o, ge_o,
+    logits, filt, mask, dens, rawq, wraw, wg, wt, ebuf, tbuf, gcol, small, pfin, ahead,
+    psx, prx, psy, pry, ps2x, pr2x, ps2y, pr2y, hx, hy, massp, massr, statg, statr, acc, spots, spotr,
+    dpa, grad, dsend, dright, dleft, dwo, dws, dwr, gps, gpr, rowsum, tile_s, tile_r, tz, gms, gmr, gmcol,
+    fsend, frecv, pair_s, pair_r,
+    hello, lc, zs_s, zs_r, ez_s, ez_r, w_s, w_r, wd_s, wd_r, pr_s, pr_r,
+    px_s, px_r, py_s, py_r, p2x_s, p2x_r, p2y_s, p2y_r, ms_s, ms_r, st_s, st_r, ag_s, ag_r,
+    dr_s, dr_r, dl_s, dl_r, dw_s, dw_r, gp_s, gp_r, tl_s, tl_r, tz_s, tz_r, gm_s, gm_r, fz_s, fz_r,
+):
+    f32, bf16 = jnp.float32, jnp.bfloat16
+    rows, cells = probs.shape
+    cd, genes = expr.shape
+    nz = nspot // GROUP
+    np_ = genes // PIECE
+    grp = GROUP * rows
+    mine = cells // GROUP
+    spots_all = nspot * 2 * rows
+    me, j = lax.axis_index("spot"), lax.axis_index("gene")
+    sib = 1 - j
+    z, q = me // GROUP, me % GROUP
+    x, y = q % 2, q // 2
+    nbr = [me, me + 1 - 2 * x, me + 2 - 4 * y, me + 3 - 2 * x - 4 * y]
+    nq = [n % GROUP for n in nbr]
+    here = (me, sib)
+    has_right, has_left = z < nz - 1, z > 0
+    ends = (z == 0, z == nz - 1)
+    chip = [(n, j) for n in nbr]
+    beside = ((me + GROUP, j), (me - GROUP, j))
+
+    def at_k(k, h=0):
+        return pl.ds(h * grp + k * rows, rows)
+
+    def piece(g):
+        return pl.ds(g * PIECE, PIECE)
+
+    def half_of(buf, r, g):
+        return buf.at[g // 2, r, pl.ds(g % 2 * PIECE, PIECE)]
+
+    def seg(p):
+        return pl.ds(pl.multiple_of(p * cd, cd), cd)
+
+    barrier = pltpu.get_barrier_semaphore()
+
+    def greet(dev):
+        pl.semaphore_signal(barrier, inc=1, device_id=dev, device_id_type=MESH)
+
+    greet(chip[1])
+    greet(chip[2])
+
+    @pl.when(has_right)
+    def _():
+        greet(beside[0])
+
+    @pl.when(has_left)
+    def _():
+        greet(beside[1])
+
+    greet(here)
+    loads = [pltpu.make_async_copy(logits_h, logits, lc.at[0])]
+    loads += [
+        pltpu.make_async_copy(s, d, lc.at[1 + i])
+        for i, (s, d) in enumerate(((filt_h, filt), (mask_h, mask), (dens_h, dens)))
+    ]
+    loads += [
+        pltpu.make_async_copy(
+            expr.at[:, pl.ds(i * 2 * PIECE, 2 * PIECE)], ebuf.at[i, seg(z), :], lc.at[4 + i]
+        )
+        for i in range(np_ // 2)
+    ]
+    loads += [
+        pltpu.make_async_copy(
+            target.at[pl.ds(pl.multiple_of(c * rows, rows), rows)],
+            tbuf.at[pl.ds(i * rows, rows)],
+            lc.at[4 + np_ // 2 + i],
+        )
+        for i, c in enumerate((j, sib))
+    ]
+    for c in loads:
+        c.start()
+    loads[0].wait()
+
+    step = 32
+
+    @pl.loop(0, rows // step)
+    def _(i):
+        at = pl.ds(pl.multiple_of(i * step, step), step)
+        s = logits[at, :].astype(f32)
+        e = jnp.exp(s - jnp.max(s, axis=1, keepdims=True))
+        p = e * (1.0 / jnp.sum(e, axis=1, keepdims=True))
+        probs[at, :] = p
+        for o in range(nspot):
+            c = o // GROUP * cd
+            rawq[o % GROUP, at, c : c + cd] = p[:, o * cd : (o + 1) * cd].astype(bf16)
+
+    for c in loads[1:]:
+        c.wait()
+    small[pl.ds(z, 1), 0 : cd // 128, :] = filt[...][None]
+    maskf = mask[pl.ds(z, 1), :].astype(f32)
+    kept_mine = jnp.sum(maskf)
+    pair_s[0] = jnp.full((8, 2 * rows), kept_mine)
+    pl.semaphore_wait(barrier, 3 + has_right.astype(jnp.int32) + has_left.astype(jnp.int32))
+
+    def zsmall(way, p):
+        return remote(small.at[p], small.at[p], zs_s.at[way, p], zs_r.at[p], beside[way])
+
+    def zsend(way, p, g):
+        u = half_of(ebuf, seg(p), g)
+        return remote(u, u, ez_s.at[way, p, g], ez_r.at[p, g], beside[way])
+
+    def both(make):
+        @pl.when(has_right)
+        def _():
+            make(0).start()
+
+        @pl.when(has_left)
+        def _():
+            make(1).start()
+
+    def hop(s, make):
+        @pl.when(z >= s)
+        def _():
+            make(0, z - s).wait_recv()
+
+            @pl.when(has_right)
+            def _():
+                make(0, z - s).start()
+
+        @pl.when(z + s <= nz - 1)
+        def _():
+            make(1, z + s).wait_recv()
+
+            @pl.when(has_left)
+            def _():
+                make(1, z + s).start()
+
+    def own(g):
+        if g < np_:
+            both(lambda way: zsend(way, z, g))
+
+    def along(s, g):
+        if 0 <= g < np_:
+            hop(s, lambda way, p: zsend(way, p, g))
+
+    both(lambda way: zsmall(way, z))
+    own(0)
+    own(1)
+
+    def wcopy(k):
+        return remote(rawq.at[nq[k]], wraw.at[at_k(k)], w_s.at[k], w_r.at[k], chip[k])
+
+    def wsib(k):
+        return remote(wraw.at[at_k(k)], wraw.at[at_k(k, 1)], wd_s.at[k], wd_r.at[k], here)
+
+    def pair(i):
+        return remote(pair_s.at[i], pair_r.at[i], pr_s.at[i], pr_r.at[i], here)
+
+    wcopy(1).start()
+    wcopy(2).start()
+    pl.semaphore_signal(hello, inc=1, device_id=chip[1], device_id_type=MESH)
+    wraw[at_k(0), :] = rawq[pl.ds(q, 1)].reshape(rows, mine)
+    wsib(0).start()
+    pair(0).start()
+    pl.semaphore_wait(hello, 1)
+    wcopy(3).start()
+
+    def gated(k, h):
+        r = at_k(k, h)
+        for c in range(0, mine, 512):
+            at = pl.ds(c, 512)
+            wg[r, at] = (gcol[0:1, at] * wraw[r, at].astype(f32)).astype(bf16)
+
+    def turned(k, h):
+        r = at_k(k, h)
+        for c in range(0, mine, 512):
+            at = pl.ds(c, 512)
+            wt[at, r] = jnp.transpose(wg[r, at].astype(f32)).astype(bf16)
+
+    def arrive(k):
+        wcopy(k).wait_recv()
+        wsib(k).start()
+        gated(k, 0)
+
+    def arrive_sib(k):
+        wsib(k).wait_recv()
+        gated(k, 1)
+
+    first, second = pl.ds(0, rows), pl.ds(rows, rows)
+
+    def pxcopy(g, n):
+        h = (first, second)[n]
+        return remote(psx.at[g, h], prx.at[g, h], px_s.at[n, g], px_r.at[n, g], chip[1])
+
+    def pycopy(g, n):
+        h = (first, second)[n]
+        return remote(psy.at[g, h], pry.at[g, h], py_s.at[n, g], py_r.at[n, g], chip[2])
+
+    def p2xcopy(g):
+        return remote(ps2x.at[g], pr2x.at[g], p2x_s.at[g], p2x_r.at[g], chip[1])
+
+    def p2ycopy(g):
+        return remote(ps2y.at[g], pr2y.at[g], p2y_s.at[g], p2y_r.at[g], chip[2])
+
+    def piece_of(g, at):
+        return ebuf[g // 2, at, g % 2 * PIECE : (g % 2 + 1) * PIECE]
+
+    def project(g):
+        share(g, jnp.dot(wg[...], piece_of(g, pl.ds(0, mine)), preferred_element_type=f32))
+
+    far = (1 - z // (nz // 2)) * (nz - 1)
+    near = pl.ds(pl.multiple_of(z // (nz // 2) * cd, cd), mine - cd)
+
+    def project_ahead(g):
+        ahead[...] = jnp.dot(wg[:, near], piece_of(g, near), preferred_element_type=f32)
+
+    def project_last(g):
+        share(g, ahead[...] + jnp.dot(wg[:, seg(far)], piece_of(g, seg(far)), preferred_element_type=f32))
+
+    def share(g, v):
+        def part(k, h):
+            s = h * grp + k * rows
+            return v[s : s + rows]
+
+        psx[g, second] = part(3, 0).astype(bf16)
+        pxcopy(g, 1).start()
+        psy[g, second] = part(3, 1).astype(bf16)
+        pycopy(g, 1).start()
+        psx[g, first] = part(1, 0).astype(bf16)
+        pxcopy(g, 0).start()
+        psy[g, first] = part(2, 1).astype(bf16)
+        pycopy(g, 0).start()
+        hx[g] = part(2, 0)
+        hy[g] = part(1, 1)
+        pfin[first, piece(g)] = part(0, 0)
+        pfin[second, piece(g)] = part(0, 1)
+
+    def relay(g):
+        pxcopy(g, 1).wait_recv()
+        ps2y[g] = (hx[g] + prx[g, second].astype(f32)).astype(bf16)
+        p2ycopy(g).start()
+        pycopy(g, 1).wait_recv()
+        ps2x[g] = (hy[g] + pry[g, second].astype(f32)).astype(bf16)
+        p2xcopy(g).start()
+
+    def whole(g):
+        at = piece(g)
+        pxcopy(g, 0).wait_recv()
+        pycopy(g, 0).wait_recv()
+        p2ycopy(g).wait_recv()
+        p2xcopy(g).wait_recv()
+        pfin[first, at] += prx[g, first].astype(f32) + pr2y[g].astype(f32)
+        pfin[second, at] += pry[g, first].astype(f32) + pr2x[g].astype(f32)
+        p = pfin[:, at]
+        t = tbuf[:, at].astype(f32)
+        for i, v in enumerate((p * p, p * t, t * t)):
+            statg[i, :, at] = jnp.sum(v, axis=0, keepdims=True)
+            acc[i] += v
+
+    parts = (pl.ds(0, (np_ - 2) * PIECE), pl.ds((np_ - 2) * PIECE, 2 * PIECE))
+
+    def stat(k, n):
+        i = 2 * k + n
+        return remote(
+            statg.at[:, :, parts[n]], statr.at[k, :, :, parts[n]], st_s.at[i], st_r.at[i], chip[k]
+        )
+
+    def gates():
+        for p in range(nz):
+            for h in range(cd // 128):
+                g = jax.nn.sigmoid(small[p, h : h + 1, :])
+                c = p * cd + h * 128
+                gcol[:, c : c + 128] = jnp.broadcast_to(g, (8, 128))
+
+    def mass_copy(k):
+        return remote(massp.at[k], massr.at[k], ms_s.at[k], ms_r.at[k], chip[k])
+
+    def masses():
+        m = dot_nt(jnp.ones((8, mine), bf16), wg[...])
+        for k in range(GROUP):
+            for h in range(2):
+                s = h * grp + k * rows
+                massp[k, h : h + 1, :] = m[0:1, s : s + rows]
+            if k:
+                mass_copy(k).start()
+
+    acc[...] = jnp.zeros_like(acc)
+    hop(1, zsmall)
+    along(1, 0)
+    own(2)
+    hop(2, zsmall)
+    along(1, 1)
+    along(2, 0)
+    own(3)
+    hop(3, zsmall)
+    gates()
+    gated(0, 0)
+    arrive(1)
+    arrive(2)
+    arrive_sib(0)
+    along(1, 2)
+    along(2, 1)
+    own(4)
+    arrive_sib(1)
+    arrive_sib(2)
+    for k in range(3):
+        turned(k, 0)
+    arrive(3)
+    arrive_sib(3)
+    along(3, 0)
+    project(0)
+    for s in range(3, np_ + 2):
+        along(1, s)
+        along(2, s - 1)
+        own(s + 2)
+        if s == np_ + 1:
+            relay(s - 3)
+        along(3, s - 2)
+        if s < np_ + 1:
+            project(s - 2)
+        else:
+            project_last(s - 2)
+        if s == 4:
+            masses()
+        if s == 5:
+            for k in range(3):
+                turned(k, 1)
+        if s == 6:
+            turned(3, 0)
+            turned(3, 1)
+        if s < np_ + 1:
+            relay(s - 3)
+        if s == np_:
+            project_ahead(np_ - 1)
+        if s > 4:
+            whole(s - 5)
+    whole(np_ - 3)
+    for k in (3, 1, 2):
+        stat(k, 0).start()
+    pair(0).wait_recv()
+    kept = jnp.maximum(kept_mine + jnp.sum(pair_r[0, 0:1, 0:1]), 1.0)
+    weight = maskf / kept / SLIDES
+    relay(np_ - 1)
+    whole(np_ - 2)
+    whole(np_ - 1)
+    for k in (3, 1, 2):
+        stat(k, 1).start()
+
+    for i in range(3):
+        spots[i] = jnp.sum(jnp.transpose(acc[i]), axis=0, keepdims=True)
+    spot_copy = remote(spots, spotr, pr_s.at[4], pr_r.at[4], here)
+    spot_copy.start()
+
+    def slide_sums(n):
+        for k in (1, 2, 3):
+            stat(k, n).wait_recv()
+        at = parts[n]
+        pred_sq, dots, truth_sq = (
+            (statg[i, :, at] + statr[1, i, :, at]) + (statr[2, i, :, at] + statr[3, i, :, at])
+            for i in range(3)
+        )
+        slide_a = lax.rsqrt(pred_sq + eps_norm)
+        slide_b = lax.rsqrt(truth_sq + eps_norm)
+        w = weight[:, at.start : at.start + at.size]
+        return (
+            -w * slide_a * slide_b,
+            w * dots * slide_a**3 * slide_b,
+            w * (dots * slide_a * slide_b),
+        )
+
+    coefs = [slide_sums(0), None]
+    spot_copy.wait_recv()
+    spot_pp, spot_dot, spot_tt = (
+        spots[i] + jnp.concatenate([spotr[i, :, rows : 2 * rows], spotr[i, :, 0:rows]], axis=1)
+        for i in range(3)
+    )
+    spot_a = lax.rsqrt(spot_pp + eps_norm)
+    spot_b = lax.rsqrt(spot_tt + eps_norm)
+    col_t = column(-(spot_a * spot_b) / spots_all, 2 * rows)
+    col_p = column(spot_dot * spot_a**3 * spot_b / spots_all, 2 * rows)
+
+    def agcopy(i, g):
+        src, dst, to = (
+            (at_k(0), at_k(1), 1), (at_k(0, 1), at_k(1, 1), 1), (at_k(0, 1), at_k(2, 1), 2),
+            (at_k(0), at_k(2), 2), (at_k(1), at_k(3), 2), (at_k(2, 1), at_k(3, 1), 1),
+        )[i]
+        return remote(half_of(dpa, src, g), half_of(dpa, dst, g), ag_s.at[i, g], ag_r.at[i, g], chip[to])
+
+    def give(g):
+        n = 0 if g < np_ - 2 else 1
+        if n and coefs[1] is None:
+            coefs[1] = slide_sums(1)
+        c = g * PIECE - parts[n].start
+        c_t, c_p = (v[:, c : c + PIECE] for v in coefs[n][0:2])
+        at = piece(g)
+        d = ((c_t + col_t) * tbuf[:, at].astype(f32) + (c_p + col_p) * pfin[:, at]).astype(bf16)
+        lanes = pl.ds(g % 2 * PIECE, PIECE)
+        dpa[g // 2, at_k(0), lanes] = d[0:rows]
+        dpa[g // 2, at_k(0, 1), lanes] = d[rows : 2 * rows]
+        for i in range(4):
+            agcopy(i, g).start()
+
+    def give_on(g):
+        agcopy(0, g).wait_recv()
+        agcopy(4, g).start()
+        agcopy(2, g).wait_recv()
+        agcopy(5, g).start()
+
+    def dcopy(way, p, g):
+        if way == 0:
+            return remote(dsend.at[p, g], dright.at[p, g], dr_s.at[p, g], dr_r.at[p, g], beside[0])
+        return remote(dsend.at[p, g], dleft.at[p, g], dl_s.at[p, g], dl_r.at[p, g], beside[1])
+
+    def expr_grad_first():
+        for i in (1, 3, 4, 5):
+            agcopy(i, 0).wait_recv()
+        up = z // (nz // 2)
+
+        @pl.loop(0, nz)
+        def _(u):
+            p = up * u + (1 - up) * (nz - 1 - u)
+            v = jnp.dot(wt[seg(p), :], dpa[0, :, 0:PIECE], preferred_element_type=f32)
+            grad[p, :, 0:PIECE] = v
+
+            @pl.when((ends[0] | ends[1]) & (p != z))
+            def _():
+                dsend[p, 0] = v.astype(bf16)
+
+            @pl.when(ends[0] & (p != z))
+            def _():
+                dcopy(0, p, 0).start()
+
+            @pl.when(ends[1] & (p != z))
+            def _():
+                dcopy(1, p, 0).start()
+
+    def expr_grad(g):
+        for i in (1, 3, 4, 5):
+            agcopy(i, g).wait_recv()
+        lanes = slice(g % 2 * PIECE, (g % 2 + 1) * PIECE)
+        v = jnp.dot(wt[...], dpa[g // 2, :, lanes], preferred_element_type=f32)
+        for p in range(nz):
+            grad[p, :, piece(g)] = v[p * cd : (p + 1) * cd]
+
+        @pl.when(ends[0])
+        def _():
+            for p in range(1, nz):
+                dsend[p, g] = v[p * cd : (p + 1) * cd].astype(bf16)
+
+        @pl.when(ends[1])
+        def _():
+            for p in range(nz - 1):
+                dsend[p, g] = v[p * cd : (p + 1) * cd].astype(bf16)
+
+    def start_from_ends(u, g):
+        if not 0 <= g < np_:
+            return
+
+        @pl.when(ends[0])
+        def _():
+            dcopy(0, nz - 1 - u, g).start()
+
+        @pl.when(ends[1])
+        def _():
+            dcopy(1, u, g).start()
+
+    def starts(*pieces):
+        for u, g in pieces:
+            start_from_ends(u, g)
+
+    def chain(hops, u, g):
+        if nz - 1 - u > hops:
+
+            @pl.when(z == hops)
+            def _():
+                p = nz - 1 - u
+                dcopy(0, p, g).wait_recv()
+                dsend[p, g] = (grad[p, :, piece(g)] + dright[p, g].astype(f32)).astype(bf16)
+                dcopy(0, p, g).start()
+
+            @pl.when(nz - 1 - z == hops)
+            def _():
+                dcopy(1, u, g).wait_recv()
+                dsend[u, g] = (grad[u, :, piece(g)] + dleft[u, g].astype(f32)).astype(bf16)
+                dcopy(1, u, g).start()
+
+    def finish(g):
+        at = piece(g)
+        ge_o[:, at] = grad[pl.ds(z, 1), :, at].reshape(cd, PIECE)
+
+        @pl.when(has_left)
+        def _():
+            dcopy(0, z, g).wait_recv()
+            ge_o[:, at] += dright[pl.ds(z, 1), g].reshape(cd, PIECE).astype(f32)
+
+        @pl.when(has_right)
+        def _():
+            dcopy(1, z, g).wait_recv()
+            ge_o[:, at] += dleft[pl.ds(z, 1), g].reshape(cd, PIECE).astype(f32)
+
+    def tile_copy(k):
+        return remote(tile_s, tile_r.at[k], tl_s.at[k], tl_r.at[k], chip[k])
+
+    def zcopy(buf, src, r, ss, rs):
+        to = (z + r) % nz
+        return remote(buf.at[src], buf.at[z], ss.at[r], rs.at[r], (to * GROUP + q, j))
+
+    def zcopy_wait(buf, r, ss, rs):
+        o = (z + nz - r) % nz
+        remote(buf.at[o], buf.at[o], ss.at[r], rs.at[r], here).wait_recv()
+
+    def chip_masses():
+        for k in (1, 2, 3):
+            mass_copy(k).wait_recv()
+        return (massp[0, 0:2] + massr[1, 0:2]) + (massr[2, 0:2] + massr[3, 0:2])
+
+    def own_dens():
+        d = dens[...].astype(f32)
+        return jnp.where(j == 0, d, jnp.concatenate([d[1:2], d[0:1]], axis=0))
+
+    def tile_start():
+        mass, d = chip_masses(), own_dens()
+        gene = fold(coefs[0][2]) + fold(coefs[1][2])
+        cos = fold(spot_dot * spot_a * spot_b)
+        tile_s[0:1] = -2.0 / GROUP * gene - cos / spots_all
+        tile_s[1:2] = d[0:1] + d[1:2]
+        f = jax.nn.sigmoid(filt[...])
+        tile_s[2:3] = f[0:1] + f[1:2]
+        tile_s[3:4] = mass[0:1] + mass[1:2]
+        kl = d * (jnp.log(d) - jnp.log(mass))
+        tile_s[4:5] = kl[0:1] + kl[1:2]
+        tile_s[5:8] = jnp.zeros((3, 128), f32)
+        for k in (3, 1, 2):
+            tile_copy(k).start()
+        return mass, d
+
+    def tile_along():
+        for k in (1, 2, 3):
+            tile_copy(k).wait_recv()
+        tz[pl.ds(z, 1)] = ((tile_s[...] + tile_r[1]) + (tile_r[2] + tile_r[3]))[None]
+        for r in range(1, nz):
+            zcopy(tz, z, r, tz_s, tz_r).start()
+
+    def gm_copy(k):
+        return remote(gms, gmr.at[k], gm_s.at[k], gm_r.at[k], chip[k])
+
+    def totals(mass, d):
+        for r in range(1, nz):
+            zcopy_wait(tz, r, tz_s, tz_r)
+        t = tz[0]
+        for p in range(1, nz):
+            t = t + tz[p]
+        loss_part, count, gate, mass_total, kl = (jnp.sum(t[i : i + 1]) for i in range(5))
+        logs = jnp.log(jnp.where(lax.broadcasted_iota(jnp.int32, (1, 128), 1) == 0, count, mass_total))
+        log_count, log_mass = jnp.sum(logs[:, 0:1]), jnp.sum(logs[:, 1:2])
+        excess = gate / count - 1.0
+        gms[...] = jnp.zeros_like(gms)
+        gms[0:2] = (1.0 / mass_total - d / count / mass).astype(bf16).astype(f32)
+        for k in (3, 1, 2):
+            gm_copy(k).start()
+        pair_s[1] = jnp.full((8, 2 * rows), loss_part + kl / count - log_count + log_mass + excess * excess)
+        pair(1).start()
+        return 2.0 * excess / count
+
+    def mass_columns():
+        gmcol[at_k(0), :] = column(gms[0:1], rows)
+        for k in (1, 2, 3):
+            gm_copy(k).wait_recv()
+            gmcol[at_k(k), :] = column(gmr[k, 0:1], rows)
+
+    def dwcopy(p):
+        return remote(dws.at[p], dwr.at[p], dw_s.at[p], dw_r.at[p], here)
+
+    def weight_grad(p):
+        cs = slice(p * cd, (p + 1) * cd)
+
+        def rows_of(h):
+            d = dot_nt(dpa[0, h * grp : (h + 1) * grp, :], ebuf[0, cs, :])
+            for c in range(1, np_ // 2):
+                d = d + dot_nt(dpa[c, h * grp : (h + 1) * grp, :], ebuf[c, cs, :])
+            return d
+
+        dws[p] = rows_of(1)
+        dwcopy(p).start()
+        dwo[p] = rows_of(0)
+
+    def gpcopy(k, p):
+        return remote(gps.at[p, at_k(k)], gpr.at[k, p], gp_s.at[k, p], gp_r.at[k, p], chip[k])
+
+    def give_back(p):
+        dwcopy(p).wait_recv()
+        cs = pl.ds(p * cd, cd)
+        total = jnp.zeros((1, cd), f32)
+        for k in (3, 1, 2, 0):
+            r = at_k(k)
+            gm = gmcol[r, :]
+            gw = dwo[p, r] + dwr[p, r] + jnp.concatenate([gm] * (cd // 128), axis=1)
+            total = total + jnp.sum(gw * wraw[r, cs].astype(f32), axis=0, keepdims=True)
+            gps[p, r] = (gcol[0:1, cs] * gw).astype(bf16)
+            if k:
+                gpcopy(k, p).start()
+        fsend[p] = total
+
+    def filter_along():
+        frecv[pl.ds(z, 1)] = fsend[pl.ds(z, 1)]
+        for r in range(1, nz):
+            to = (z + r) % nz
+            remote(fsend.at[to], frecv.at[z], fz_s.at[r], fz_r.at[r], (to * GROUP + q, j)).start()
+
+    def take(k, p, start=False):
+        if k:
+            gpcopy(k, p).wait_recv()
+            v = gpr[k, p]
+        else:
+            v = gps[p, at_k(0)]
+        at = pl.ds(pl.multiple_of((p * GROUP + nq[k]) * cd, cd), cd)
+        gpb[:, at] = v
+        s = fold(probs[:, at] * v.astype(f32))
+        if start:
+            rowsum[...] = s
+        else:
+            rowsum[...] += s
+
+    def sent_first():
+        for k in (1, 2, 3):
+            wcopy(k).wait_send()
+            mass_copy(k).wait_send()
+            for n in (0, 1):
+                stat(k, n).wait_send()
+        for k in range(GROUP):
+            wsib(k).wait_send()
+        pair(0).wait_send()
+        spot_copy.wait_send()
+
+        @pl.loop(0, np_)
+        def _(g):
+            for c in (pxcopy, pycopy):
+                c(g, 0).wait_send()
+                c(g, 1).wait_send()
+            p2xcopy(g).wait_send()
+            p2ycopy(g).wait_send()
+
+    def sent_along():
+        @pl.loop(0, nz)
+        def _(p):
+            @pl.when(has_right & (p <= z))
+            def _():
+                zsmall(0, p).wait_send()
+                for g in range(np_):
+                    zsend(0, p, g).wait_send()
+
+            @pl.when(has_left & (p >= z))
+            def _():
+                zsmall(1, p).wait_send()
+                for g in range(np_):
+                    zsend(1, p, g).wait_send()
+
+    def sent_back():
+        for g in range(np_):
+            for i in range(6):
+                agcopy(i, g).wait_send()
+
+    def sent_last():
+        for k in (1, 2, 3):
+            tile_copy(k).wait_send()
+            gm_copy(k).wait_send()
+            for p in range(nz):
+                gpcopy(k, p).wait_send()
+        for r in range(1, nz):
+            zcopy(tz, z, r, tz_s, tz_r).wait_send()
+            zcopy(fsend, z, r, fz_s, fz_r).wait_send()
+        for p in range(nz):
+            dwcopy(p).wait_send()
+        for i in (1, 2):
+            pair(i).wait_send()
+
+    def sent_sums():
+        @pl.loop(0, nz)
+        def _(p):
+            @pl.when(has_right & (p > z))
+            def _():
+                for g in range(np_):
+                    dcopy(0, p, g).wait_send()
+
+            @pl.when(has_left & (p < z))
+            def _():
+                for g in range(np_):
+                    dcopy(1, p, g).wait_send()
+
+    give(0)
+    give(1)
+    coefs[1] = slide_sums(1)
+    mass, d = tile_start()
+    give_on(0)
+    give(2)
+    give_on(1)
+    give(3)
+    expr_grad_first()
+    give_on(2)
+    give(4)
+    tile_along()
+    expr_grad(1)
+    starts((0, 1), (1, 1), (2, 1))
+    give_on(3)
+    give(5)
+    chain(1, 0, 0)
+    give_on(4)
+    expr_grad(2)
+    starts((0, 2), (1, 2))
+    chain(1, 1, 0)
+    give(6)
+    give_on(5)
+    expr_grad(3)
+    starts((0, 3), (1, 3))
+    chain(1, 0, 1)
+    chain(2, 0, 0)
+    give(7)
+    give_on(6)
+    chain(1, 1, 1)
+    expr_grad(4)
+    starts((0, 4), (2, 2), (1, 4))
+    push = totals(mass, d)
+    give_on(7)
+    chain(2, 0, 1)
+    chain(1, 0, 2)
+    expr_grad(5)
+    starts((0, 5), (2, 3), (1, 5))
+    finish(0)
+    chain(1, 1, 2)
+    expr_grad(6)
+    starts((0, 6), (2, 4))
+    chain(1, 0, 3)
+    mass_columns()
+    expr_grad(7)
+    starts((0, 7), (1, 6), (1, 7))
+    finish(1)
+    chain(2, 0, 2)
+    chain(1, 1, 3)
+    weight_grad(0)
+    chain(1, 0, 4)
+    chain(2, 0, 3)
+    weight_grad(1)
+    give_back(0)
+    finish(2)
+    chain(1, 1, 4)
+    weight_grad(2)
+    give_back(1)
+    chain(2, 0, 4)
+    chain(1, 0, 5)
+    weight_grad(3)
+    give_back(2)
+    finish(3)
+    give_back(3)
+    filter_along()
+    starts((2, 5), (2, 6), (2, 7))
+    chain(1, 1, 5)
+    chain(2, 0, 5)
+    take(0, 0, True)
+    for p in range(1, nz):
+        take(0, p)
+    chain(1, 0, 6)
+    sent_first()
+    finish(4)
+    chain(1, 0, 7)
+    for k in (1, 2, 3):
+        take(k, 0)
+    sent_along()
+    chain(2, 0, 6)
+    chain(1, 1, 6)
+    for k in (1, 2, 3):
+        take(k, 1)
+    chain(1, 1, 7)
+    sent_back()
+    chain(2, 0, 7)
+    for k in (1, 2, 3):
+        take(k, 2)
+    finish(5)
+    for r in range(1, nz):
+        zcopy_wait(frecv, r, fz_s, fz_r)
+    ftotal = frecv[0]
+    for p in range(1, nz):
+        ftotal = ftotal + frecv[p]
+    pair_s[2, 0:1, 0:cd] = ftotal
+    pair(2).start()
+    for k in (1, 2, 3):
+        take(k, 3)
+    tot_o[...] = jnp.broadcast_to(jnp.sum(rowsum[...], axis=1, keepdims=True), (rows, 128))
+    sent_last()
+    finish(6)
+    pair(1).wait_recv()
+    pair(2).wait_recv()
+    my_gate = jax.nn.sigmoid(filt[...])
+    fsum = ftotal + pair_r[2, 0:1, 0:cd] + push
+    for h in range(cd // 128):
+        g = my_gate[h : h + 1, :]
+        last_o[h : h + 1, :] = fsum[:, h * 128 : (h + 1) * 128] * g * (1.0 - g)
+    last_o[cd // 128 : cd // 128 + 1, :] = 0.5 * (pair_s[1, 0:1, 0:128] + pair_r[1, 0:1, 0:128])
+    finish(7)
+    sent_sums()
+
+
+def finish_kernel(probs, gp, tot, ge, last, gl_o, ge_o, loss_o, gf_o, gl, loss, out_s):
+    f32 = jnp.float32
+    parts = 4
+    cc = probs.shape[1] // parts
+    copies = []
+
+    def send(src, dst):
+        copies.append(pltpu.make_async_copy(src, dst, out_s.at[len(copies)]))
+        copies[-1].start()
+
+    send(ge, ge_o)
+    n = gf_o.shape[0]
+    loss[...] = last[n : n + 1, 0:1]
+    send(last.at[pl.ds(0, n)], gf_o)
+    send(loss, loss_o)
+    for i in range(parts):
+        for c in range(i * cc, (i + 1) * cc, 128):
+            at = slice(c, c + 128)
+            gl[:, at] = probs[:, at] * (gp[:, at].astype(f32) - tot[...])
+        at = pl.ds(i * cc, cc)
+        send(gl.at[:, at], gl_o.at[:, at])
+    for c in copies:
+        c.wait()
+
+
+def grouped(logits, filt, expr, target, gene_mask, density):
+    f32, bf16, i32 = jnp.float32, jnp.bfloat16, jnp.int32
+    nspot = lax.axis_size("spot")
+    rows, cells = logits.shape
+    cd, genes = expr.shape
+    nz = nspot // GROUP
+    n = genes // PIECE
+    grp = GROUP * rows
+    mine = cells // GROUP
+    spots = 2 * rows
+
+    def vmem(*shape, dtype=f32):
+        return pltpu.VMEM(shape, dtype)
+
+    def dma(*shape):
+        return pltpu.SemaphoreType.DMA(shape)
+
+    def low(*shape):
+        return pltpu.VMEM(shape, bf16)
+
+    buffers = [
+        low(rows, cells), vmem(cd // 128, 128), vmem(*gene_mask.shape, dtype=i32), vmem(spots // 128, 128, dtype=i32),
+        low(GROUP, rows, mine), low(2 * grp, mine), low(2 * grp, mine), low(mine, 2 * grp),
+        low(n // 2, mine, 2 * PIECE), low(spots, genes), vmem(8, mine), vmem(nz, 8, 128), vmem(spots, genes),
+        vmem(2 * grp, PIECE),
+        low(n, 2 * rows, PIECE), low(n, 2 * rows, PIECE), low(n, 2 * rows, PIECE), low(n, 2 * rows, PIECE),
+        low(n, rows, PIECE), low(n, rows, PIECE), low(n, rows, PIECE), low(n, rows, PIECE),
+        vmem(n, rows, PIECE), vmem(n, rows, PIECE), vmem(GROUP, 8, 128), vmem(GROUP, 8, 128),
+        vmem(3, 1, genes), vmem(GROUP, 3, 1, genes), vmem(3, spots, PIECE), vmem(3, 1, spots), vmem(3, 1, spots),
+        low(n // 2, 2 * grp, 2 * PIECE), vmem(nz, cd, genes),
+        low(nz, n, cd, PIECE), low(nz, n, cd, PIECE), low(nz, n, cd, PIECE),
+        vmem(nz, grp, cd), vmem(nz, grp, cd), vmem(nz, grp, cd), low(nz, grp, cd), low(GROUP, nz, rows, cd),
+        vmem(rows, 128), vmem(8, 128), vmem(GROUP, 8, 128), vmem(nz, 8, 128), vmem(8, 128), vmem(GROUP, 8, 128),
+        vmem(grp, 128), vmem(nz, 1, cd), vmem(nz, 1, cd), vmem(3, 8, spots), vmem(3, 8, spots),
+    ]
+    sems = [
+        pltpu.SemaphoreType.REGULAR, dma(4 + n // 2 + 2), dma(2, nz), dma(nz), dma(2, nz, n), dma(nz, n),
+        dma(4), dma(4), dma(4), dma(4), dma(5), dma(5),
+        dma(2, n), dma(2, n), dma(2, n), dma(2, n), dma(n), dma(n), dma(n), dma(n),
+        dma(4), dma(4), dma(8), dma(8), dma(6, n), dma(6, n),
+        dma(nz, n), dma(nz, n), dma(nz, n), dma(nz, n), dma(nz), dma(nz), dma(4, nz), dma(4, nz),
+        dma(4), dma(4), dma(nz), dma(nz), dma(4), dma(4), dma(nz), dma(nz),
+    ]
+    v, a = pl.BlockSpec(memory_space=pltpu.VMEM), pl.BlockSpec(memory_space=pl.ANY)
+    shape = jax.ShapeDtypeStruct
+    fparts = (cd // 128, 128)
+    given = (logits, filt.reshape(-1, 128), expr, target, gene_mask, density.reshape(-1, 128))
+    probs, gp, tot, last, grad_expr = pl.pallas_call(
+        functools.partial(group_kernel, nspot),
+        out_shape=[vmem(rows, cells), low(rows, cells), vmem(rows, 128), vmem(8, 128), vmem(cd, genes)],
+        in_specs=[a] * 6,
+        out_specs=[v] * 5,
+        scratch_shapes=buffers + sems,
+        compiler_params=pltpu.CompilerParams(
+            collective_id=0, has_side_effects=True, vmem_limit_bytes=VMEM_BYTES
+        ),
+        name="group_step",
+    )(*(pltpu.with_memory_space_constraint(g, pltpu.HBM) for g in given))
+    grad_logits, grad_expr, loss, grad_filt = pl.pallas_call(
+        finish_kernel,
+        out_shape=[shape((rows, cells), f32), shape((cd, genes), f32), shape((1, 1), f32), shape(fparts, f32)],
+        in_specs=[v] * 5,
+        out_specs=[a] * 4,
+        scratch_shapes=[vmem(rows, cells), vmem(1, 1), dma(7)],
+        compiler_params=pltpu.CompilerParams(vmem_limit_bytes=LAST_BYTES),
+        name="finish_step",
+    )(probs, gp, tot, grad_expr, last)
+    return (loss.reshape(()), grad_logits, grad_filt.reshape(-1), grad_expr)
+
+
+def fits(logits, filt, expr):
+    nspot = lax.axis_size("spot")
+    rows, cells = logits.shape
+    sizes = (rows, cells, filt.shape[0], expr.shape[1])
+    return (
+        nspot == GROUP * SLIDES and lax.axis_size("gene") == 2 and sizes == (128, 4096, 256, 1024)
+    )
+
+
+def per_device(logits, filt, expr, target, gene_mask, density):
+    plan = grouped if fits(logits, filt, expr) else streamed
+    return plan(logits, filt, expr, target, gene_mask, density)
+
+
 def solution(mesh):
     in_specs = (
         P(("spot", "gene"), None),

time: 750 us -> 104 us (0.14)
  blocking collectives: 382 us -> 0 us
  waiting for transfers between devices: 295 us -> 0 us
  Pallas kernels: 0 us -> 103 us
  matrix products: 28 us -> 0 us
  other arithmetic: 20.3 us -> 0 us
  between operations: 20.3 us -> 0.8 us
    reduce_scatter x2 -> x0, waiting for transfers between devices: 214 us -> none  [the longest x1 214 us: per_device(): lax.psum_scatter(partial_pred.reshape(nspot, owned, half), 'spot', scatte...]
    all_to_all x2 -> x0, blocking collectives: 132 us -> none  [the longest x1 97.5 us: per_device(): lax.all_to_all(terms, 'spot', split_axis=0, concat_axis=3, tiled=True)]
    psum x5 -> x0, blocking collectives: 125 us -> none  [the longest x2 118 us: per_device(): lax.psum((slide_moments(onehot, pred, truth), jnp.sum(mass), gate_part, j...]
    pallas_call x0 -> x2, Pallas kernels: none -> 103 us  [the longest x1 102 us: grouped(): pl.pallas_call(functools.partial(group_kernel, nspot), out_shape=[vmem(ro...]
    unnamed x1 -> x0, blocking collectives: 88.4 us -> none
    all_gather x2 -> x0, waiting for transfers between devices: 81.7 us -> none  [the longest x1 73.4 us: per_device(): lax.all_gather(grad_pred.astype(bf16).reshape(1, owned, half), 'spot', ax...]
    all_gather x1 -> x0, blocking collectives: 35.7 us -> none  [per_device(): lax.all_gather(grad_mass.astype(bf16).reshape(1, owned), 'spot', axis=0,...]
    dot_general x8 -> x0, matrix products: 28 us -> none  [the longest x1 9.65 us: per_device(): partial_pred = jnp.dot(weighted, expr, preferred_element_type=f32)]
  transfers between devices with their start and end apart: 4 -> 0, of which waited for: 3 -> 0; matrix products, arithmetic and copies ran while one was open for 2% -> 0% of each run, Pallas kernels for 0% -> 0%
where the time goes in v4:
time: 104 us
  Pallas kernels  103 us (99%)
    pallas_call x1, Pallas kernels, grouped(): pl.pallas_call(functools.partial(group_kernel, nspot), out_shape=[vmem(ro...  102 us

profile of v4, /device:TPU:0, one launch (start us, length us, event | category | flops | bytes accessed | tf_op | source)
XLA Modules:
  0.0 104.1 jit_solution(12590548451467947044)
XLA Ops:
  0.6 101.6 %group_step.1 = (f32[128,4096]{1,0:T(8,128)S(1)}, bf16[128,4096]{1,0:T(8,128)(2,1)S(1)}, f32[128,128]{1,0:T(8,128)S(1)}, f32[8,128]{1,0:T(8,128)S(1)}, f32[256,1024]{1,0:T(8,128)S(1)}) custom-call(bf16[128,4096]{1,0:T(8,128)(2,1)} %logits_h.1, f32[2,128]{1,0:T(2,128)} %bitcast.4, bf16[256,1024]{1,0:T(8,128)(2,1)} %expr.1, bf16[256,1024]{1,0:T(8,128)(2,1)} %target.1, ...), custom_call_target="tpu_custom_call" | custom-call | tf_op jit(solution)/shard_map/group_step/pallas_call | solution.py:1053
  102.2 1.7 %finish_step.1 = (f32[128,4096]{1,0:T(8,128)}, f32[256,1024]{1,0:T(8,128)}, f32[1,1]{1,0:T(1,128)}, f32[2,128]{1,0:T(2,128)}) custom-call(f32[128,4096]{1,0:T(8,128)S(1)} %get-tuple-element.13.probs, bf16[128,4096]{1,0:T(8,128)(2,1)S(1)} %get-tuple-element.14.gp, f32[128,128]{1,0:T(8,128)S(1)} %get-tuple-element.15.tot, ...), custom_call_target="tpu_custom_call" | custom-call | tf_op jit(solution)/shard_map/finish_step/pallas_call | solution.py:1064

commit v5 on v4

--- a/solution.py
+++ b/solution.py
@@ -181,11 +181,11 @@
     nspot, logits_h, filt_h, expr, target, mask_h, dens_h,
     probs, gpb, tot_o, last_o, ge_o,
     logits, filt, mask, dens, rawq, wraw, wg, wt, ebuf, tbuf, gcol, small, pfin, ahead,
-    psx, prx, psy, pry, ps2x, pr2x, ps2y, pr2y, hx, hy, massp, massr, statg, statr, acc, spots, spotr,
+    psx, prx, psy, pry, ps2x, pr2x, ps2y, pr2y, hx, hy, massp, massr, statg, statr, acc, spots, spotr, tlead, plead,
     dpa, grad, dsend, dright, dleft, dwo, dws, dwr, gps, gpr, rowsum, tile_s, tile_r, tz, gms, gmr, gmcol,
     fsend, frecv, pair_s, pair_r,
     hello, lc, zs_s, zs_r, ez_s, ez_r, w_s, w_r, wd_s, wd_r, pr_s, pr_r,
-    px_s, px_r, py_s, py_r, p2x_s, p2x_r, p2y_s, p2y_r, ms_s, ms_r, st_s, st_r, ag_s, ag_r,
+    px_s, px_r, py_s, py_r, p2x_s, p2x_r, p2y_s, p2y_r, ms_s, ms_r, st_s, st_r, ld_s, ld_r, sp_s, sp_r, ag_s, ag_r,
     dr_s, dr_r, dl_s, dl_r, dw_s, dw_r, gp_s, gp_r, tl_s, tl_r, tz_s, tz_r, gm_s, gm_r, fz_s, fz_r,
 ):
     f32, bf16 = jnp.float32, jnp.bfloat16
@@ -335,6 +335,22 @@
     def pair(i):
         return remote(pair_s.at[i], pair_r.at[i], pr_s.at[i], pr_r.at[i], here)
 
+    def lead_copy(buf, i, k, h):
+        r = at_k(0, h)
+        return remote(buf.at[r], buf.at[at_k(k, h)], ld_s.at[i, k, h], ld_r.at[i, k, h], chip[k])
+
+    def lead(buf, i, values):
+        for h in range(2):
+            buf[at_k(0, h), :] = values[h * rows : (h + 1) * rows]
+        for k in (3, 1, 2):
+            for h in range(2):
+                lead_copy(buf, i, k, h).start()
+
+    def lead_wait(buf, i):
+        for k in (1, 2, 3):
+            for h in range(2):
+                lead_copy(buf, i, k, h).wait_recv()
+
     wcopy(1).start()
     wcopy(2).start()
     pl.semaphore_signal(hello, inc=1, device_id=chip[1], device_id_type=MESH)
@@ -390,11 +406,12 @@
     far = (1 - z // (nz // 2)) * (nz - 1)
     near = pl.ds(pl.multiple_of(z // (nz // 2) * cd, cd), mine - cd)
 
-    def project_ahead(g):
-        ahead[...] = jnp.dot(wg[:, near], piece_of(g, near), preferred_element_type=f32)
+    def project_ahead():
+        ahead[...] = jnp.dot(wg[:, near], ebuf[np_ // 2 - 1, near, :], preferred_element_type=f32)
 
     def project_last(g):
-        share(g, ahead[...] + jnp.dot(wg[:, seg(far)], piece_of(g, seg(far)), preferred_element_type=f32))
+        v = jnp.dot(wg[:, seg(far)], piece_of(g, seg(far)), preferred_element_type=f32)
+        share(g, ahead[:, g % 2 * PIECE : (g % 2 + 1) * PIECE] + v)
 
     def share(g, v):
         def part(k, h):
@@ -492,10 +509,10 @@
         along(1, s)
         along(2, s - 1)
         own(s + 2)
-        if s == np_ + 1:
-            relay(s - 3)
+        if s == np_:
+            project_ahead()
         along(3, s - 2)
-        if s < np_ + 1:
+        if s < np_:
             project(s - 2)
         else:
             project_last(s - 2)
@@ -507,12 +524,13 @@
         if s == 6:
             turned(3, 0)
             turned(3, 1)
-        if s < np_ + 1:
-            relay(s - 3)
-        if s == np_:
-            project_ahead(np_ - 1)
+        relay(s - 3)
+        if s == 4:
+            lead(tlead, 0, tbuf[:, 0:PIECE])
         if s > 4:
             whole(s - 5)
+        if s == 5:
+            lead(plead, 1, pfin[:, 0:PIECE].astype(bf16))
     whole(np_ - 3)
     for k in (3, 1, 2):
         stat(k, 0).start()
@@ -527,8 +545,14 @@
 
     for i in range(3):
         spots[i] = jnp.sum(jnp.transpose(acc[i]), axis=0, keepdims=True)
-    spot_copy = remote(spots, spotr, pr_s.at[4], pr_r.at[4], here)
-    spot_copy.start()
+    def spot_copy(k, h):
+        i = 2 * k + h
+        dev = (nbr[k], sib) if h else chip[k]
+        return remote(spots, spotr.at[h, k], sp_s.at[i], sp_r.at[i], dev)
+
+    others = [(k, h) for k in (3, 1, 2, 0) for h in (1, 0) if k or h]
+    for k, h in others:
+        spot_copy(k, h).start()
 
     def slide_sums(n):
         for k in (1, 2, 3):
@@ -548,15 +572,24 @@
         )
 
     coefs = [slide_sums(0), None]
-    spot_copy.wait_recv()
-    spot_pp, spot_dot, spot_tt = (
-        spots[i] + jnp.concatenate([spotr[i, :, rows : 2 * rows], spotr[i, :, 0:rows]], axis=1)
-        for i in range(3)
-    )
-    spot_a = lax.rsqrt(spot_pp + eps_norm)
-    spot_b = lax.rsqrt(spot_tt + eps_norm)
-    col_t = column(-(spot_a * spot_b) / spots_all, 2 * rows)
-    col_p = column(spot_dot * spot_a**3 * spot_b / spots_all, 2 * rows)
+
+    def spot_coefs(k):
+        if k:
+            spot_copy(k, 0).wait_recv()
+        spot_copy(k, 1).wait_recv()
+        pp, dot, tt = (
+            (spotr[0, k, i] if k else spots[i])
+            + jnp.concatenate([spotr[1, k, i, :, rows : 2 * rows], spotr[1, k, i, :, 0:rows]], axis=1)
+            for i in range(3)
+        )
+        a, b = lax.rsqrt(pp + eps_norm), lax.rsqrt(tt + eps_norm)
+        return (
+            column(-(a * b) / spots_all, 2 * rows),
+            column(dot * a**3 * b / spots_all, 2 * rows),
+            dot * a * b,
+        )
+
+    col_t, col_p, cos_spot = spot_coefs(0)
 
     def agcopy(i, g):
         src, dst, to = (
@@ -579,6 +612,17 @@
         for i in range(4):
             agcopy(i, g).start()
 
+    def lead_grad():
+        lead_wait(tlead, 0)
+        lead_wait(plead, 1)
+        c_t, c_p = (v[:, 0:PIECE] for v in coefs[0][0:2])
+        for k in (0, 1, 2, 3):
+            t, p = (col_t, col_p) if k == 0 else spot_coefs(k)[0:2]
+            for h in range(2):
+                r, m = at_k(k, h), slice(h * rows, (h + 1) * rows)
+                d = (c_t + t[m]) * tlead[r, :].astype(f32) + (c_p + p[m]) * plead[r, :].astype(f32)
+                dpa[0, r, 0:PIECE] = d.astype(bf16)
+
     def give_on(g):
         agcopy(0, g).wait_recv()
         agcopy(4, g).start()
@@ -591,8 +635,6 @@
         return remote(dsend.at[p, g], dleft.at[p, g], dl_s.at[p, g], dl_r.at[p, g], beside[1])
 
     def expr_grad_first():
-        for i in (1, 3, 4, 5):
-            agcopy(i, 0).wait_recv()
         up = z // (nz // 2)
 
         @pl.loop(0, nz)
@@ -700,7 +742,7 @@
     def tile_start():
         mass, d = chip_masses(), own_dens()
         gene = fold(coefs[0][2]) + fold(coefs[1][2])
-        cos = fold(spot_dot * spot_a * spot_b)
+        cos = fold(cos_spot)
         tile_s[0:1] = -2.0 / GROUP * gene - cos / spots_all
         tile_s[1:2] = d[0:1] + d[1:2]
         f = jax.nn.sigmoid(filt[...])
@@ -809,7 +851,12 @@
         for k in range(GROUP):
             wsib(k).wait_send()
         pair(0).wait_send()
-        spot_copy.wait_send()
+        for k, h in others:
+            spot_copy(k, h).wait_send()
+        for k in (1, 2, 3):
+            for h in range(2):
+                lead_copy(tlead, 0, k, h).wait_send()
+                lead_copy(plead, 1, k, h).wait_send()
 
         @pl.loop(0, np_)
         def _(g):
@@ -835,7 +882,7 @@
                     zsend(1, p, g).wait_send()
 
     def sent_back():
-        for g in range(np_):
+        for g in range(1, np_):
             for i in range(6):
                 agcopy(i, g).wait_send()
 
@@ -866,15 +913,14 @@
                 for g in range(np_):
                     dcopy(1, p, g).wait_send()
 
-    give(0)
     give(1)
+    give(2)
     coefs[1] = slide_sums(1)
     mass, d = tile_start()
-    give_on(0)
-    give(2)
+    lead_grad()
+    expr_grad_first()
     give_on(1)
     give(3)
-    expr_grad_first()
     give_on(2)
     give(4)
     tile_along()
@@ -897,22 +943,22 @@
     give_on(6)
     chain(1, 1, 1)
     expr_grad(4)
-    starts((0, 4), (2, 2), (1, 4))
+    starts((0, 4), (1, 4), (2, 2))
     push = totals(mass, d)
     give_on(7)
     chain(2, 0, 1)
     chain(1, 0, 2)
     expr_grad(5)
-    starts((0, 5), (2, 3), (1, 5))
+    starts((0, 5), (1, 5))
     finish(0)
     chain(1, 1, 2)
     expr_grad(6)
-    starts((0, 6), (2, 4))
+    starts((0, 6), (1, 6))
     chain(1, 0, 3)
+    finish(1)
     mass_columns()
     expr_grad(7)
-    starts((0, 7), (1, 6), (1, 7))
-    finish(1)
+    starts((0, 7), (2, 3), (1, 7))
     chain(2, 0, 2)
     chain(1, 1, 3)
     weight_grad(0)
@@ -920,37 +966,37 @@
     chain(2, 0, 3)
     weight_grad(1)
     give_back(0)
+    chain(1, 1, 4)
     finish(2)
-    chain(1, 1, 4)
     weight_grad(2)
     give_back(1)
     chain(2, 0, 4)
     chain(1, 0, 5)
     weight_grad(3)
     give_back(2)
-    finish(3)
+    chain(1, 1, 5)
     give_back(3)
     filter_along()
-    starts((2, 5), (2, 6), (2, 7))
-    chain(1, 1, 5)
-    chain(2, 0, 5)
+    starts((2, 4), (2, 5), (2, 6), (2, 7))
+    chain(1, 0, 6)
     take(0, 0, True)
     for p in range(1, nz):
         take(0, p)
-    chain(1, 0, 6)
+    chain(2, 0, 5)
+    chain(1, 1, 6)
     sent_first()
-    finish(4)
     chain(1, 0, 7)
     for k in (1, 2, 3):
         take(k, 0)
     sent_along()
     chain(2, 0, 6)
-    chain(1, 1, 6)
+    finish(3)
     for k in (1, 2, 3):
         take(k, 1)
     chain(1, 1, 7)
     sent_back()
     chain(2, 0, 7)
+    finish(4)
     for k in (1, 2, 3):
         take(k, 2)
     finish(5)
@@ -1027,11 +1073,11 @@
         low(rows, cells), vmem(cd // 128, 128), vmem(*gene_mask.shape, dtype=i32), vmem(spots // 128, 128, dtype=i32),
         low(GROUP, rows, mine), low(2 * grp, mine), low(2 * grp, mine), low(mine, 2 * grp),
         low(n // 2, mine, 2 * PIECE), low(spots, genes), vmem(8, mine), vmem(nz, 8, 128), vmem(spots, genes),
-        vmem(2 * grp, PIECE),
+        vmem(2 * grp, 2 * PIECE),
         low(n, 2 * rows, PIECE), low(n, 2 * rows, PIECE), low(n, 2 * rows, PIECE), low(n, 2 * rows, PIECE),
         low(n, rows, PIECE), low(n, rows, PIECE), low(n, rows, PIECE), low(n, rows, PIECE),
         vmem(n, rows, PIECE), vmem(n, rows, PIECE), vmem(GROUP, 8, 128), vmem(GROUP, 8, 128),
-        vmem(3, 1, genes), vmem(GROUP, 3, 1, genes), vmem(3, spots, PIECE), vmem(3, 1, spots), vmem(3, 1, spots),
+        vmem(3, 1, genes), vmem(GROUP, 3, 1, genes), vmem(3, spots, PIECE), vmem(3, 1, spots), vmem(2, GROUP, 3, 1, spots), low(2 * grp, PIECE), low(2 * grp, PIECE),
         low(n // 2, 2 * grp, 2 * PIECE), vmem(nz, cd, genes),
         low(nz, n, cd, PIECE), low(nz, n, cd, PIECE), low(nz, n, cd, PIECE),
         vmem(nz, grp, cd), vmem(nz, grp, cd), vmem(nz, grp, cd), low(nz, grp, cd), low(GROUP, nz, rows, cd),
@@ -1040,9 +1086,9 @@
     ]
     sems = [
         pltpu.SemaphoreType.REGULAR, dma(4 + n // 2 + 2), dma(2, nz), dma(nz), dma(2, nz, n), dma(nz, n),
-        dma(4), dma(4), dma(4), dma(4), dma(5), dma(5),
+        dma(4), dma(4), dma(4), dma(4), dma(3), dma(3),
         dma(2, n), dma(2, n), dma(2, n), dma(2, n), dma(n), dma(n), dma(n), dma(n),
-        dma(4), dma(4), dma(8), dma(8), dma(6, n), dma(6, n),
+        dma(4), dma(4), dma(8), dma(8), dma(2, 4, 2), dma(2, 4, 2), dma(8), dma(8), dma(6, n), dma(6, n),
         dma(nz, n), dma(nz, n), dma(nz, n), dma(nz, n), dma(nz), dma(nz), dma(4, nz), dma(4, nz),
         dma(4), dma(4), dma(nz), dma(nz), dma(4), dma(4), dma(nz), dma(nz),
     ]

time: 104 us -> 98.6 us (0.948)
  Pallas kernels: 103 us -> 97.7 us
    pallas_call x1, Pallas kernels: 102 us -> 96 us  [grouped(): pl.pallas_call(functools.partial(group_kernel, nspot), out_shape=[vmem(ro...]
where the time goes in v5:
time: 98.6 us; the launch traced here: 98.5 us
  Pallas kernels  97.7 us (99%)
    pallas_call x1, Pallas kernels, grouped(): pl.pallas_call(functools.partial(group_kernel, nspot), out_shape=[vmem(ro...  96 us

profile of v5, /device:TPU:0, one launch (start us, length us, event | category | flops | bytes accessed | tf_op | source)
XLA Modules:
  0.0 98.5 jit_solution(18066913770314173454)
XLA Ops:
  0.6 96.0 %group_step.1 = (f32[128,4096]{1,0:T(8,128)S(1)}, bf16[128,4096]{1,0:T(8,128)(2,1)S(1)}, f32[128,128]{1,0:T(8,128)S(1)}, f32[8,128]{1,0:T(8,128)S(1)}, f32[256,1024]{1,0:T(8,128)S(1)}) custom-call(bf16[128,4096]{1,0:T(8,128)(2,1)} %logits_h.1, f32[2,128]{1,0:T(2,128)} %bitcast.4, bf16[256,1024]{1,0:T(8,128)(2,1)} %expr.1, bf16[256,1024]{1,0:T(8,128)(2,1)} %target.1, ...), custom_call_target="tpu_custom_call" | custom-call | tf_op jit(solution)/shard_map/group_step/pallas_call | solution.py:1099
  96.6 1.7 %finish_step.1 = (f32[128,4096]{1,0:T(8,128)}, f32[256,1024]{1,0:T(8,128)}, f32[1,1]{1,0:T(1,128)}, f32[2,128]{1,0:T(2,128)}) custom-call(f32[128,4096]{1,0:T(8,128)S(1)} %get-tuple-element.13.probs, bf16[128,4096]{1,0:T(8,128)(2,1)S(1)} %get-tuple-element.14.gp, f32[128,128]{1,0:T(8,128)S(1)} %get-tuple-element.15.tot, ...), custom_call_target="tpu_custom_call" | custom-call | tf_op jit(solution)/shard_map/finish_step/pallas_call | solution.py:1110

commit v6 on v5

--- a/solution.py
+++ b/solution.py
@@ -258,6 +258,56 @@
     ]
     for c in loads:
         c.start()
+    for c in loads[1 : 4 + np_ // 2]:
+        c.wait()
+    small[pl.ds(z, 1), 0 : cd // 128, :] = filt[...][None]
+    pl.semaphore_wait(barrier, 3 + has_right.astype(jnp.int32) + has_left.astype(jnp.int32))
+
+    def zsmall(way, p):
+        return remote(small.at[p], small.at[p], zs_s.at[way, p], zs_r.at[p], beside[way])
+
+    def zsend(way, p, g):
+        u = half_of(ebuf, seg(p), g)
+        return remote(u, u, ez_s.at[way, p, g], ez_r.at[p, g], beside[way])
+
+    def both(make):
+        @pl.when(has_right)
+        def _():
+            make(0).start()
+
+        @pl.when(has_left)
+        def _():
+            make(1).start()
+
+    def hop(s, make):
+        @pl.when(z >= s)
+        def _():
+            make(0, z - s).wait_recv()
+
+            @pl.when(has_right)
+            def _():
+                make(0, z - s).start()
+
+        @pl.when(z + s <= nz - 1)
+        def _():
+            make(1, z + s).wait_recv()
+
+            @pl.when(has_left)
+            def _():
+                make(1, z + s).start()
+
+    def own(g):
+        if g < np_:
+            both(lambda way: zsend(way, z, g))
+
+    def along(s, g):
+        if 0 <= g < np_:
+            hop(s, lambda way, p: zsend(way, p, g))
+
+    both(lambda way: zsmall(way, z))
+    own(0)
+    own(1)
+
     loads[0].wait()
 
     step = 32
@@ -273,58 +323,11 @@
             c = o // GROUP * cd
             rawq[o % GROUP, at, c : c + cd] = p[:, o * cd : (o + 1) * cd].astype(bf16)
 
-    for c in loads[1:]:
+    for c in loads[4 + np_ // 2 :]:
         c.wait()
-    small[pl.ds(z, 1), 0 : cd // 128, :] = filt[...][None]
     maskf = mask[pl.ds(z, 1), :].astype(f32)
     kept_mine = jnp.sum(maskf)
     pair_s[0] = jnp.full((8, 2 * rows), kept_mine)
-    pl.semaphore_wait(barrier, 3 + has_right.astype(jnp.int32) + has_left.astype(jnp.int32))
-
-    def zsmall(way, p):
-        return remote(small.at[p], small.at[p], zs_s.at[way, p], zs_r.at[p], beside[way])
-
-    def zsend(way, p, g):
-        u = half_of(ebuf, seg(p), g)
-        return remote(u, u, ez_s.at[way, p, g], ez_r.at[p, g], beside[way])
-
-    def both(make):
-        @pl.when(has_right)
-        def _():
-            make(0).start()
-
-        @pl.when(has_left)
-        def _():
-            make(1).start()
-
-    def hop(s, make):
-        @pl.when(z >= s)
-        def _():
-            make(0, z - s).wait_recv()
-
-            @pl.when(has_right)
-            def _():
-                make(0, z - s).start()
-
-        @pl.when(z + s <= nz - 1)
-        def _():
-            make(1, z + s).wait_recv()
-
-            @pl.when(has_left)
-            def _():
-                make(1, z + s).start()
-
-    def own(g):
-        if g < np_:
-            both(lambda way: zsend(way, z, g))
-
-    def along(s, g):
-        if 0 <= g < np_:
-            hop(s, lambda way, p: zsend(way, p, g))
-
-    both(lambda way: zsmall(way, z))
-    own(0)
-    own(1)
 
     def wcopy(k):
         return remote(rawq.at[nq[k]], wraw.at[at_k(k)], w_s.at[k], w_r.at[k], chip[k])
@@ -936,69 +939,69 @@
     give(6)
     give_on(5)
     expr_grad(3)
-    starts((0, 3), (1, 3))
+    starts((0, 3))
     chain(1, 0, 1)
     chain(2, 0, 0)
     give(7)
     give_on(6)
     chain(1, 1, 1)
     expr_grad(4)
-    starts((0, 4), (1, 4), (2, 2))
+    starts((0, 4), (1, 3))
     push = totals(mass, d)
     give_on(7)
     chain(2, 0, 1)
     chain(1, 0, 2)
     expr_grad(5)
-    starts((0, 5), (1, 5))
+    starts((0, 5), (1, 4))
     finish(0)
     chain(1, 1, 2)
     expr_grad(6)
-    starts((0, 6), (1, 6))
+    starts((0, 6))
     chain(1, 0, 3)
     finish(1)
     mass_columns()
+    chain(2, 0, 2)
     expr_grad(7)
-    starts((0, 7), (2, 3), (1, 7))
-    chain(2, 0, 2)
+    starts((0, 7), (1, 5), (2, 2), (1, 6), (2, 3), (1, 7))
+    chain(1, 0, 4)
     chain(1, 1, 3)
     weight_grad(0)
-    chain(1, 0, 4)
     chain(2, 0, 3)
+    chain(1, 0, 5)
     weight_grad(1)
+    chain(2, 0, 4)
     give_back(0)
     chain(1, 1, 4)
-    finish(2)
     weight_grad(2)
+    chain(1, 0, 6)
     give_back(1)
-    chain(2, 0, 4)
-    chain(1, 0, 5)
+    chain(2, 0, 5)
     weight_grad(3)
+    chain(1, 0, 7)
     give_back(2)
     chain(1, 1, 5)
     give_back(3)
     filter_along()
     starts((2, 4), (2, 5), (2, 6), (2, 7))
-    chain(1, 0, 6)
+    chain(2, 0, 6)
+    finish(2)
     take(0, 0, True)
     for p in range(1, nz):
         take(0, p)
-    chain(2, 0, 5)
+    chain(2, 0, 7)
     chain(1, 1, 6)
-    sent_first()
-    chain(1, 0, 7)
     for k in (1, 2, 3):
         take(k, 0)
-    sent_along()
-    chain(2, 0, 6)
     finish(3)
+    sent_first()
+    chain(1, 1, 7)
     for k in (1, 2, 3):
         take(k, 1)
-    chain(1, 1, 7)
-    sent_back()
-    chain(2, 0, 7)
+    sent_along()
     finish(4)
     for k in (1, 2, 3):
         take(k, 2)
+    sent_back()
     finish(5)
     for r in range(1, nz):
         zcopy_wait(frecv, r, fz_s, fz_r)

time: 98.6 us -> 96.2 us (0.976)
  Pallas kernels: 97.7 us -> 95.2 us
    pallas_call x1, Pallas kernels: 96 us -> 93.5 us  [grouped(): pl.pallas_call(functools.partial(group_kernel, nspot), out_shape=[vmem(ro...]
where the time goes in v6:
time: 96.2 us; the launch traced here: 96 us
  Pallas kernels  95.2 us (99%)
    pallas_call x1, Pallas kernels, grouped(): pl.pallas_call(functools.partial(group_kernel, nspot), out_shape=[vmem(ro...  93.5 us

profile of v6, /device:TPU:0, one launch (start us, length us, event | category | flops | bytes accessed | tf_op | source)
XLA Modules:
  0.0 96.0 jit_solution(9120758574649964284)
XLA Ops:
  0.6 93.5 %group_step.1 = (f32[128,4096]{1,0:T(8,128)S(1)}, bf16[128,4096]{1,0:T(8,128)(2,1)S(1)}, f32[128,128]{1,0:T(8,128)S(1)}, f32[8,128]{1,0:T(8,128)S(1)}, f32[256,1024]{1,0:T(8,128)S(1)}) custom-call(bf16[128,4096]{1,0:T(8,128)(2,1)} %logits_h.1, f32[2,128]{1,0:T(2,128)} %bitcast.4, bf16[256,1024]{1,0:T(8,128)(2,1)} %expr.1, bf16[256,1024]{1,0:T(8,128)(2,1)} %target.1, ...), custom_call_target="tpu_custom_call" | custom-call | tf_op jit(solution)/shard_map/group_step/pallas_call | solution.py:1102
  94.1 1.7 %finish_step.1 = (f32[128,4096]{1,0:T(8,128)}, f32[256,1024]{1,0:T(8,128)}, f32[1,1]{1,0:T(1,128)}, f32[2,128]{1,0:T(2,128)}) custom-call(f32[128,4096]{1,0:T(8,128)S(1)} %get-tuple-element.13.probs, bf16[128,4096]{1,0:T(8,128)(2,1)S(1)} %get-tuple-element.14.gp, f32[128,128]{1,0:T(8,128)S(1)} %get-tuple-element.15.tot, ...), custom_call_target="tpu_custom_call" | custom-call | tf_op jit(solution)/shard_map/finish_step/pallas_call | solution.py:1113

commit v7 on v6

--- a/solution.py
+++ b/solution.py
@@ -181,7 +181,7 @@
     nspot, logits_h, filt_h, expr, target, mask_h, dens_h,
     probs, gpb, tot_o, last_o, ge_o,
     logits, filt, mask, dens, rawq, wraw, wg, wt, ebuf, tbuf, gcol, small, pfin, ahead,
-    psx, prx, psy, pry, ps2x, pr2x, ps2y, pr2y, hx, hy, massp, massr, statg, statr, acc, spots, spotr, tlead, plead,
+    psx, prx, psy, pry, ps2x, pr2x, ps2y, pr2y, hx, hy, massp, massr, statg, statr, acc, spots, spotr, tlead, plead, tturn, pturn, dturn, coefrow,
     dpa, grad, dsend, dright, dleft, dwo, dws, dwr, gps, gpr, rowsum, tile_s, tile_r, tz, gms, gmr, gmcol,
     fsend, frecv, pair_s, pair_r,
     hello, lc, zs_s, zs_r, ez_s, ez_r, w_s, w_r, wd_s, wd_r, pr_s, pr_r,
@@ -300,13 +300,35 @@
         if g < np_:
             both(lambda way: zsend(way, z, g))
 
-    def along(s, g):
-        if 0 <= g < np_:
-            hop(s, lambda way, p: zsend(way, p, g))
+    def passes(s, g):
+        if not 0 <= g < np_:
+            return
+
+        @pl.when((z >= s) & has_right)
+        def _():
+            zsend(0, z - s, g).wait_recv()
+            zsend(0, z - s, g).start()
+
+        @pl.when((z + s <= nz - 1) & has_left)
+        def _():
+            zsend(1, z + s, g).wait_recv()
+            zsend(1, z + s, g).start()
+
+    def ends_here(s, g):
+        if not 0 <= g < np_:
+            return
+
+        @pl.when((z >= s) & ends[1])
+        def _():
+            zsend(0, z - s, g).wait_recv()
+
+        @pl.when((z + s <= nz - 1) & ends[0])
+        def _():
+            zsend(1, z + s, g).wait_recv()
 
     both(lambda way: zsmall(way, z))
-    own(0)
-    own(1)
+    for g in range(4):
+        own(g)
 
     loads[0].wait()
 
@@ -348,6 +370,11 @@
         for k in (3, 1, 2):
             for h in range(2):
                 lead_copy(buf, i, k, h).start()
+
+    def lead_turned(buf, i, out):
+        lead_wait(buf, i)
+        for c in range(0, 2 * grp, rows):
+            out[:, c : c + rows] = jnp.transpose(buf[c : c + rows, :].astype(f32))
 
     def lead_wait(buf, i):
         for k in (1, 2, 3):
@@ -485,36 +512,47 @@
 
     acc[...] = jnp.zeros_like(acc)
     hop(1, zsmall)
-    along(1, 0)
-    own(2)
+    passes(1, 0)
     hop(2, zsmall)
-    along(1, 1)
-    along(2, 0)
-    own(3)
+    passes(1, 1)
+    passes(2, 0)
     hop(3, zsmall)
     gates()
     gated(0, 0)
     arrive(1)
     arrive(2)
     arrive_sib(0)
-    along(1, 2)
-    along(2, 1)
+    passes(1, 2)
+    passes(2, 1)
     own(4)
+    lead(tlead, 0, tbuf[:, 0:PIECE])
     arrive_sib(1)
     arrive_sib(2)
     for k in range(3):
         turned(k, 0)
+    passes(1, 3)
+    passes(2, 2)
+    own(5)
     arrive(3)
     arrive_sib(3)
-    along(3, 0)
+    passes(1, 4)
+    passes(2, 3)
+    own(6)
+    for n in (1, 2, 3):
+        ends_here(n, 0)
     project(0)
     for s in range(3, np_ + 2):
-        along(1, s)
-        along(2, s - 1)
-        own(s + 2)
+        passes(1, s + 2)
+        passes(2, s + 1)
+        own(s + 4)
+        if s < np_ + 1:
+            for n in (1, 2):
+                ends_here(n, s - 2)
         if s == np_:
+            for n in (1, 2):
+                ends_here(n, np_ - 1)
             project_ahead()
-        along(3, s - 2)
+        ends_here(3, s - 2)
         if s < np_:
             project(s - 2)
         else:
@@ -527,14 +565,14 @@
         if s == 6:
             turned(3, 0)
             turned(3, 1)
+            lead_turned(tlead, 0, tturn)
         relay(s - 3)
-        if s == 4:
-            lead(tlead, 0, tbuf[:, 0:PIECE])
         if s > 4:
             whole(s - 5)
         if s == 5:
             lead(plead, 1, pfin[:, 0:PIECE].astype(bf16))
     whole(np_ - 3)
+    lead_turned(plead, 1, pturn)
     for k in (3, 1, 2):
         stat(k, 0).start()
     pair(0).wait_recv()
@@ -586,13 +624,16 @@
             for i in range(3)
         )
         a, b = lax.rsqrt(pp + eps_norm), lax.rsqrt(tt + eps_norm)
-        return (
-            column(-(a * b) / spots_all, 2 * rows),
-            column(dot * a**3 * b / spots_all, 2 * rows),
-            dot * a * b,
-        )
-
-    col_t, col_p, cos_spot = spot_coefs(0)
+        t, p = -(a * b) / spots_all, dot * a**3 * b / spots_all
+        for h in range(2):
+            c = h * grp + k * rows
+            coefrow[0:1, c : c + rows] = t[:, h * rows : (h + 1) * rows]
+            coefrow[1:2, c : c + rows] = p[:, h * rows : (h + 1) * rows]
+        return t, p, dot * a * b
+
+    lead_t, lead_p = (column(v[:, 0:PIECE], PIECE) for v in coefs[0][0:2])
+    row_t, row_p, cos_spot = spot_coefs(0)
+    col_t, col_p = column(row_t, 2 * rows), column(row_p, 2 * rows)
 
     def agcopy(i, g):
         src, dst, to = (
@@ -616,15 +657,16 @@
             agcopy(i, g).start()
 
     def lead_grad():
-        lead_wait(tlead, 0)
-        lead_wait(plead, 1)
-        c_t, c_p = (v[:, 0:PIECE] for v in coefs[0][0:2])
-        for k in (0, 1, 2, 3):
-            t, p = (col_t, col_p) if k == 0 else spot_coefs(k)[0:2]
-            for h in range(2):
-                r, m = at_k(k, h), slice(h * rows, (h + 1) * rows)
-                d = (c_t + t[m]) * tlead[r, :].astype(f32) + (c_p + p[m]) * plead[r, :].astype(f32)
-                dpa[0, r, 0:PIECE] = d.astype(bf16)
+        for k in (1, 2, 3):
+            spot_coefs(k)
+        for c in range(0, 2 * grp, 128):
+            at = slice(c, c + 128)
+            d = (lead_t + coefrow[0:1, at]) * tturn[:, at] + (lead_p + coefrow[1:2, at]) * pturn[:, at]
+            dturn[:, at] = d.astype(bf16)
+
+    def lead_back():
+        for c in range(0, 2 * grp, rows):
+            dpa[0, c : c + rows, 0:PIECE] = jnp.transpose(dturn[:, c : c + rows].astype(f32)).astype(bf16)
 
     def give_on(g):
         agcopy(0, g).wait_recv()
@@ -643,7 +685,7 @@
         @pl.loop(0, nz)
         def _(u):
             p = up * u + (1 - up) * (nz - 1 - u)
-            v = jnp.dot(wt[seg(p), :], dpa[0, :, 0:PIECE], preferred_element_type=f32)
+            v = dot_nt(wt[seg(p), :], dturn[...])
             grad[p, :, 0:PIECE] = v
 
             @pl.when((ends[0] | ends[1]) & (p != z))
@@ -658,9 +700,14 @@
             def _():
                 dcopy(1, p, 0).start()
 
-    def expr_grad(g):
-        for i in (1, 3, 4, 5):
-            agcopy(i, g).wait_recv()
+            @pl.when(u == 0)
+            def _():
+                give_on(1)
+
+    def expr_grad(g, wait=True):
+        if wait:
+            for i in (1, 3, 4, 5):
+                agcopy(i, g).wait_recv()
         lanes = slice(g % 2 * PIECE, (g % 2 + 1) * PIECE)
         v = jnp.dot(wt[...], dpa[g // 2, :, lanes], preferred_element_type=f32)
         for p in range(nz):
@@ -922,85 +969,87 @@
     mass, d = tile_start()
     lead_grad()
     expr_grad_first()
-    give_on(1)
+    lead_back()
+    give_on(2)
     give(3)
-    give_on(2)
     give(4)
     tile_along()
     expr_grad(1)
     starts((0, 1), (1, 1), (2, 1))
+    chain(1, 0, 0)
     give_on(3)
     give(5)
-    chain(1, 0, 0)
+    chain(1, 1, 0)
     give_on(4)
+    give(6)
     expr_grad(2)
     starts((0, 2), (1, 2))
-    chain(1, 1, 0)
-    give(6)
+    chain(2, 0, 0)
+    chain(1, 0, 1)
     give_on(5)
+    give(7)
     expr_grad(3)
     starts((0, 3))
-    chain(1, 0, 1)
-    chain(2, 0, 0)
-    give(7)
+    chain(1, 1, 1)
     give_on(6)
-    chain(1, 1, 1)
     expr_grad(4)
     starts((0, 4), (1, 3))
     push = totals(mass, d)
-    give_on(7)
     chain(2, 0, 1)
     chain(1, 0, 2)
+    give_on(7)
     expr_grad(5)
     starts((0, 5), (1, 4))
     finish(0)
     chain(1, 1, 2)
     expr_grad(6)
-    starts((0, 6))
+    starts((0, 6), (1, 5))
     chain(1, 0, 3)
+    for i in (1, 3, 4, 5):
+        agcopy(i, np_ - 1).wait_recv()
+    weight_grad(0)
+    chain(2, 0, 2)
+    chain(1, 0, 4)
+    weight_grad(1)
     finish(1)
     mass_columns()
-    chain(2, 0, 2)
-    expr_grad(7)
-    starts((0, 7), (1, 5), (2, 2), (1, 6), (2, 3), (1, 7))
-    chain(1, 0, 4)
+    give_back(0)
     chain(1, 1, 3)
-    weight_grad(0)
+    expr_grad(7, False)
+    starts((0, 7), (2, 2), (1, 6), (2, 3), (1, 7))
     chain(2, 0, 3)
     chain(1, 0, 5)
-    weight_grad(1)
+    weight_grad(2)
+    give_back(1)
     chain(2, 0, 4)
-    give_back(0)
     chain(1, 1, 4)
-    weight_grad(2)
+    weight_grad(3)
+    give_back(2)
     chain(1, 0, 6)
-    give_back(1)
-    chain(2, 0, 5)
-    weight_grad(3)
-    chain(1, 0, 7)
-    give_back(2)
-    chain(1, 1, 5)
     give_back(3)
     filter_along()
     starts((2, 4), (2, 5), (2, 6), (2, 7))
-    chain(2, 0, 6)
-    finish(2)
+    chain(1, 1, 5)
     take(0, 0, True)
     for p in range(1, nz):
         take(0, p)
-    chain(2, 0, 7)
-    chain(1, 1, 6)
+    chain(2, 0, 5)
+    chain(1, 0, 7)
+    sent_first()
+    chain(2, 0, 6)
+    finish(2)
     for k in (1, 2, 3):
         take(k, 0)
+    chain(1, 1, 6)
+    chain(2, 0, 7)
+    for k in (1, 2, 3):
+        take(k, 1)
     finish(3)
-    sent_first()
+    sent_along()
     chain(1, 1, 7)
     for k in (1, 2, 3):
-        take(k, 1)
-    sent_along()
+        take(k, 2)
     finish(4)
-    for k in (1, 2, 3):
-        take(k, 2)
     sent_back()
     finish(5)
     for r in range(1, nz):
@@ -1081,6 +1130,7 @@
         low(n, rows, PIECE), low(n, rows, PIECE), low(n, rows, PIECE), low(n, rows, PIECE),
         vmem(n, rows, PIECE), vmem(n, rows, PIECE), vmem(GROUP, 8, 128), vmem(GROUP, 8, 128),
         vmem(3, 1, genes), vmem(GROUP, 3, 1, genes), vmem(3, spots, PIECE), vmem(3, 1, spots), vmem(2, GROUP, 3, 1, spots), low(2 * grp, PIECE), low(2 * grp, PIECE),
+        vmem(PIECE, 2 * grp), vmem(PIECE, 2 * grp), low(PIECE, 2 * grp), vmem(2, 2 * grp),
         low(n // 2, 2 * grp, 2 * PIECE), vmem(nz, cd, genes),
         low(nz, n, cd, PIECE), low(nz, n, cd, PIECE), low(nz, n, cd, PIECE),
         vmem(nz, grp, cd), vmem(nz, grp, cd), vmem(nz, grp, cd), low(nz, grp, cd), low(GROUP, nz, rows, cd),

time: 96.2 us -> 95.2 us (0.990)
  Pallas kernels: 95.2 us -> 94.2 us
    pallas_call x1, Pallas kernels: 93.5 us -> 92.5 us  [grouped(): pl.pallas_call(functools.partial(group_kernel, nspot), out_shape=[vmem(ro...]
where the time goes in v7:
time: 95.2 us; the launch traced here: 95 us
  Pallas kernels  94.2 us (99%)
    pallas_call x1, Pallas kernels, grouped(): pl.pallas_call(functools.partial(group_kernel, nspot), out_shape=[vmem(ro...  92.5 us

profile of v7, /device:TPU:0, one launch (start us, length us, event | category | flops | bytes accessed | tf_op | source)
XLA Modules:
  0.0 95.0 jit_solution(11886998816749435232)
XLA Ops:
  0.6 92.5 %group_step.1 = (f32[128,4096]{1,0:T(8,128)S(1)}, bf16[128,4096]{1,0:T(8,128)(2,1)S(1)}, f32[128,128]{1,0:T(8,128)S(1)}, f32[8,128]{1,0:T(8,128)S(1)}, f32[256,1024]{1,0:T(8,128)S(1)}) custom-call(bf16[128,4096]{1,0:T(8,128)(2,1)} %logits_h.1, f32[2,128]{1,0:T(2,128)} %bitcast.4, bf16[256,1024]{1,0:T(8,128)(2,1)} %expr.1, bf16[256,1024]{1,0:T(8,128)(2,1)} %target.1, ...), custom_call_target="tpu_custom_call" | custom-call | tf_op jit(solution)/shard_map/group_step/pallas_call | solution.py:1152
  93.1 1.7 %finish_step.1 = (f32[128,4096]{1,0:T(8,128)}, f32[256,1024]{1,0:T(8,128)}, f32[1,1]{1,0:T(1,128)}, f32[2,128]{1,0:T(2,128)}) custom-call(f32[128,4096]{1,0:T(8,128)S(1)} %get-tuple-element.13.probs, bf16[128,4096]{1,0:T(8,128)(2,1)S(1)} %get-tuple-element.14.gp, f32[128,128]{1,0:T(8,128)S(1)} %get-tuple-element.15.tot, ...), custom_call_target="tpu_custom_call" | custom-call | tf_op jit(solution)/shard_map/finish_step/pallas_call | solution.py:1163

commit v8 on v7

--- a/solution.py
+++ b/solution.py
@@ -152,6 +152,7 @@
 GROUP = 4
 PIECE = 128
 MESH = pl.DeviceIdType.MESH
+PAIRS = (4, 6,)
 VMEM_BYTES = 44 << 20
 LAST_BYTES = 16 << 20
 
@@ -436,12 +437,23 @@
     far = (1 - z // (nz // 2)) * (nz - 1)
     near = pl.ds(pl.multiple_of(z // (nz // 2) * cd, cd), mine - cd)
 
-    def project_ahead():
-        ahead[...] = jnp.dot(wg[:, near], ebuf[np_ // 2 - 1, near, :], preferred_element_type=f32)
+    def project_ahead(g):
+        ahead[...] = jnp.dot(wg[:, near], ebuf[g // 2, near, :], preferred_element_type=f32)
 
     def project_last(g):
-        v = jnp.dot(wg[:, seg(far)], piece_of(g, seg(far)), preferred_element_type=f32)
-        share(g, ahead[:, g % 2 * PIECE : (g % 2 + 1) * PIECE] + v)
+        e = piece_of(g, seg(far))
+        lanes = pl.ds(g % 2 * PIECE, PIECE)
+
+        def rows_of(r):
+            return ahead[r, lanes] + jnp.dot(wg[r, seg(far)], e, preferred_element_type=f32)
+
+        relayed = [rows_of(at_k(3, h)) for h in range(2)]
+        psx[g, second] = relayed[0].astype(bf16)
+        pxcopy(g, 1).start()
+        psy[g, second] = relayed[1].astype(bf16)
+        pycopy(g, 1).start()
+        rest = [rows_of(pl.ds(h * grp, 3 * rows)) for h in range(2)]
+        share_rest(g, lambda k, h: rest[h][k * rows : (k + 1) * rows])
 
     def share(g, v):
         def part(k, h):
@@ -452,6 +464,9 @@
         pxcopy(g, 1).start()
         psy[g, second] = part(3, 1).astype(bf16)
         pycopy(g, 1).start()
+        share_rest(g, part)
+
+    def share_rest(g, part):
         psx[g, first] = part(1, 0).astype(bf16)
         pxcopy(g, 0).start()
         psy[g, first] = part(2, 1).astype(bf16)
@@ -545,18 +560,20 @@
         passes(1, s + 2)
         passes(2, s + 1)
         own(s + 4)
-        if s < np_ + 1:
+        g = s - 2
+        if g in PAIRS:
             for n in (1, 2):
-                ends_here(n, s - 2)
-        if s == np_:
+                ends_here(n, g)
+                ends_here(n, g + 1)
+            project_ahead(g)
+        elif g - 1 not in PAIRS:
             for n in (1, 2):
-                ends_here(n, np_ - 1)
-            project_ahead()
-        ends_here(3, s - 2)
-        if s < np_:
-            project(s - 2)
+                ends_here(n, g)
+        ends_here(3, g)
+        if g in PAIRS or g - 1 in PAIRS:
+            project_last(g)
         else:
-            project_last(s - 2)
+            project(g)
         if s == 4:
             masses()
         if s == 5:
@@ -969,7 +986,6 @@
     mass, d = tile_start()
     lead_grad()
     expr_grad_first()
-    lead_back()
     give_on(2)
     give(3)
     give(4)
@@ -995,6 +1011,7 @@
     expr_grad(4)
     starts((0, 4), (1, 3))
     push = totals(mass, d)
+    lead_back()
     chain(2, 0, 1)
     chain(1, 0, 2)
     give_on(7)

time: 95.2 us -> 94.6 us (level)
  no operation moved by 1% of the time
where the time goes in v8:
time: 94.6 us; the launch traced here: 94.5 us
  Pallas kernels  93.7 us (99%)
    pallas_call x1, Pallas kernels, grouped(): pl.pallas_call(functools.partial(group_kernel, nspot), out_shape=[vmem(ro...  91.9 us

profile of v8, /device:TPU:0, one launch (start us, length us, event | category | flops | bytes accessed | tf_op | source)
XLA Modules:
  0.0 94.5 jit_solution(4416389558045893934)
XLA Ops:
  0.6 91.9 %group_step.1 = (f32[128,4096]{1,0:T(8,128)S(1)}, bf16[128,4096]{1,0:T(8,128)(2,1)S(1)}, f32[128,128]{1,0:T(8,128)S(1)}, f32[8,128]{1,0:T(8,128)S(1)}, f32[256,1024]{1,0:T(8,128)S(1)}) custom-call(bf16[128,4096]{1,0:T(8,128)(2,1)} %logits_h.1, f32[2,128]{1,0:T(2,128)} %bitcast.4, bf16[256,1024]{1,0:T(8,128)(2,1)} %expr.1, bf16[256,1024]{1,0:T(8,128)(2,1)} %target.1, ...), custom_call_target="tpu_custom_call" | custom-call | tf_op jit(solution)/shard_map/group_step/pallas_call | solution.py:1169
  92.6 1.7 %finish_step.1 = (f32[128,4096]{1,0:T(8,128)}, f32[256,1024]{1,0:T(8,128)}, f32[1,1]{1,0:T(1,128)}, f32[2,128]{1,0:T(2,128)}) custom-call(f32[128,4096]{1,0:T(8,128)S(1)} %get-tuple-element.13.probs, bf16[128,4096]{1,0:T(8,128)(2,1)S(1)} %get-tuple-element.14.gp, f32[128,128]{1,0:T(8,128)S(1)} %get-tuple-element.15.tot, ...), custom_call_target="tpu_custom_call" | custom-call | tf_op jit(solution)/shard_map/finish_step/pallas_call | solution.py:1180

commit v9 on v8

--- a/solution.py
+++ b/solution.py
@@ -494,9 +494,16 @@
         pfin[second, at] += pry[g, first].astype(f32) + pr2x[g].astype(f32)
         p = pfin[:, at]
         t = tbuf[:, at].astype(f32)
-        for i, v in enumerate((p * p, p * t, t * t)):
+        for i, v in enumerate((p * p, p * t)):
             statg[i, :, at] = jnp.sum(v, axis=0, keepdims=True)
             acc[i] += v
+
+    def target_moments():
+        for g in range(np_):
+            t = tbuf[:, piece(g)].astype(f32)
+            statg[2, :, piece(g)] = jnp.sum(t * t, axis=0, keepdims=True)
+            acc[2] += t * t
+        spots[2] = jnp.sum(jnp.transpose(acc[2]), axis=0, keepdims=True)
 
     parts = (pl.ds(0, (np_ - 2) * PIECE), pl.ds((np_ - 2) * PIECE, 2 * PIECE))
 
@@ -548,6 +555,7 @@
     passes(1, 3)
     passes(2, 2)
     own(5)
+    target_moments()
     arrive(3)
     arrive_sib(3)
     passes(1, 4)
@@ -574,7 +582,7 @@
             project_last(g)
         else:
             project(g)
-        if s == 4:
+        if s == 3:
             masses()
         if s == 5:
             for k in range(3):
@@ -601,7 +609,7 @@
     for k in (3, 1, 2):
         stat(k, 1).start()
 
-    for i in range(3):
+    for i in range(2):
         spots[i] = jnp.sum(jnp.transpose(acc[i]), axis=0, keepdims=True)
     def spot_copy(k, h):
         i = 2 * k + h

time: 94.6 us -> 94.4 us (level)
  no operation moved by 1% of the time
where the time goes in v9:
time: 94.4 us; the launch traced here: 94.2 us
  Pallas kernels  93.4 us (99%)
    pallas_call x1, Pallas kernels, grouped(): pl.pallas_call(functools.partial(group_kernel, nspot), out_shape=[vmem(ro...  91.7 us

profile of v9, /device:TPU:0, one launch (start us, length us, event | category | flops | bytes accessed | tf_op | source)
XLA Modules:
  0.0 94.2 jit_solution(1232312076591295494)
XLA Ops:
  0.6 91.7 %group_step.1 = (f32[128,4096]{1,0:T(8,128)S(1)}, bf16[128,4096]{1,0:T(8,128)(2,1)S(1)}, f32[128,128]{1,0:T(8,128)S(1)}, f32[8,128]{1,0:T(8,128)S(1)}, f32[256,1024]{1,0:T(8,128)S(1)}) custom-call(bf16[128,4096]{1,0:T(8,128)(2,1)} %logits_h.1, f32[2,128]{1,0:T(2,128)} %bitcast.4, bf16[256,1024]{1,0:T(8,128)(2,1)} %expr.1, bf16[256,1024]{1,0:T(8,128)(2,1)} %target.1, ...), custom_call_target="tpu_custom_call" | custom-call | tf_op jit(solution)/shard_map/group_step/pallas_call | solution.py:1177
  92.3 1.7 %finish_step.1 = (f32[128,4096]{1,0:T(8,128)}, f32[256,1024]{1,0:T(8,128)}, f32[1,1]{1,0:T(1,128)}, f32[2,128]{1,0:T(2,128)}) custom-call(f32[128,4096]{1,0:T(8,128)S(1)} %get-tuple-element.13.probs, bf16[128,4096]{1,0:T(8,128)(2,1)S(1)} %get-tuple-element.14.gp, f32[128,128]{1,0:T(8,128)S(1)} %get-tuple-element.15.tot, ...), custom_call_target="tpu_custom_call" | custom-call | tf_op jit(solution)/shard_map/finish_step/pallas_call | solution.py:1188
